TPU v7x, 32 devices: a whole 2x2x4 slice. The times are simulated.
32 devices in a mesh: dp: 4 (over x, core), expert: 8 (over z, y).
Axes of the slice: x: 2, y: 2, z: 4, core: 2. Of those that a mesh axis runs over, the one named last changes fastest.
Arguments:
- tokens: bfloat16 [8192, 768], P(('dp', 'expert')), may hold values from -6 to 6
- upstream: bfloat16 [8192, 768], P(('dp', 'expert')), may hold values from -4 to 4
- gate_prob: float32 [8192], P(('dp', 'expert')), may hold values from 0.2 to 1
- expert_id: int32 [8192], P(('dp', 'expert')), may hold values from 0 to 7
- slot_index: int32 [8192], P(('dp', 'expert')), may hold values from -1 to 39, as said below
- segment_id: int32 [32, 256], P(('dp', 'expert')), may hold values from 0 to 3, never falling along the last dimension, each value on 1 to 128 neighbouring positions
- weight_in: bfloat16 [8, 3072, 768], P('expert'), may hold values from -0.21875 to 0.21875
- weight_out: bfloat16 [8, 3072, 768], P('expert'), may hold values from -0.109375 to 0.109375
Outputs:
- d_tokens: bfloat16 [8192, 768], P(('dp', 'expert'))
- d_gate: float32 [8192], P(('dp', 'expert'))
- grad_in: bfloat16 [8, 3072, 768], P('expert', 'dp')
- grad_out: bfloat16 [8, 3072, 768], P('expert', 'dp')
Inputs may be any that keep to these rules, and one draw needn't show every extreme that they name: `slot_index`: -1 marks a dropped token; otherwise the number of earlier tokens of the same row with the same expert_id. A token is dropped exactly when 40 or more earlier tokens of its row chose its expert. `segment_id`: never falling along a row.
All inputs are finite; a program needn't handle non-finite values.
Results may differ from a plain program's by a relative error of at most 0.02.
Values may be sent and summed in bfloat16 or wider, within the bound.
No kernel may reach another device: no remote copies, remote signals or barrier semaphores. Data moves between devices by JAX's collectives and lax.ppermute only.
A program may use at most 128 MiB of HBM per device.

v0:
```python
from functools import partial

import jax
import jax.numpy as jnp
from jax import lax
from jax.sharding import PartitionSpec as P

SEGS = 4


def gelu_back(pre_act, grad_rows):
    return jax.vjp(partial(jax.nn.gelu, approximate=True), pre_act)[1](grad_rows)[0]


def pick_rows(values, owners):
    padding = jnp.zeros((1,) + values.shape[1:], values.dtype)
    return jnp.concatenate([values, padding], axis=0)[owners]


def body(tokens, upstream, gate_prob, expert_id, slot_index, segment_id, weight_in, weight_out):
    experts = lax.axis_size("expert")
    tok_rows, model_width = tokens.shape
    hidden_units = weight_in.shape[1]
    capacity = 5 * tok_rows // (4 * experts)
    slots_all = experts * capacity
    first_weight = weight_in[0]
    second_weight = weight_out[0]
    labels = jnp.arange(SEGS, dtype=jnp.int32)
    member = (segment_id[0][:, None] == labels[None, :]).astype(jnp.float32)
    counts = jnp.sum(member, axis=0)
    length = jnp.sum(member * counts[None, :], axis=1)
    doc_weight = tok_rows / (SEGS * length)
    cotangent = (upstream.astype(jnp.float32) * doc_weight[:, None]).astype(jnp.bfloat16)
    position = jnp.where(slot_index >= 0, expert_id * capacity + slot_index, slots_all)
    filled = jnp.full((slots_all + 1,), tok_rows, jnp.int32)
    owners = filled.at[position].set(jnp.arange(tok_rows, dtype=jnp.int32))[:slots_all]
    send_x = pick_rows(tokens, owners).reshape(experts, capacity, model_width)
    send_c = pick_rows(cotangent, owners).reshape(experts, capacity, model_width)
    send_g = pick_rows(gate_prob, owners).reshape(experts, capacity)
    x_part = lax.all_to_all(send_x, "expert", split_axis=0, concat_axis=0, tiled=True)
    c_part = lax.all_to_all(send_c, "expert", split_axis=0, concat_axis=0, tiled=True)
    g_part = lax.all_to_all(
        send_g.astype(jnp.bfloat16), "expert", split_axis=0, concat_axis=0, tiled=True
    ).astype(send_g.dtype)
    pre_act = jnp.einsum("skd,fd->skf", x_part, first_weight, preferred_element_type=jnp.float32)
    hidden = jax.nn.gelu(pre_act, approximate=True).astype(jnp.bfloat16)
    produced = jnp.einsum("skf,fd->skd", hidden, second_weight, preferred_element_type=jnp.float32)
    c_float = c_part.astype(jnp.float32)
    d_gate_rows = jnp.sum(produced * c_float, axis=2)
    d_out = (g_part[:, :, None] * c_float).astype(jnp.bfloat16)
    d_hidden = jnp.einsum("skd,fd->skf", d_out, second_weight, preferred_element_type=jnp.float32)
    d_pre = gelu_back(pre_act, d_hidden).astype(jnp.bfloat16)
    d_in_rows = jnp.einsum(
        "skf,fd->skd", d_pre, first_weight, preferred_element_type=jnp.float32
    ).astype(jnp.bfloat16)
    x_rows, d_in_rows, d_gate_rows, hidden, d_out, d_pre = (
        x_part,
        d_in_rows,
        d_gate_rows,
        hidden,
        d_out,
        d_pre,
    )
    back_rows, back_gate = (
        lax.all_to_all(d_in_rows, "expert", split_axis=0, concat_axis=0, tiled=True),
        lax.all_to_all(
            d_gate_rows.astype(jnp.bfloat16), "expert", split_axis=0, concat_axis=0, tiled=True
        ).astype(d_gate_rows.dtype),
    )
    d_tokens = pick_rows(back_rows.reshape(slots_all, model_width), position)
    d_gate = pick_rows(back_gate.reshape(slots_all), position)
    x_flat = x_rows.reshape(slots_all, model_width)
    d_out_flat = d_out.reshape(slots_all, model_width)
    hidden_flat = hidden.reshape(slots_all, hidden_units)
    d_pre_flat = d_pre.reshape(slots_all, hidden_units)
    columns = d_pre_flat
    grad_first = lax.psum_scatter(
        jnp.einsum("rf,rd->fd", columns, x_flat, preferred_element_type=jnp.float32).astype(
            jnp.bfloat16
        ),
        "dp",
        scatter_dimension=0,
        tiled=True,
    )
    columns = hidden_flat
    grad_second = lax.psum_scatter(
        jnp.einsum("rf,rd->fd", columns, d_out_flat, preferred_element_type=jnp.float32).astype(
            jnp.bfloat16
        ),
        "dp",
        scatter_dimension=0,
        tiled=True,
    )
    return (d_tokens, d_gate, grad_first[None], grad_second[None])


def solution(mesh):
    in_specs = (
        P(("dp", "expert"), None),
        P(("dp", "expert"), None),
        P(("dp", "expert")),
        P(("dp", "expert")),
        P(("dp", "expert")),
        P(("dp", "expert"), None),
        P("expert", None, None),
        P("expert", None, None),
    )
    out_specs = (
        P(("dp", "expert"), None),
        P(("dp", "expert")),
        P("expert", "dp", None),
        P("expert", "dp", None),
    )
    return jax.shard_map(body, mesh=mesh, in_specs=in_specs, out_specs=out_specs, check_vma=False)
```

profile of v0, /device:TPU:0, one launch (start us, length us, event | category | flops | bytes accessed | tf_op | source)
XLA Modules:
  0.0 172.5 jit_solution(4260251885139793129)
XLA Ops:
  7.2 0.0 copy-start.1
  7.2 0.0 copy-start
  7.2 0.8 compare_select_fusion.1
  7.9 1.4 scatter_custom_fusion
  9.4 0.7 pad_maximum_fusion
  10.1 2.5 %gather_fusion = bf16[320]{0:T(512)(128)(2,1)S(1)} fusion(bf16[257]{0:T(512)(128)(2,1)S(1)} %pad_maximum_fusion, s32[1024]{0:T(1024)S(1)} %pad_clamp_fusion.1), kind=kCustom, calls=%fused_computation | custom fusion | bytes 2560 | tf_op jit(solution)/shard_map/gather | solution.py:17
  12.5 0.7 convert_element_type.89
  13.2 7.3 %all-to-all-start = ((bf16[8,1,40]{2,1,0:T(2,128)(2,1)}), bf16[8,1,40]{2,1,0:T(2,128)(2,1)S(1)}, u32[]{:S(2)}, u32[]{:S(2)}) async-start(bf16[8,1,40]{2,1,0:T(2,128)(2,1)} %convert_element_type.89), calls=%async_computation | async-start | bytes 8192 | tf_op jit(solution)/shard_map/all_to_all | solution.py:42
  20.5 1.0 concatenate.20
  21.5 2.6 %gather_fusion.2 = bf16[320,768]{1,0:T(8,128)(2,1)} fusion(bf16[257,768]{1,0:T(8,128)(2,1)S(1)} %concatenate.20, s32[1024]{0:T(1024)S(1)} %pad_clamp_fusion.1), kind=kCustom, calls=%fused_computation.2 | custom fusion | bytes 984320 | tf_op jit(solution)/shard_map/gather | solution.py:17
  24.1 2.8 %all-to-all-done = bf16[8,1,40]{2,1,0:T(2,128)(2,1)S(1)} async-done(((bf16[8,1,40]{2,1,0:T(2,128)(2,1)}), bf16[8,1,40]{2,1,0:T(2,128)(2,1)S(1)}, u32[]{:S(2)}, u32[]{:S(2)}) %all-to-all-start) | async-done | bytes 672 | tf_op jit(solution)/shard_map/all_to_all | solution.py:42
  26.9 3.5 %all-to-all-start.2 = ((bf16[8,40,768]{2,1,0:T(8,128)(2,1)}), bf16[8,40,768]{2,1,0:T(8,128)(2,1)S(1)}, u32[]{:S(2)}, u32[]{:S(2)}) async-start(bf16[8,40,768]{2,1,0:T(8,128)(2,1)} %bitcast.5), calls=%async_computation.2 | async-start | bytes 983040 | tf_op jit(solution)/shard_map/all_to_all | solution.py:40
  30.4 0.0 copy-done.1
  30.4 0.1 convert_reduce_fusion
  30.5 0.1 select_reduce_fusion
  30.6 0.0 copy-done
  30.6 0.1 multiply_convert_fusion.1
  30.8 2.6 %gather_fusion.1 = bf16[320,768]{1,0:T(8,128)(2,1)} fusion(bf16[257,768]{1,0:T(8,128)(2,1)S(1)} %concatenate.19, s32[1024]{0:T(1024)S(1)} %pad_clamp_fusion.1), kind=kCustom, calls=%fused_computation.1 | custom fusion | bytes 984320 | tf_op jit(solution)/shard_map/gather | solution.py:17
  33.4 10.0 %all-to-all-done.2 = bf16[8,40,768]{2,1,0:T(8,128)(2,1)S(1)} async-done(((bf16[8,40,768]{2,1,0:T(8,128)(2,1)}), bf16[8,40,768]{2,1,0:T(8,128)(2,1)S(1)}, u32[]{:S(2)}, u32[]{:S(2)}) %all-to-all-start.2) | async-done | bytes 491552 | tf_op jit(solution)/shard_map/all_to_all | solution.py:40
  43.4 3.6 %all-to-all-start.1 = ((bf16[8,40,768]{2,1,0:T(8,128)(2,1)}), bf16[8,40,768]{2,1,0:T(8,128)(2,1)S(1)}, u32[]{:S(2)}, u32[]{:S(2)}) async-start(bf16[8,40,768]{2,1,0:T(8,128)(2,1)} %bitcast.2), calls=%async_computation.1 | async-start | bytes 983040 | tf_op jit(solution)/shard_map/all_to_all | solution.py:41
  47.0 0.0 reduce-scatter.5.cloned.1.call-start
  47.1 6.0 %fusion.2 = f32[8,40,3072]{2,1,0:T(8,128)} fusion(bf16[8,40,768]{2,1,0:T(8,128)(2,1)S(1)} %all-to-all-done.2, bf16[1,3072,768]{2,1,0:T(8,128)(2,1)} %param.14), kind=kOutput, calls=%fused_computation.12 | convolution fusion | flops 1509949440 | bytes 9142272 | tf_op jit(solution)/shard_map/skd,fd->skf/dot_general | solution.py:45
  53.1 7.0 %all-to-all-done.1 = bf16[8,40,768]{2,1,0:T(8,128)(2,1)S(1)} async-done(((bf16[8,40,768]{2,1,0:T(8,128)(2,1)}), bf16[8,40,768]{2,1,0:T(8,128)(2,1)S(1)}, u32[]{:S(2)}, u32[]{:S(2)}) %all-to-all-start.1) | async-done | bytes 491552 | tf_op jit(solution)/shard_map/all_to_all | solution.py:41
  60.2 7.2 %bitcast_convert_fusion = bf16[3072,768]{1,0:T(8,128)(2,1)} fusion(bf16[8,40,768]{2,1,0:T(8,128)(2,1)S(1)} %all-to-all-done.1, f32[8,40]{1,0:T(8,128)S(1)} %bitcast.40, f32[8,40,3072]{2,1,0:T(8,128)} %fusion.2), kind=kOutput, calls=%fused_computation.6 | convolution fusion | flops 1521893376 | bytes 9143552 | tf_op jit(solution)/shard_map/rf,rd->fd/dot_general | solution.py:87
  67.4 0.0 reduce-scatter.5.cloned.1.call-update
  67.4 0.2 reduce-scatter.3.cloned.1.call-start
  67.6 7.3 %fusion.14 = bf16[8,40,3072]{2,1,0:T(8,128)(2,1)S(1)} fusion(f32[8,40,3072]{2,1,0:T(8,128)} %fusion.2, bf16[1,3072,768]{2,1,0:T(8,128)(2,1)} %param.15, bf16[8,40,768]{2,1,0:T(8,128)(2,1)S(1)} %all-to-all-done.1, f32[8,40]{1,0:T(8,128)S(1)} %bitcast.41), kind=kOutput, calls=%fused_computation.24 | convolution fusion | flops 1530347520 | bytes 11109632 | tf_op jit(solution)/shard_map/skd,fd->skf/dot_general | solution.py:51
  75.0 4.3 %bitcast_convert_fusion.1 = bf16[3072,768]{1,0:T(8,128)(2,1)} fusion(bf16[8,40,3072]{2,1,0:T(8,128)(2,1)S(1)} %fusion.14, bf16[8,40,768]{2,1,0:T(8,128)(2,1)S(1)} %all-to-all-done.2), kind=kOutput, calls=%fused_computation.7 | convolution fusion | flops 1512308736 | bytes 7176192 | tf_op jit(solution)/shard_map/rf,rd->fd/dot_general | solution.py:78
  79.3 0.0 reduce-scatter.3.cloned.1.call-update
  79.3 6.2 %fusion.23 = bf16[8,40]{1,0:T(8,128)(2,1)S(1)} fusion(bf16[1,3072,768]{2,1,0:T(8,128)(2,1)} %param.15, bf16[8,40,768]{2,1,0:T(8,128)(2,1)S(1)} %all-to-all-done.1, f32[8,40,3072]{2,1,0:T(8,128)} %fusion.2), kind=kOutput, calls=%fused_computation.28 | convolution fusion | flops 1519533824 | bytes 9142912 | tf_op jit(solution)/shard_map/skf,fd->skd/dot_general | solution.py:47
  85.5 0.6 copy.15
  86.1 3.8 %all-to-all-start.4 = ((bf16[8,1,40]{2,1,0:T(2,128)(2,1)}), bf16[8,1,40]{2,1,0:T(2,128)(2,1)S(1)}, u32[]{:S(2)}, u32[]{:S(2)}) async-start(bf16[8,1,40]{2,1,0:T(2,128)(2,1)} %copy.15), calls=%async_computation.4 | async-start | bytes 8192 | tf_op jit(solution)/shard_map/all_to_all | solution.py:66
  89.9 4.9 %fusion.20 = bf16[8,40,768]{2,1,0:T(8,128)(2,1)} fusion(bf16[8,40,3072]{2,1,0:T(8,128)(2,1)S(1)} %fusion.14, bf16[1,3072,768]{2,1,0:T(8,128)(2,1)} %param.14), kind=kOutput, calls=%fused_computation.27 | convolution fusion | flops 1510195200 | bytes 7176192 | tf_op jit(solution)/shard_map/skf,fd->skd/dot_general | solution.py:53
  94.7 1.5 all-to-all-done.4
  96.3 4.5 %all-to-all-start.3 = ((bf16[8,40,768]{2,1,0:T(8,128)(2,1)}), bf16[8,40,768]{2,1,0:T(8,128)(2,1)S(1)}, u32[]{:S(2)}, u32[]{:S(2)}) async-start(bf16[8,40,768]{2,1,0:T(8,128)(2,1)} %fusion.20), calls=%async_computation.3 | async-start | bytes 983040 | tf_op jit(solution)/shard_map/all_to_all | solution.py:65
  100.8 0.1 convert_element_type.85
  100.9 0.1 maximum_convert_fusion
  100.9 2.5 %gather_fusion.4 = f32[256]{0:T(256)} fusion(f32[321]{0:T(512)S(1)} %maximum_convert_fusion, s32[1024]{0:T(1024)S(1)} %pad_clamp_fusion), kind=kCustom, calls=%fused_computation.4 | custom fusion | bytes 3072 | tf_op jit(solution)/shard_map/gather | solution.py:17
  103.5 10.1 %all-to-all-done.3 = bf16[8,40,768]{2,1,0:T(8,128)(2,1)S(1)} async-done(((bf16[8,40,768]{2,1,0:T(8,128)(2,1)}), bf16[8,40,768]{2,1,0:T(8,128)(2,1)S(1)}, u32[]{:S(2)}, u32[]{:S(2)}) %all-to-all-start.3) | async-done | bytes 491552 | tf_op jit(solution)/shard_map/all_to_all | solution.py:65
  113.6 1.9 %gather_fusion.3 = bf16[256,768]{1,0:T(8,128)(2,1)} fusion(bf16[321,768]{1,0:T(8,128)(2,1)S(1)} %concatenate.21, s32[1024]{0:T(1024)S(1)} %pad_clamp_fusion), kind=kCustom, calls=%fused_computation.3 | custom fusion | bytes 787456 | tf_op jit(solution)/shard_map/gather | solution.py:17
  115.5 0.0 reduce-scatter.5.cloned.1.call-done
  115.5 50.1 %reduce-scatter.3.cloned.1.call-done = bf16[768,768]{1,0:T(8,128)(2,1)} async-done(((bf16[3072,768]{1,0:T(8,128)(2,1)}), bf16[768,768]{1,0:T(8,128)(2,1)}) %reduce-scatter.3.cloned.1.call-update) | async-done | bytes 1179664 | tf_op jit(solution)/shard_map/reduce_scatter | solution.py:77
  (9 shorter events, 0.1 us)
Async XLA Ops:
  7.2 23.2 %copy-start.1 = (s32[1,256]{1,0:T(1,128)S(1)}, s32[1,256]{1,0:T(1,128)}, u32[]{:S(2)}) copy-start(s32[1,256]{1,0:T(1,128)} %param.13) | copy-start | bytes 3076
  7.2 23.4 %copy-start = (bf16[256,768]{1,0:T(8,128)(2,1)S(1)}, bf16[256,768]{1,0:T(8,128)(2,1)}, u32[]{:S(2)}) copy-start(bf16[256,768]{1,0:T(8,128)(2,1)} %param.9) | copy-start | bytes 1179652
  13.2 13.7 %all-to-all-start = ((bf16[8,1,40]{2,1,0:T(2,128)(2,1)}), bf16[8,1,40]{2,1,0:T(2,128)(2,1)S(1)}, u32[]{:S(2)}, u32[]{:S(2)}) async-start(bf16[8,1,40]{2,1,0:T(2,128)(2,1)} %convert_element_type.89), calls=%async_computation | async-start | bytes 8192 | tf_op jit(solution)/shard_map/all_to_all | solution.py:42
  26.9 16.5 %all-to-all-start.2 = ((bf16[8,40,768]{2,1,0:T(8,128)(2,1)}), bf16[8,40,768]{2,1,0:T(8,128)(2,1)S(1)}, u32[]{:S(2)}, u32[]{:S(2)}) async-start(bf16[8,40,768]{2,1,0:T(8,128)(2,1)} %bitcast.5), calls=%async_computation.2 | async-start | bytes 983040 | tf_op jit(solution)/shard_map/all_to_all | solution.py:40
  43.4 16.8 %all-to-all-start.1 = ((bf16[8,40,768]{2,1,0:T(8,128)(2,1)}), bf16[8,40,768]{2,1,0:T(8,128)(2,1)S(1)}, u32[]{:S(2)}, u32[]{:S(2)}) async-start(bf16[8,40,768]{2,1,0:T(8,128)(2,1)} %bitcast.2), calls=%async_computation.1 | async-start | bytes 983040 | tf_op jit(solution)/shard_map/all_to_all | solution.py:41
  47.0 68.5 %reduce-scatter.5.cloned.1.call-start = ((), (), s32[]{:S(2)}) async-start(), calls=%async_computation.8 | async-start | bytes 5898240 | tf_op jit(solution)/shard_map/reduce_scatter | solution.py:86
  67.4 98.2 %reduce-scatter.3.cloned.1.call-start = ((), (), s32[]{:S(2)}) async-start(), calls=%async_computation.7 | async-start | bytes 5898240 | tf_op jit(solution)/shard_map/reduce_scatter | solution.py:77
  86.1 10.2 %all-to-all-start.4 = ((bf16[8,1,40]{2,1,0:T(2,128)(2,1)}), bf16[8,1,40]{2,1,0:T(2,128)(2,1)S(1)}, u32[]{:S(2)}, u32[]{:S(2)}) async-start(bf16[8,1,40]{2,1,0:T(2,128)(2,1)} %copy.15), calls=%async_computation.4 | async-start | bytes 8192 | tf_op jit(solution)/shard_map/all_to_all | solution.py:66
  96.3 17.2 %all-to-all-start.3 = ((bf16[8,40,768]{2,1,0:T(8,128)(2,1)}), bf16[8,40,768]{2,1,0:T(8,128)(2,1)S(1)}, u32[]{:S(2)}, u32[]{:S(2)}) async-start(bf16[8,40,768]{2,1,0:T(8,128)(2,1)} %fusion.20), calls=%async_computation.3 | async-start | bytes 983040 | tf_op jit(solution)/shard_map/all_to_all | solution.py:65
Sparse Core Ops, SparseCore 0:
  67.5 46.8 reduce-scatter.4
  117.7 47.8 reduce-scatter.2
where the time goes:
time: 173 us; the launch traced here: 172 us
  waiting for transfers between devices  81.5 us (47%)
  matrix products  35.9 us (21%)
  starting transfers between devices  23 us (13%)
  local copies, waits for them, and re-layouts  16 us (9%)
  between operations  14.2 us (8%)
  other arithmetic  1.91 us (1%)
    reduce_scatter x1, waiting for transfers between devices, body(): lax.psum_scatter(jnp.einsum('rf,rd->fd', columns, x_flat, preferred_eleme...  50.1 us
    gather x5, local copies, waits for them, and re-layouts, pick_rows(): return jnp.concatenate([values, padding], axis=0)[owners]  12.1 us
    all_to_all x1, waiting for transfers between devices, body(): lax.all_to_all(d_in_rows, 'expert', split_axis=0, concat_axis=0, tiled=True)  10.1 us
    all_to_all x1, waiting for transfers between devices, body(): lax.all_to_all(send_x, 'expert', split_axis=0, concat_axis=0, tiled=True)  10 us
    dot_general x1, matrix products, body(): jnp.einsum('skd,fd->skf', d_out, second_weight, preferred_element_type=jn...  7.3 us
    all_to_all x1, starting transfers between devices, body(): lax.all_to_all(send_g.astype(jnp.bfloat16), 'expert', split_axis=0, conca...  7.28 us
    dot_general x1, matrix products, body(): jnp.einsum('rf,rd->fd', columns, d_out_flat, preferred_element_type=jnp.f...  7.24 us
    all_to_all x1, waiting for transfers between devices, body(): lax.all_to_all(send_c, 'expert', split_axis=0, concat_axis=0, tiled=True)  7.04 us
  transfers between devices with their start and end apart: 7, of which 6 were waited for; matrix products, arithmetic and copies ran while one was open for 24% of the time, Pallas kernels for 0%

commit v1 on v0

v1 whole, which is shorter than its diff:
```python
from functools import partial

import jax
import jax.numpy as jnp
from jax import lax
from jax.experimental import pallas as pl
from jax.experimental.pallas import tpu as pltpu
from jax.sharding import PartitionSpec as P

SEGS = 4
LANES = 128
SUBLANES = 8
MIB = 1024 * 1024
ROOT_2_PI = 0.7978845608028654
CUBIC = 0.044715


def dot_nn(a, b):
    return lax.dot_general(a, b, (((1,), (0,)), ((), ())), preferred_element_type=jnp.float32)


def dot_nt(a, b):
    return lax.dot_general(a, b, (((1,), (1,)), ((), ())), preferred_element_type=jnp.float32)


def dot_tn(a, b):
    return lax.dot_general(a, b, (((0,), (0,)), ((), ())), preferred_element_type=jnp.float32)


def gelu_and_slope(v):
    square = v * v
    t = jnp.tanh(v * (ROOT_2_PI + (ROOT_2_PI * CUBIC) * square))
    half = 0.5 + 0.5 * t
    hidden = v * half
    slope = half + hidden * (1.0 - t) * (ROOT_2_PI + (3.0 * ROOT_2_PI * CUBIC) * square)
    return hidden.astype(jnp.bfloat16), slope


def owner_table(chunk, slot, cap_rows, slots):
    place = jnp.where(slot >= 0, chunk * cap_rows + slot, -1)
    rows = lax.broadcasted_iota(jnp.int32, (slots, slot.shape[1]), 0)
    return rows == place


def pack_kernel(cap_rows, experts, me_ref, *refs):
    pairs = experts // 2
    sources, x_refs, (keep_ref, cross_ref) = refs[:6], refs[6 : 6 + pairs], refs[6 + pairs : 8 + pairs]
    scratch, sems = refs[8 + pairs : 14 + pairs], refs[14 + pairs]
    copies = [
        pltpu.make_async_copy(src, dst, sems.at[i])
        for i, (src, dst) in enumerate(zip(sources, scratch))
    ]
    for copy in copies:
        copy.start()
    for copy in copies:
        copy.wait()
    tok_ref, up_ref, gate_ref, expert_ref, slot_ref, seg_ref = scratch
    tok_rows = tok_ref.shape[0]
    slots = experts * cap_rows
    chunk, slot = expert_ref[...] ^ me_ref[0], slot_ref[...]
    table = owner_table(chunk, slot, cap_rows, slots).astype(jnp.bfloat16)
    split_rows(dot_nn(table, tok_ref[...]), x_refs)
    seg = seg_ref[...]
    length = jnp.zeros(seg.shape, jnp.float32)
    for label in range(SEGS):
        member = (seg == label).astype(jnp.float32)
        length = length + member * jnp.sum(member, axis=1, keepdims=True)
    weight = tok_rows / (SEGS * length)
    chosen = owner_table((chunk & 1) * pairs + (chunk >> 1), slot, cap_rows, slots)
    table = chosen.astype(jnp.bfloat16)
    weight_col = jnp.sum(jnp.where(chosen, weight, 0.0), axis=1, keepdims=True)
    gate_col = jnp.sum(jnp.where(chosen, gate_ref[...], 0.0), axis=1, keepdims=True)
    cotangent = (dot_nn(table, up_ref[...]) * weight_col).astype(jnp.bfloat16)
    split_rows(cotangent.astype(jnp.float32) * gate_col, (keep_ref, cross_ref))


def split_rows(value, refs):
    rows = value.shape[0] // len(refs)
    for i, ref in enumerate(refs):
        ref[...] = value[i * rows : (i + 1) * rows].astype(ref.dtype)


def halves(refs):
    values = [ref[...].astype(jnp.float32) for ref in refs]
    half = values[0].shape[0] // 2
    return [jnp.concatenate([v[b * half : (b + 1) * half] for v in values], axis=0) for b in (0, 1)]


def turn_d_kernel(pairs, keep_ref, near_ref, *out_refs):
    both = [ref[...].astype(jnp.float32) for ref in (keep_ref, near_ref)]
    rows = both[0].shape[0] // pairs
    for i, ref in enumerate(out_refs):
        ref[...] = jnp.concatenate([v[i * rows : (i + 1) * rows] for v in both], axis=0).astype(ref.dtype)


def turn_x_kernel(after_ref, *refs):
    for ref, value in zip(refs[-2:], halves(refs[:-2])):
        ref[...] = value.astype(ref.dtype)


def join_kernel(after_ref, x_ref, *refs):
    refs, (d_ref, own_ref) = refs[:-2], refs[-2:]
    rows = x_ref.shape[0]
    value = jnp.concatenate(halves(refs), axis=0).astype(d_ref.dtype)
    d_ref[...] = value
    own_ref[:rows, :] = x_ref[...]
    own_ref[rows:, :] = value


def copy_share(which_ref, source, target, sem):
    share = target.shape[0]
    start = pl.multiple_of(which_ref[0] * share, share)
    return pltpu.make_async_copy(source.at[pl.ds(start, share), :], target, sem)


def forward_kernel(after_ref, x_ref, d_ref, out_ref):
    gather_rows((x_ref, d_ref), out_ref)


def tile_copies(pairs, sems, i, tile):
    here = block(i, tile)
    return [
        pltpu.make_async_copy(source.at[here, :], target.at[here, :], sems.at[i, k])
        for k, (source, target) in enumerate(pairs)
    ]


def over_tiles(pairs, sems, steps, tile, work):
    def start(i):
        for copy in tile_copies(pairs, sems, i, tile):
            copy.start()

    start(0)
    start(1)

    def step(i, carry):
        @pl.when(i + 2 < steps)
        def _():
            start(i + 2)

        for copy in tile_copies(pairs, sems, i, tile):
            copy.wait()
        work(i)
        return carry

    lax.fori_loop(0, steps, step, 0)


def own_first_kernel(rows_ref, first_src, hidden_ref, slope_ref, first_ref, sems):
    steps, tile = hidden_ref.shape[0], hidden_ref.shape[2]

    def work(i):
        hidden, slope = gelu_and_slope(dot_nt(rows_ref[...], first_ref[block(i, tile), :]))
        hidden_ref[i] = hidden
        slope_ref[i] = slope.astype(slope_ref.dtype)

    over_tiles([(first_src, first_ref)], sems, steps, tile, work)


def own_second_kernel(
    rows_ref,
    hidden_ref,
    slope_ref,
    first_src,
    second_src,
    total_ref,
    gate_ref,
    first_ref,
    second_ref,
    sems,
):
    steps, tile = hidden_ref.shape[0], hidden_ref.shape[2]
    total_ref[...] = jnp.zeros_like(total_ref)
    gate_ref[...] = jnp.zeros_like(gate_ref)

    def work(j):
        here = block(j, tile)
        back = dot_nt(rows_ref[...], second_ref[here, :])
        terms = hidden_ref[j].astype(jnp.float32) * back
        gate = gate_ref[...]
        for i in range(tile // LANES):
            gate = gate + terms[:, i * LANES : (i + 1) * LANES]
        gate_ref[...] = gate
        d_pre = (back * slope_ref[j].astype(jnp.float32)).astype(jnp.bfloat16)
        total_ref[...] += dot_nn(d_pre, first_ref[here, :])

    over_tiles([(second_src, second_ref), (first_src, first_ref)], sems, steps, tile, work)


def chunks_kernel(cap_rows, me_ref, x_over, core, total_ref, gate_ref, out_ref):
    experts = out_ref.shape[0]
    total = total_ref[...]
    gates = jnp.sum(gate_ref[...], axis=1, keepdims=True)
    lane = lax.broadcasted_iota(jnp.int32, (SUBLANES, LANES), 1)
    for k in range(experts):
        start = k * cap_rows
        tail = jnp.zeros((SUBLANES, LANES), jnp.float32)
        for i in range(cap_rows // SUBLANES):
            here = start + i * SUBLANES
            tail = jnp.where(lane == i, gates[here : here + SUBLANES], tail)
        parts = [
            total[start : start + cap_rows, i * LANES : (i + 1) * LANES]
            for i in range(total.shape[1] // LANES)
        ]
        source = me_ref[0] ^ (2 * (k % (experts // 2)) + k // (experts // 2))
        out_ref[source] = jnp.concatenate(parts + [tail], axis=0).astype(out_ref.dtype)


def gather_rows(refs, all_ref):
    rows = refs[0].shape[0]
    for i, ref in enumerate(refs):
        all_ref[i * rows : (i + 1) * rows, :] = ref[...]


def block(i, tile=256):
    return pl.ds(pl.multiple_of(i * tile, tile), tile)


def gelu_rows(weights_ref, rows_ref, hidden_ref, slope_ref):
    tile = weights_ref.shape[0] // 2

    def step(i, carry):
        here = block(i, tile)
        hidden, slope = gelu_and_slope(dot_nt(weights_ref[here, :], rows_ref[...]))
        hidden_ref[here, :] = hidden
        slope_ref[here, :] = slope.astype(slope_ref.dtype)
        return carry

    lax.fori_loop(0, 2, step, 0)


def weight_terms(weights_ref, x_ref, d_ref, hidden_ref, slope_ref, finish):
    tile = weights_ref.shape[0] // 2

    def step(i, carry):
        here = block(i, tile)
        back = dot_nt(weights_ref[here, :], d_ref[...])
        d_pre = (back * slope_ref[here, :].astype(jnp.float32)).astype(jnp.bfloat16)
        finish(i, here, dot_nn(d_pre, x_ref[...]), dot_nn(hidden_ref[here, :], d_ref[...]))
        return carry

    lax.fori_loop(0, 2, step, 0)


def near_first_kernel(
    which_ref,
    after_ref,
    a_ref,
    b_ref,
    first_src,
    second_src,
    hidden_ref,
    slope_ref,
    all_ref,
    first_ref,
    second_ref,
    sems,
):
    first_copy = copy_share(which_ref, first_src, first_ref, sems.at[0])
    second_copy = copy_share(which_ref, second_src, second_ref, sems.at[1])
    first_copy.start()
    second_copy.start()
    rows = a_ref.shape[0] // 2
    gather_rows((a_ref.at[:rows], b_ref.at[:rows]), all_ref)
    first_copy.wait()
    gelu_rows(first_ref, all_ref, hidden_ref, slope_ref)
    second_copy.wait()


def near_second_kernel(
    after_ref, a_ref, b_ref, x_ref, hidden_ref, slope_ref, second_ref, gin_ref, gout_ref, all_ref
):
    rows = a_ref.shape[0] // 2
    gather_rows((a_ref.at[rows:], b_ref.at[rows:]), all_ref)

    def finish(i, here, gin, gout):
        gin_ref[here, :] = gin
        gout_ref[here, :] = gout

    weight_terms(second_ref, x_ref, all_ref, hidden_ref, slope_ref, finish)


def far_first_kernel(after_ref, x_over, diagonal_ref, first_ref, hidden_ref, slope_ref, x_ref):
    gather_rows((x_over, diagonal_ref.at[: x_over.shape[0]]), x_ref)
    gelu_rows(first_ref, x_ref, hidden_ref, slope_ref)


def far_second_kernel(
    after_ref,
    d_over,
    diagonal_ref,
    x_ref,
    hidden_ref,
    slope_ref,
    second_ref,
    gin_near,
    gout_near,
    gin_out,
    gout_out,
    d_ref,
    gin_ref,
    gout_ref,
    sems,
):
    gather_rows((d_over, diagonal_ref.at[d_over.shape[0] :]), d_ref)
    tile = second_ref.shape[0] // 2

    def copies(i):
        here = block(i, tile)
        return [
            pltpu.make_async_copy(gin_ref.at[here, :], gin_out.at[here, :], sems.at[i, 0]),
            pltpu.make_async_copy(gout_ref.at[here, :], gout_out.at[here, :], sems.at[i, 1]),
        ]

    def finish(i, here, gin, gout):
        gin_ref[here, :] = (gin_near[here, :] + gin).astype(gin_ref.dtype)
        gout_ref[here, :] = (gout_near[here, :] + gout).astype(gout_ref.dtype)
        for copy in copies(i):
            copy.start()

    weight_terms(second_ref, x_ref, d_ref, hidden_ref, slope_ref, finish)
    for i in range(2):
        for copy in copies(i):
            copy.wait()


def unpack_kernel(
    cap_rows, after_ref, back_ref, gate_ref, expert_ref, slot_ref, tok_ref, dgate_ref
):
    experts = back_ref.shape[0]
    blocks = tok_ref.shape[1] // LANES
    lane = lax.broadcasted_iota(jnp.int32, (SUBLANES, LANES), 1)
    rows, gates = [], []
    for e in range(experts):
        value = back_ref[e].astype(jnp.float32)
        pieces = [value[i * cap_rows : (i + 1) * cap_rows] for i in range(blocks)]
        rows.append(jnp.concatenate(pieces, axis=1))
        tail = value[cap_rows * blocks :]
        gates += [jnp.where(lane == i, tail, 0.0) for i in range(cap_rows // SUBLANES)]
    rows = jnp.concatenate(rows, axis=0).astype(jnp.bfloat16)
    gates = jnp.concatenate(gates, axis=0).astype(jnp.bfloat16)
    chosen = owner_table(expert_ref[...], slot_ref[...], cap_rows, experts * cap_rows)
    table = chosen.astype(jnp.bfloat16)
    tok_ref[...] = dot_tn(table, rows).astype(jnp.bfloat16)
    picked = jnp.sum(dot_tn(gates, table), axis=0, keepdims=True)
    dgate_ref[...] = picked / gate_ref[...]


def in_hbm(*arrays):
    return [pltpu.with_memory_space_constraint(a, pltpu.HBM) for a in arrays]


def body(tokens, upstream, gate_prob, expert_id, slot_index, segment_id, weight_in, weight_out):
    experts = lax.axis_size("expert")
    groups = lax.axis_size("dp")
    tok_rows, width = tokens.shape
    hidden_units = weight_in.shape[1]
    capacity = 5 * tok_rows // (4 * experts)
    cap_rows = -(-capacity // SUBLANES) * SUBLANES
    slots = experts * cap_rows
    share = hidden_units // groups
    gate_row = gate_prob.reshape(1, tok_rows)
    expert_row = expert_id.reshape(1, tok_rows)
    slot_row = slot_index.reshape(1, tok_rows)
    pairs = experts // 2
    which = lax.axis_index("dp").astype(jnp.int32).reshape(1)
    me = lax.axis_index("expert").astype(jnp.int32).reshape(1)
    bf16 = jnp.bfloat16
    anywhere = pl.BlockSpec(memory_space=pl.ANY)
    smem = pl.BlockSpec(memory_space=pltpu.SMEM)
    vmem = pl.BlockSpec(memory_space=pltpu.VMEM)

    unit = 2 * slots * width * hidden_units

    def call(kernel, name, ins, outs, scratch=(), out_spec=vmem, limit=10, work=0.0):
        return pl.pallas_call(
            kernel,
            in_specs=ins,
            out_specs=[out_spec] * len(outs),
            out_shape=[jax.ShapeDtypeStruct(shape, dtype) for shape, dtype in outs],
            scratch_shapes=list(scratch),
            compiler_params=pltpu.CompilerParams(vmem_limit_bytes=limit * MIB),
            cost_estimate=pl.CostEstimate(
                flops=int(work * unit), bytes_accessed=int(work * unit) // 512, transcendentals=0
            ),
            name=name,
        )

    def across(chunk, mask):
        return lax.ppermute(chunk, "expert", [(i, i ^ mask) for i in range(experts)])

    def over(chunk, mask):
        return lax.ppermute(chunk, "dp", [(i, i ^ mask) for i in range(groups)])

    row = (1, tok_rows)
    part = ((2 * cap_rows, width), bf16)
    half = ((pairs * cap_rows, width), bf16)
    *x_parts, d_keep, d_cross = call(
        partial(pack_kernel, cap_rows, experts),
        "pack",
        [smem] + [anywhere] * 6,
        [part] * pairs + [half] * 2,
        [
            pltpu.VMEM((tok_rows, width), bf16),
            pltpu.VMEM((tok_rows, width), bf16),
            pltpu.VMEM(row, jnp.float32),
            pltpu.VMEM(row, jnp.int32),
            pltpu.VMEM(row, jnp.int32),
            pltpu.VMEM(row, jnp.int32),
            pltpu.SemaphoreType.DMA((6,)),
        ],
    )(me, *in_hbm(tokens, upstream, gate_row, expert_row, slot_row, segment_id))
    order = list(range(pairs - 1, 0, -1))
    x_near = {s: across(x_parts[s], 2 * s) for s in order}
    x_near = [x_parts[0]] + [x_near[s] for s in range(1, pairs)]
    d_near = across(d_cross, 1)
    d_parts = call(
        partial(turn_d_kernel, pairs),
        "turn_d",
        [vmem] * 2,
        [part] * pairs,
    )(d_keep, d_near)
    x_keep, x_cross = call(
        turn_x_kernel,
        "turn_x",
        [anywhere] + [vmem] * pairs,
        [half] * 2,
    )(d_parts[0], *x_near)
    d_far = {s: across(d_parts[s], 2 * s) for s in order}
    d_far = [d_parts[0]] + [d_far[s] for s in range(1, pairs)]
    x_own = jnp.concatenate([x_keep, across(x_cross, 1)], axis=0)

    wide = ((groups, slots, share), bf16)
    weights = pltpu.VMEM((hidden_units, width), bf16)
    hidden, slope = call(
        own_first_kernel,
        "own_first",
        [vmem, anywhere],
        [wide] * 2,
        [weights, pltpu.SemaphoreType.DMA((groups, 1))],
        limit=20,
        work=1,
    )(x_own, *in_hbm(weight_in[0]))
    pair_rows = ((2 * slots, width), bf16)
    d_own, own = call(
        join_kernel,
        "join",
        [anywhere] + [vmem] * (pairs + 1),
        [((slots, width), bf16), pair_rows],
    )(hidden, x_own, *d_far)
    x_over, d_over, core = over(x_own, 2), over(d_own, 2), over(own, 1)

    stride = cap_rows * width // LANES + SUBLANES
    total, gates = call(
        own_second_kernel,
        "own_second",
        [vmem] * 3 + [anywhere] * 2,
        [((slots, width), jnp.float32), ((slots, LANES), jnp.float32)],
        [weights, weights, pltpu.SemaphoreType.DMA((groups, 2))],
        limit=24,
        work=20,
    )(d_own, hidden, slope, *in_hbm(weight_in[0], weight_out[0]))
    (back,) = call(
        partial(chunks_kernel, cap_rows),
        "chunks",
        [smem] + [anywhere] * 2 + [vmem] * 2,
        [((experts, stride, LANES), bf16)],
    )(me, x_over, core, total, gates)
    returned = lax.all_to_all(back, "expert", split_axis=0, concat_axis=0, tiled=True)

    wide = ((share, 2 * slots), bf16)
    share_rows = ((share, width), bf16)
    term = ((share, width), jnp.float32)
    hidden_t, slope_t, x_near, first_share, second_share = call(
        near_first_kernel,
        "near_first",
        [smem] + [anywhere] + [vmem] * 2 + [anywhere] * 2,
        [wide, wide, pair_rows, share_rows, share_rows],
        [pltpu.SemaphoreType.DMA((2,))],
        work=0.5,
    )(which, back, own, core, *in_hbm(weight_in[0], weight_out[0]))
    gin_near, gout_near = call(
        near_second_kernel,
        "near_second",
        [anywhere] + [vmem] * 6,
        [term, term],
        [pltpu.VMEM(*pair_rows)],
        work=15,
    )(back, own, core, x_near, hidden_t, slope_t, second_share)
    (moved,) = call(
        forward_kernel,
        "forward",
        [anywhere, vmem, vmem],
        [pair_rows],
    )(hidden_t, x_over, d_over)
    diagonal = over(moved, 1)
    hidden_t, slope_t, x_far = call(
        far_first_kernel,
        "far_first",
        [anywhere] + [vmem] * 3,
        [wide, wide, pair_rows],
    )(gin_near, x_over, diagonal, first_share)
    share_block = pltpu.VMEM((share, width), bf16)
    grad_first, grad_second = call(
        far_second_kernel,
        "far_second",
        [anywhere] + [vmem] * 8,
        [share_rows] * 2,
        [pltpu.VMEM(*pair_rows), share_block, share_block, pltpu.SemaphoreType.DMA((2, 2))],
        out_spec=anywhere,
        limit=20,
    )(hidden_t, d_over, diagonal, x_far, hidden_t, slope_t, second_share, gin_near, gout_near)

    d_tokens, d_gate = call(
        partial(unpack_kernel, cap_rows),
        "unpack",
        [anywhere] + [vmem] * 4,
        [((tok_rows, width), bf16), (row, jnp.float32)],
    )(*in_hbm(grad_first), returned, gate_row, expert_row, slot_row)
    return (d_tokens, d_gate.reshape(tok_rows), grad_first[None], grad_second[None])


def solution(mesh):
    in_specs = (
        P(("dp", "expert"), None),
        P(("dp", "expert"), None),
        P(("dp", "expert")),
        P(("dp", "expert")),
        P(("dp", "expert")),
        P(("dp", "expert"), None),
        P("expert", None, None),
        P("expert", None, None),
    )
    out_specs = (
        P(("dp", "expert"), None),
        P(("dp", "expert")),
        P("expert", "dp", None),
        P("expert", "dp", None),
    )
    return jax.shard_map(body, mesh=mesh, in_specs=in_specs, out_specs=out_specs, check_vma=False)
```

time: 173 us -> 63.8 us (0.37)
  waiting for transfers between devices: 81.5 us -> 13.5 us
  matrix products: 35.9 us -> 0 us
  Pallas kernels: 0 us -> 28.4 us
  local copies, waits for them, and re-layouts: 16 us -> 0.05 us
  between operations: 14.2 us -> 0.8 us
  starting transfers between devices: 23 us -> 20.7 us
  other arithmetic: 1.91 us -> 0 us
    reduce_scatter x2 -> x0, waiting for transfers between devices: 50.1 us -> none  [the longest x1 50.1 us: body(): lax.psum_scatter(jnp.einsum('rf,rd->fd', columns, x_flat, preferred_eleme...]
    dot_general x6 -> x0, matrix products: 35.9 us -> none  [the longest x1 7.3 us: body(): jnp.einsum('skd,fd->skf', d_out, second_weight, preferred_element_type=jn...]
    all_to_all x5 -> x1, waiting for transfers between devices: 31.4 us -> 2.34 us  [body(): lax.all_to_all(back, 'expert', split_axis=0, concat_axis=0, tiled=True)]
    pallas_call x0 -> x13, Pallas kernels: none -> 28.4 us  [the longest x1 7.24 us: body(): call(own_second_kernel, 'own_second', [vmem] * 3 + [anywhere] * 2, [((slo...]
    all_to_all x5 -> x1, starting transfers between devices: 22.7 us -> 5.17 us  [body(): lax.all_to_all(back, 'expert', split_axis=0, concat_axis=0, tiled=True)]
    ppermute x0 -> x12, starting transfers between devices: none -> 15.5 us  [the longest x8 12.4 us: across(): lax.ppermute(chunk, 'expert', [(i, i ^ mask) for i in range(experts)])]
    gather x5 -> x0, local copies, waits for them, and re-layouts: 12.1 us -> none  [pick_rows(): return jnp.concatenate([values, padding], axis=0)[owners]]
    ppermute x0 -> x12, waiting for transfers between devices: none -> 11.2 us  [the longest x8 11.2 us: across(): lax.ppermute(chunk, 'expert', [(i, i ^ mask) for i in range(experts)])]
  transfers between devices with their start and end apart: 7 -> 13, of which waited for: 6 -> 6; matrix products, arithmetic and copies ran while one was open for 24% -> 0% of each run, Pallas kernels for 0% -> 40%
where the time goes in v1:
time: 63.8 us; the launch traced here: 63.5 us
  Pallas kernels  28.4 us (45%)
  starting transfers between devices  20.7 us (32%)
  waiting for transfers between devices  13.5 us (21%)
  between operations  0.8 us (1%)
    ppermute x8, starting transfers between devices, across(): lax.ppermute(chunk, 'expert', [(i, i ^ mask) for i in range(experts)])  12.4 us
    ppermute x8, waiting for transfers between devices, across(): lax.ppermute(chunk, 'expert', [(i, i ^ mask) for i in range(experts)])  11.2 us
    pallas_call x1, Pallas kernels, body(): call(own_second_kernel, 'own_second', [vmem] * 3 + [anywhere] * 2, [((slo...  7.24 us
    all_to_all x1, starting transfers between devices, body(): lax.all_to_all(back, 'expert', split_axis=0, concat_axis=0, tiled=True)  5.17 us
    pallas_call x1, Pallas kernels, body(): call(own_first_kernel, 'own_first', [vmem, anywhere], [wide] * 2, [weight...  4.5 us
    pallas_call x1, Pallas kernels, body(): call(far_second_kernel, 'far_second', [anywhere] + [vmem] * 8, [share_row...  4.06 us
    pallas_call x1, Pallas kernels, body(): call(near_second_kernel, 'near_second', [anywhere] + [vmem] * 6, [term, t...  3.2 us
    ppermute x4, starting transfers between devices, over(): return lax.ppermute(chunk, 'dp', [(i, i ^ mask) for i in range(groups)])  3.11 us
  transfers between devices with their start and end apart: 13, of which 6 were waited for; matrix products, arithmetic and copies ran while one was open for 0% of the time, Pallas kernels for 40%

profile of v1, /device:TPU:0, one launch (start us, length us, event | category | flops | bytes accessed | tf_op | source)
XLA Modules:
  0.0 63.5 jit_solution(7142730612023947507)
XLA Ops:
  0.6 1.6 %pack.1 = (bf16[80,768]{1,0:T(8,128)(2,1)S(1)}, bf16[80,768]{1,0:T(8,128)(2,1)S(1)}, bf16[80,768]{1,0:T(8,128)(2,1)S(1)}, bf16[80,768]{1,0:T(8,128)(2,1)S(1)}, b...) custom-call(s32[1]{0:T(128)} %bitcast.me_ref, bf16[256,768]{1,0:T(8,128)(2,1)} %refs_0_.1, ...), custom_call_target="tpu_custom_call" | custom-call | tf_op jit(solution)/shard_map/pack/pallas_call | solution.py:398
  2.3 3.0 %collective-permute-start = (bf16[160,768]{1,0:T(8,128)(2,1)S(1)}, bf16[160,768]{1,0:T(8,128)(2,1)S(1)}, u32[]{:S(2)}, u32[]{:S(2)}) collective-permute-start(bf16[160,768]{1,0:T(8,128)(2,1)S(1)} %get-tuple-element.37), channel_id=1, source_target_pairs={{0,1},{1,0},{2,3},{3,2},{4,5},{5,4},{6,7},{7,6},{8,9},{9,8},{10,11... | collective-permute-start | bytes 737288 | tf_op jit(solution)/shard_map/ppermute | solution.py:390
  5.3 1.6 %collective-permute-start.1 = (bf16[80,768]{1,0:T(8,128)(2,1)S(1)}, bf16[80,768]{1,0:T(8,128)(2,1)S(1)}, u32[]{:S(2)}, u32[]{:S(2)}) collective-permute-start(bf16[80,768]{1,0:T(8,128)(2,1)S(1)} %get-tuple-element.40), channel_id=1, source_target_pairs={{0,2},{1,3},{2,0},{3,1},{4,6},{5,7},{6,4},{7,5},{8,10},{9,11},{10,... | collective-permute-start | bytes 368648 | tf_op jit(solution)/shard_map/ppermute | solution.py:390
  6.9 2.6 %collective-permute-start.2 = (bf16[80,768]{1,0:T(8,128)(2,1)S(1)}, bf16[80,768]{1,0:T(8,128)(2,1)S(1)}, u32[]{:S(2)}, u32[]{:S(2)}) collective-permute-start(bf16[80,768]{1,0:T(8,128)(2,1)S(1)} %get-tuple-element.41), channel_id=1, source_target_pairs={{0,4},{1,5},{2,6},{3,7},{4,0},{5,1},{6,2},{7,3},{8,12},{9,13},{10,... | collective-permute-start | bytes 368648 | tf_op jit(solution)/shard_map/ppermute | solution.py:390
  9.5 0.2 collective-permute-start.3
  9.7 1.6 %collective-permute-done.near_ref = bf16[160,768]{1,0:T(8,128)(2,1)S(1)} collective-permute-done((bf16[160,768]{1,0:T(8,128)(2,1)S(1)}, bf16[160,768]{1,0:T(8,128)(2,1)S(1)}, u32[]{:S(2)}, u32[]{:S(2)}) %collective-permute-start) | collective-permute-done | bytes 245792 | tf_op jit(solution)/shard_map/ppermute | solution.py:390
  11.3 0.2 collective-permute-done.1.refs_1_
  11.5 7.4 %collective-permute-done.2.refs_2_ = bf16[80,768]{1,0:T(8,128)(2,1)S(1)} collective-permute-done((bf16[80,768]{1,0:T(8,128)(2,1)S(1)}, bf16[80,768]{1,0:T(8,128)(2,1)S(1)}, u32[]{:S(2)}, u32[]{:S(2)}) %collective-permute-start.2) | collective-permute-done | bytes 122912 | tf_op jit(solution)/shard_map/ppermute | solution.py:390
  18.9 0.0 collective-permute-done.3.refs_3_
  19.0 0.6 collective-permute-start.4
  19.5 1.9 %collective-permute-start.6 = (bf16[80,768]{1,0:T(8,128)(2,1)S(1)}, bf16[80,768]{1,0:T(8,128)(2,1)S(1)}, u32[]{:S(2)}, u32[]{:S(2)}) collective-permute-start(bf16[80,768]{1,0:T(8,128)(2,1)S(1)} %get-tuple-element.46), channel_id=1, source_target_pairs={{0,2},{1,3},{2,0},{3,1},{4,6},{5,7},{6,4},{7,5},{8,10},{9,11},{10,... | collective-permute-start | bytes 368648 | tf_op jit(solution)/shard_map/ppermute | solution.py:390
  21.4 1.2 %collective-permute-start.7 = (bf16[80,768]{1,0:T(8,128)(2,1)S(1)}, bf16[80,768]{1,0:T(8,128)(2,1)S(1)}, u32[]{:S(2)}, u32[]{:S(2)}) collective-permute-start(bf16[80,768]{1,0:T(8,128)(2,1)S(1)} %get-tuple-element.47), channel_id=1, source_target_pairs={{0,4},{1,5},{2,6},{3,7},{4,0},{5,1},{6,2},{7,3},{8,12},{9,13},{10,... | collective-permute-start | bytes 368648 | tf_op jit(solution)/shard_map/ppermute | solution.py:390
  22.6 1.4 %collective-permute-start.8 = (bf16[80,768]{1,0:T(8,128)(2,1)S(1)}, bf16[80,768]{1,0:T(8,128)(2,1)S(1)}, u32[]{:S(2)}, u32[]{:S(2)}) collective-permute-start(bf16[80,768]{1,0:T(8,128)(2,1)S(1)} %get-tuple-element.48), channel_id=1, source_target_pairs={{0,6},{1,7},{2,4},{3,5},{4,2},{5,3},{6,0},{7,1},{8,14},{9,15},{10,... | collective-permute-start | bytes 368648 | tf_op jit(solution)/shard_map/ppermute | solution.py:390
  23.9 1.3 %collective-permute-done.4 = bf16[160,768]{1,0:T(8,128)(2,1)S(1)} collective-permute-done((bf16[160,768]{1,0:T(8,128)(2,1)S(1)}, bf16[160,768]{1,0:T(8,128)(2,1)S(1)}, u32[]{:S(2)}, u32[]{:S(2)}) %collective-permute-start.4) | collective-permute-done | bytes 245792 | tf_op jit(solution)/shard_map/ppermute | solution.py:390
  25.2 1.6 %collective-permute-start.5 = (bf16[320,768]{1,0:T(8,128)(2,1)S(1)}, bf16[320,768]{1,0:T(8,128)(2,1)S(1)}, u32[]{:S(2)}, u32[]{:S(2)}) collective-permute-start(bf16[320,768]{1,0:T(8,128)(2,1)S(1)} %constant_dynamic-update-slice_fusion.rows_ref.x_ref), channel_id=1, source_target_pairs={{0,16},{8,24},{16,0},{24,8},{1,17},{9,25},{17,1},{25,9},{2,18},{10... | collective-permute-start | bytes 1474568 | tf_op jit(solution)/shard_map/ppermute | solution.py:393
  26.8 4.5 %own_first.1 = (bf16[4,320,768]{2,1,0:T(8,128)(2,1)S(1)}, bf16[4,320,768]{2,1,0:T(8,128)(2,1)S(1)}) custom-call(bf16[320,768]{1,0:T(8,128)(2,1)S(1)} %constant_dynamic-update-slice_fusion.rows_ref.x_ref, bf16[3072,768]{1,0:T(8,128)(2,1)} %bitcast.16), custom_call_target="tpu_custom_call" | custom-call | flops 1509949440 | bytes 2949120 | tf_op jit(solution)/shard_map/own_first/pallas_call | solution.py:435
  31.3 0.0 collective-permute-done.6.refs_1_
  31.3 0.7 %collective-permute-done.7.refs_2_ = bf16[80,768]{1,0:T(8,128)(2,1)S(1)} collective-permute-done((bf16[80,768]{1,0:T(8,128)(2,1)S(1)}, bf16[80,768]{1,0:T(8,128)(2,1)S(1)}, u32[]{:S(2)}, u32[]{:S(2)}) %collective-permute-start.7) | collective-permute-done | bytes 122912 | tf_op jit(solution)/shard_map/ppermute | solution.py:390
  32.0 0.0 collective-permute-done.8.refs_3_
  32.0 0.9 %join.1 = (bf16[320,768]{1,0:T(8,128)(2,1)}, bf16[640,768]{1,0:T(8,128)(2,1)S(1)}) custom-call(bf16[4,320,768]{2,1,0:T(8,128)(2,1)S(1)} %get-tuple-element.45.after_ref.hidden_ref, bf16[320,768]{1,0:T(8,128)(2,1)S(1)} %constant_dynamic-update-slice_fusion.rows_ref.x_ref, bf16[80,768]{1,0:T(8,128)(2,1)S(1)} %get-tuple-element.38.after_ref.refs_0_, ...), custom_call_target="tpu_custom_call" | custom-call | tf_op jit(solution)/shard_map/join/pallas_call | solution.py:445
  32.9 0.0 collective-permute-start.9
  32.9 1.5 %collective-permute-start.10 = (bf16[320,768]{1,0:T(8,128)(2,1)}, bf16[320,768]{1,0:T(8,128)(2,1)S(1)}, u32[]{:S(2)}, u32[]{:S(2)}) collective-permute-start(bf16[320,768]{1,0:T(8,128)(2,1)} %get-tuple-element.50.rows_ref), channel_id=1, source_target_pairs={{0,16},{8,24},{16,0},{24,8},{1,17},{9,25},{17,1},{25,9},{2,18},{10... | collective-permute-start | bytes 1474568 | tf_op jit(solution)/shard_map/ppermute | solution.py:393
  34.4 7.2 %own_second.1 = (f32[320,768]{1,0:T(8,128)S(1)}, f32[320,128]{1,0:T(8,128)S(1)}) custom-call(bf16[320,768]{1,0:T(8,128)(2,1)} %get-tuple-element.50.rows_ref, bf16[4,320,768]{2,1,0:T(8,128)(2,1)S(1)} %get-tuple-element.45.after_ref.hidden_ref, bf16[4,320,768]{2,1,0:T(8,128)(2,1)S(1)} %get-tuple-element.51.slope_ref, bf16[3072,768]{1,0:T(8,128)(2,1)} %bitcast.17, ...), custom_call_target="tpu_custom_call" | custom-call | flops 30198988800 | bytes 58982400 | tf_op jit(solution)/shard_map/own_second/pallas_call | solution.py:454
  41.6 0.0 collective-permute-done.5.x_over.x_ref
  41.6 0.0 collective-permute-done.9.core.b_ref
  41.6 0.9 %chunks.1.after_ref = bf16[8,248,128]{2,1,0:T(8,128)(2,1)} custom-call(s32[1]{0:T(128)} %bitcast.me_ref, bf16[320,768]{1,0:T(8,128)(2,1)S(1)} %collective-permute-done.5.x_over.x_ref, bf16[640,768]{1,0:T(8,128)(2,1)S(1)} %collective-permute-done.9.core.b_ref, f32[320,768]{1,0:T(8,128)S(1)} %get-tuple-element.52.total_ref, ...), custom_call_target="tpu_custom_call" | custom-call | tf_op jit(solution)/shard_map/chunks/pallas_call | solution.py:463
  42.6 5.2 %all-to-all-start = ((bf16[8,248,128]{2,1,0:T(8,128)(2,1)}), bf16[8,248,128]{2,1,0:T(8,128)(2,1)S(1)}, u32[]{:S(2)}, u32[]{:S(2)}) async-start(bf16[8,248,128]{2,1,0:T(8,128)(2,1)} %chunks.1.after_ref), calls=%async_computation | async-start | bytes 1015808 | tf_op jit(solution)/shard_map/all_to_all | solution.py:469
  47.7 3.0 %near_first.1 = (bf16[768,640]{1,0:T(8,128)(2,1)S(1)}, bf16[768,640]{1,0:T(8,128)(2,1)S(1)}, bf16[640,768]{1,0:T(8,128)(2,1)S(1)}, bf16[768,768]{1,0:T(8,128)(2,1)S(1)}, bf16[768,768]{1,0:T(8,128)(2,1)S(1)}) custom-call(s32[1]{0:T(128)} %bitcast.6.which_ref, bf16[8,248,128]{2,1,0:T(8,128)(2,1)} %chunks.1.after_ref, ...), custom_call_target="tpu_custom_call" | custom-call | flops 754974720 | bytes 1474560 | tf_op jit(solution)/shard_map/near_first/pallas_call | solution.py:474
  50.7 0.0 collective-permute-done.10.d_ref.d_over
  50.7 0.1 forward.1
  50.8 0.1 collective-permute-start.11
  50.9 3.2 %near_second.1 = (f32[768,768]{1,0:T(8,128)S(1)}, f32[768,768]{1,0:T(8,128)S(1)}) custom-call(bf16[8,248,128]{2,1,0:T(8,128)(2,1)} %chunks.1.after_ref, bf16[640,768]{1,0:T(8,128)(2,1)S(1)} %get-tuple-element.49.a_ref, bf16[640,768]{1,0:T(8,128)(2,1)S(1)} %collective-permute-done.9.core.b_ref, bf16[640,768]{1,0:T(8,128)(2,1)S(1)} %get-tuple-element.54.x_ref, ...), custom_call_target="tpu_custom_call" | custom-call | flops 22649241600 | bytes 44236800 | tf_op jit(solution)/shard_map/near_second/pallas_call | solution.py:482
  54.1 0.0 collective-permute-done.11.diagonal_ref
  54.1 1.7 %far_first.1 = (bf16[768,640]{1,0:T(8,128)(2,1)S(1)}, bf16[768,640]{1,0:T(8,128)(2,1)S(1)}, bf16[640,768]{1,0:T(8,128)(2,1)S(1)}) custom-call(f32[768,768]{1,0:T(8,128)S(1)} %get-tuple-element.58.after_ref.gin_near, bf16[320,768]{1,0:T(8,128)(2,1)S(1)} %collective-permute-done.5.x_over.x_ref, bf16[640,768]{1,0:T(8,128)(2,1)S(1)} %collective-permute-done.11.diagonal_ref, ...), custom_call_target="tpu_custom_call" | custom-call | tf_op jit(solution)/shard_map/far_first/pallas_call | solution.py:497
  55.8 0.0 copy-start
  55.8 0.0 copy-start.1
  55.8 0.0 copy-start.2
  55.8 4.1 %far_second.1 = (bf16[768,768]{1,0:T(8,128)(2,1)}, bf16[768,768]{1,0:T(8,128)(2,1)}) custom-call(bf16[768,640]{1,0:T(8,128)(2,1)S(1)} %get-tuple-element.60.after_ref.hidden_ref, bf16[320,768]{1,0:T(8,128)(2,1)S(1)} %collective-permute-done.10.d_ref.d_over, bf16[640,768]{1,0:T(8,128)(2,1)S(1)} %collective-permute-done.11.diagonal_ref, ...), custom_call_target="tpu_custom_call" | custom-call | tf_op jit(solution)/shard_map/far_second/pallas_call | solution.py:504
  59.9 2.3 %all-to-all-done.back_ref = bf16[8,248,128]{2,1,0:T(8,128)(2,1)S(1)} async-done(((bf16[8,248,128]{2,1,0:T(8,128)(2,1)}), bf16[8,248,128]{2,1,0:T(8,128)(2,1)S(1)}, u32[]{:S(2)}, u32[]{:S(2)}) %all-to-all-start) | async-done | bytes 507936 | tf_op jit(solution)/shard_map/all_to_all | solution.py:469
  62.3 0.0 copy-done
  62.3 0.0 copy-done.1
  62.3 0.0 copy-done.2
  62.3 1.2 %unpack.1 = (bf16[256,768]{1,0:T(8,128)(2,1)}, f32[1,256]{1,0:T(1,128)}) custom-call(bf16[768,768]{1,0:T(8,128)(2,1)} %get-tuple-element.64.after_ref, bf16[8,248,128]{2,1,0:T(8,128)(2,1)S(1)} %all-to-all-done.back_ref, f32[1,256]{1,0:T(1,128)S(1)} %bitcast.11, s32[1,256]{1,0:T(1,128)S(1)} %bitcast.13, s32[1,256]{1,0:T(1,128)S(1)} %bitcast.15), custom_call_target="tpu_custom_call" | custom-call | tf_op jit(solution)/shard_map/unpack/pallas_call | solution.py:514
  (4 shorter events, 0.1 us)
Async XLA Ops:
  2.3 9.0 %collective-permute-start = (bf16[160,768]{1,0:T(8,128)(2,1)S(1)}, bf16[160,768]{1,0:T(8,128)(2,1)S(1)}, u32[]{:S(2)}, u32[]{:S(2)}) collective-permute-start(bf16[160,768]{1,0:T(8,128)(2,1)S(1)} %get-tuple-element.37), channel_id=1, source_target_pairs={{0,1},{1,0},{2,3},{3,2},{4,5},{5,4},{6,7},{7,6},{8,9},{9,8},{10,11... | collective-permute-start | bytes 737288 | tf_op jit(solution)/shard_map/ppermute | solution.py:390
  5.3 6.2 %collective-permute-start.1 = (bf16[80,768]{1,0:T(8,128)(2,1)S(1)}, bf16[80,768]{1,0:T(8,128)(2,1)S(1)}, u32[]{:S(2)}, u32[]{:S(2)}) collective-permute-start(bf16[80,768]{1,0:T(8,128)(2,1)S(1)} %get-tuple-element.40), channel_id=1, source_target_pairs={{0,2},{1,3},{2,0},{3,1},{4,6},{5,7},{6,4},{7,5},{8,10},{9,11},{10,... | collective-permute-start | bytes 368648 | tf_op jit(solution)/shard_map/ppermute | solution.py:390
  6.9 12.0 %collective-permute-start.2 = (bf16[80,768]{1,0:T(8,128)(2,1)S(1)}, bf16[80,768]{1,0:T(8,128)(2,1)S(1)}, u32[]{:S(2)}, u32[]{:S(2)}) collective-permute-start(bf16[80,768]{1,0:T(8,128)(2,1)S(1)} %get-tuple-element.41), channel_id=1, source_target_pairs={{0,4},{1,5},{2,6},{3,7},{4,0},{5,1},{6,2},{7,3},{8,12},{9,13},{10,... | collective-permute-start | bytes 368648 | tf_op jit(solution)/shard_map/ppermute | solution.py:390
  9.5 9.4 %collective-permute-start.3 = (bf16[80,768]{1,0:T(8,128)(2,1)S(1)}, bf16[80,768]{1,0:T(8,128)(2,1)S(1)}, u32[]{:S(2)}, u32[]{:S(2)}) collective-permute-start(bf16[80,768]{1,0:T(8,128)(2,1)S(1)} %get-tuple-element.42), channel_id=1, source_target_pairs={{0,6},{1,7},{2,4},{3,5},{4,2},{5,3},{6,0},{7,1},{8,14},{9,15},{10,... | collective-permute-start | bytes 368648 | tf_op jit(solution)/shard_map/ppermute | solution.py:390
  19.0 6.3 %collective-permute-start.4 = (bf16[160,768]{1,0:T(8,128)(2,1)S(1)}, bf16[160,768]{1,0:T(8,128)(2,1)S(1)}, u32[]{:S(2)}, u32[]{:S(2)}) collective-permute-start(bf16[160,768]{1,0:T(8,128)(2,1)S(1)} %get-tuple-element.44), channel_id=1, source_target_pairs={{0,1},{1,0},{2,3},{3,2},{4,5},{5,4},{6,7},{7,6},{8,9},{9,8},{10,11... | collective-permute-start | bytes 737288 | tf_op jit(solution)/shard_map/ppermute | solution.py:390
  19.5 11.8 %collective-permute-start.6 = (bf16[80,768]{1,0:T(8,128)(2,1)S(1)}, bf16[80,768]{1,0:T(8,128)(2,1)S(1)}, u32[]{:S(2)}, u32[]{:S(2)}) collective-permute-start(bf16[80,768]{1,0:T(8,128)(2,1)S(1)} %get-tuple-element.46), channel_id=1, source_target_pairs={{0,2},{1,3},{2,0},{3,1},{4,6},{5,7},{6,4},{7,5},{8,10},{9,11},{10,... | collective-permute-start | bytes 368648 | tf_op jit(solution)/shard_map/ppermute | solution.py:390
  21.4 10.6 %collective-permute-start.7 = (bf16[80,768]{1,0:T(8,128)(2,1)S(1)}, bf16[80,768]{1,0:T(8,128)(2,1)S(1)}, u32[]{:S(2)}, u32[]{:S(2)}) collective-permute-start(bf16[80,768]{1,0:T(8,128)(2,1)S(1)} %get-tuple-element.47), channel_id=1, source_target_pairs={{0,4},{1,5},{2,6},{3,7},{4,0},{5,1},{6,2},{7,3},{8,12},{9,13},{10,... | collective-permute-start | bytes 368648 | tf_op jit(solution)/shard_map/ppermute | solution.py:390
  22.6 9.4 %collective-permute-start.8 = (bf16[80,768]{1,0:T(8,128)(2,1)S(1)}, bf16[80,768]{1,0:T(8,128)(2,1)S(1)}, u32[]{:S(2)}, u32[]{:S(2)}) collective-permute-start(bf16[80,768]{1,0:T(8,128)(2,1)S(1)} %get-tuple-element.48), channel_id=1, source_target_pairs={{0,6},{1,7},{2,4},{3,5},{4,2},{5,3},{6,0},{7,1},{8,14},{9,15},{10,... | collective-permute-start | bytes 368648 | tf_op jit(solution)/shard_map/ppermute | solution.py:390
  25.2 16.4 %collective-permute-start.5 = (bf16[320,768]{1,0:T(8,128)(2,1)S(1)}, bf16[320,768]{1,0:T(8,128)(2,1)S(1)}, u32[]{:S(2)}, u32[]{:S(2)}) collective-permute-start(bf16[320,768]{1,0:T(8,128)(2,1)S(1)} %constant_dynamic-update-slice_fusion.rows_ref.x_ref), channel_id=1, source_target_pairs={{0,16},{8,24},{16,0},{24,8},{1,17},{9,25},{17,1},{25,9},{2,18},{10... | collective-permute-start | bytes 1474568 | tf_op jit(solution)/shard_map/ppermute | solution.py:393
  32.9 8.7 %collective-permute-start.9 = (bf16[640,768]{1,0:T(8,128)(2,1)S(1)}, bf16[640,768]{1,0:T(8,128)(2,1)S(1)}, u32[]{:S(2)}, u32[]{:S(2)}) collective-permute-start(bf16[640,768]{1,0:T(8,128)(2,1)S(1)} %get-tuple-element.49.a_ref), channel_id=1, source_target_pairs={{0,8},{8,0},{16,24},{24,16},{1,9},{9,1},{17,25},{25,17},{2,10},{10... | collective-permute-start | bytes 2949128 | tf_op jit(solution)/shard_map/ppermute | solution.py:393
  32.9 17.8 %collective-permute-start.10 = (bf16[320,768]{1,0:T(8,128)(2,1)}, bf16[320,768]{1,0:T(8,128)(2,1)S(1)}, u32[]{:S(2)}, u32[]{:S(2)}) collective-permute-start(bf16[320,768]{1,0:T(8,128)(2,1)} %get-tuple-element.50.rows_ref), channel_id=1, source_target_pairs={{0,16},{8,24},{16,0},{24,8},{1,17},{9,25},{17,1},{25,9},{2,18},{10... | collective-permute-start | bytes 1474568 | tf_op jit(solution)/shard_map/ppermute | solution.py:393
  42.6 19.7 %all-to-all-start = ((bf16[8,248,128]{2,1,0:T(8,128)(2,1)}), bf16[8,248,128]{2,1,0:T(8,128)(2,1)S(1)}, u32[]{:S(2)}, u32[]{:S(2)}) async-start(bf16[8,248,128]{2,1,0:T(8,128)(2,1)} %chunks.1.after_ref), calls=%async_computation | async-start | bytes 1015808 | tf_op jit(solution)/shard_map/all_to_all | solution.py:469
  50.8 3.3 %collective-permute-start.11 = (bf16[640,768]{1,0:T(8,128)(2,1)S(1)}, bf16[640,768]{1,0:T(8,128)(2,1)S(1)}, u32[]{:S(2)}, u32[]{:S(2)}) collective-permute-start(bf16[640,768]{1,0:T(8,128)(2,1)S(1)} %forward.1), channel_id=1, source_target_pairs={{0,8},{8,0},{16,24},{24,16},{1,9},{9,1},{17,25},{25,17},{2,10},{10... | collective-permute-start | bytes 2949128 | tf_op jit(solution)/shard_map/ppermute | solution.py:393
  55.8 6.5 %copy-start = (f32[256]{0:T(256)S(1)}, f32[256]{0:T(256)}, u32[]{:S(2)}) copy-start(f32[256]{0:T(256)} %param.10) | copy-start | bytes 3076
  55.8 6.4 %copy-start.1 = (s32[256]{0:T(256)S(1)}, s32[256]{0:T(256)}, u32[]{:S(2)}) copy-start(s32[256]{0:T(256)} %param.11) | copy-start | bytes 3076
  55.8 6.4 %copy-start.2 = (s32[256]{0:T(256)S(1)}, s32[256]{0:T(256)}, u32[]{:S(2)}) copy-start(s32[256]{0:T(256)} %param.12) | copy-start | bytes 3076

commit v2 on v1

--- a/solution.py
+++ b/solution.py
@@ -99,12 +99,10 @@
 
 
 def join_kernel(after_ref, x_ref, *refs):
-    refs, (d_ref, own_ref) = refs[:-2], refs[-2:]
+    refs, own_ref = refs[:-1], refs[-1]
     rows = x_ref.shape[0]
-    value = jnp.concatenate(halves(refs), axis=0).astype(d_ref.dtype)
-    d_ref[...] = value
     own_ref[:rows, :] = x_ref[...]
-    own_ref[rows:, :] = value
+    own_ref[rows:, :] = jnp.concatenate(halves(refs), axis=0).astype(own_ref.dtype)
 
 
 def copy_share(which_ref, source, target, sem):
@@ -126,21 +124,16 @@
 
 
 def over_tiles(pairs, sems, steps, tile, work):
-    def start(i):
+    for i in range(steps):
         for copy in tile_copies(pairs, sems, i, tile):
             copy.start()
 
-    start(0)
-    start(1)
-
     def step(i, carry):
-        @pl.when(i + 2 < steps)
-        def _():
-            start(i + 2)
-
-        for copy in tile_copies(pairs, sems, i, tile):
-            copy.wait()
-        work(i)
+        def arrived():
+            for copy in tile_copies(pairs, sems, i, tile):
+                copy.wait()
+
+        work(i, arrived)
         return carry
 
     lax.fori_loop(0, steps, step, 0)
@@ -149,7 +142,8 @@
 def own_first_kernel(rows_ref, first_src, hidden_ref, slope_ref, first_ref, sems):
     steps, tile = hidden_ref.shape[0], hidden_ref.shape[2]
 
-    def work(i):
+    def work(i, arrived):
+        arrived()
         hidden, slope = gelu_and_slope(dot_nt(rows_ref[...], first_ref[block(i, tile), :]))
         hidden_ref[i] = hidden
         slope_ref[i] = slope.astype(slope_ref.dtype)
@@ -158,38 +152,41 @@
 
 
 def own_second_kernel(
-    rows_ref,
+    cap_rows,
+    me_ref,
+    own_ref,
     hidden_ref,
     slope_ref,
+    second_ref,
     first_src,
-    second_src,
+    out_ref,
     total_ref,
     gate_ref,
+    held_ref,
     first_ref,
-    second_ref,
     sems,
+    out_sems,
 ):
     steps, tile = hidden_ref.shape[0], hidden_ref.shape[2]
-    total_ref[...] = jnp.zeros_like(total_ref)
-    gate_ref[...] = jnp.zeros_like(gate_ref)
-
-    def work(j):
+    rows = total_ref.shape[0]
+
+    def work(j, arrived):
         here = block(j, tile)
-        back = dot_nt(rows_ref[...], second_ref[here, :])
+        back = dot_nt(own_ref[rows:, :], second_ref[here, :])
         terms = hidden_ref[j].astype(jnp.float32) * back
         gate = gate_ref[...]
         for i in range(tile // LANES):
             gate = gate + terms[:, i * LANES : (i + 1) * LANES]
         gate_ref[...] = gate
         d_pre = (back * slope_ref[j].astype(jnp.float32)).astype(jnp.bfloat16)
+        arrived()
         total_ref[...] += dot_nn(d_pre, first_ref[here, :])
 
-    over_tiles([(second_src, second_ref), (first_src, first_ref)], sems, steps, tile, work)
-
-
-def chunks_kernel(cap_rows, me_ref, x_over, core, total_ref, gate_ref, out_ref):
-    experts = out_ref.shape[0]
-    total = total_ref[...]
+    total_ref[...] = jnp.zeros_like(total_ref)
+    gate_ref[...] = jnp.zeros_like(gate_ref)
+    over_tiles([(first_src, first_ref)], sems, steps, tile, work)
+
+    experts, copies = out_ref.shape[0], []
     gates = jnp.sum(gate_ref[...], axis=1, keepdims=True)
     lane = lax.broadcasted_iota(jnp.int32, (SUBLANES, LANES), 1)
     for k in range(experts):
@@ -199,11 +196,15 @@
             here = start + i * SUBLANES
             tail = jnp.where(lane == i, gates[here : here + SUBLANES], tail)
         parts = [
-            total[start : start + cap_rows, i * LANES : (i + 1) * LANES]
-            for i in range(total.shape[1] // LANES)
+            total_ref[start : start + cap_rows, i * LANES : (i + 1) * LANES]
+            for i in range(total_ref.shape[1] // LANES)
         ]
+        held_ref[k] = jnp.concatenate(parts + [tail], axis=0).astype(held_ref.dtype)
         source = me_ref[0] ^ (2 * (k % (experts // 2)) + k // (experts // 2))
-        out_ref[source] = jnp.concatenate(parts + [tail], axis=0).astype(out_ref.dtype)
+        copies.append(pltpu.make_async_copy(held_ref.at[k], out_ref.at[source], out_sems.at[k]))
+        copies[-1].start()
+    for copy in copies:
+        copy.wait()
 
 
 def gather_rows(refs, all_ref):
@@ -430,42 +431,45 @@
     d_far = [d_parts[0]] + [d_far[s] for s in range(1, pairs)]
     x_own = jnp.concatenate([x_keep, across(x_cross, 1)], axis=0)
 
-    wide = ((groups, slots, share), bf16)
+    steps = groups
+    wide = ((steps, slots, share), bf16)
     weights = pltpu.VMEM((hidden_units, width), bf16)
     hidden, slope = call(
         own_first_kernel,
         "own_first",
         [vmem, anywhere],
         [wide] * 2,
-        [weights, pltpu.SemaphoreType.DMA((groups, 1))],
-        limit=20,
+        [weights, pltpu.SemaphoreType.DMA((steps, 1))],
+        limit=14,
         work=1,
     )(x_own, *in_hbm(weight_in[0]))
     pair_rows = ((2 * slots, width), bf16)
-    d_own, own = call(
+    (own,) = call(
         join_kernel,
         "join",
         [anywhere] + [vmem] * (pairs + 1),
-        [((slots, width), bf16), pair_rows],
+        [pair_rows],
     )(hidden, x_own, *d_far)
-    x_over, d_over, core = over(x_own, 2), over(d_own, 2), over(own, 1)
+    x_over, d_over, core = over(x_own, 2), over(own[slots:], 2), over(own, 1)
 
     stride = cap_rows * width // LANES + SUBLANES
-    total, gates = call(
-        own_second_kernel,
+    (back,) = call(
+        partial(own_second_kernel, cap_rows),
         "own_second",
-        [vmem] * 3 + [anywhere] * 2,
-        [((slots, width), jnp.float32), ((slots, LANES), jnp.float32)],
-        [weights, weights, pltpu.SemaphoreType.DMA((groups, 2))],
-        limit=24,
+        [smem] + [vmem] * 4 + [anywhere],
+        [((experts, stride, LANES), bf16)],
+        [
+            pltpu.VMEM((slots, width), jnp.float32),
+            pltpu.VMEM((slots, LANES), jnp.float32),
+            pltpu.VMEM((experts, stride, LANES), bf16),
+            weights,
+            pltpu.SemaphoreType.DMA((steps, 1)),
+            pltpu.SemaphoreType.DMA((experts,)),
+        ],
+        out_spec=anywhere,
+        limit=14,
         work=20,
-    )(d_own, hidden, slope, *in_hbm(weight_in[0], weight_out[0]))
-    (back,) = call(
-        partial(chunks_kernel, cap_rows),
-        "chunks",
-        [smem] + [anywhere] * 2 + [vmem] * 2,
-        [((experts, stride, LANES), bf16)],
-    )(me, x_over, core, total, gates)
+    )(me, own, hidden, slope, weight_out[0], *in_hbm(weight_in[0]))
     returned = lax.all_to_all(back, "expert", split_axis=0, concat_axis=0, tiled=True)
 
     wide = ((share, 2 * slots), bf16)

time: 63.8 us -> 62.3 us (0.976)
  waiting for transfers between devices: 13.5 us -> 11.1 us
  Pallas kernels: 28.4 us -> 29.1 us
    all_to_all x1, waiting for transfers between devices: 2.34 us -> 0.01 us  [body(): lax.all_to_all(back, 'expert', split_axis=0, concat_axis=0, tiled=True)]
    pallas_call x3 -> x2, Pallas kernels: 9.04 us -> 7.22 us  [the longest x1 7.16 us: body(): call(partial(own_second_kernel, cap_rows), 'own_second', [smem] + [vmem]...]
    pallas_call x1, Pallas kernels: 2.95 us -> 4.16 us  [body(): call(near_first_kernel, 'near_first', [smem] + [anywhere] + [vmem] * 2 +...]
    pallas_call x1, Pallas kernels: 3.2 us -> 4.4 us  [body(): call(near_second_kernel, 'near_second', [anywhere] + [vmem] * 6, [term, t...]
  transfers between devices with their start and end apart: 13 -> 13, of which waited for: 6 -> 5; matrix products, arithmetic and copies ran while one was open for 0% -> 0% of each run, Pallas kernels for 40% -> 42%
where the time goes in v2:
time: 62.3 us; the launch traced here: 62 us
  Pallas kernels  29.1 us (47%)
  starting transfers between devices  20.8 us (33%)
  waiting for transfers between devices  11.1 us (18%)
  between operations  0.84 us (1%)
    ppermute x8, starting transfers between devices, across(): lax.ppermute(chunk, 'expert', [(i, i ^ mask) for i in range(experts)])  12.4 us
    ppermute x8, waiting for transfers between devices, across(): lax.ppermute(chunk, 'expert', [(i, i ^ mask) for i in range(experts)])  11.1 us
    pallas_call x1, Pallas kernels, body(): call(partial(own_second_kernel, cap_rows), 'own_second', [smem] + [vmem]...  7.16 us
    all_to_all x1, starting transfers between devices, body(): lax.all_to_all(back, 'expert', split_axis=0, concat_axis=0, tiled=True)  5.19 us
    pallas_call x1, Pallas kernels, body(): call(own_first_kernel, 'own_first', [vmem, anywhere], [wide] * 2, [weight...  4.56 us
    pallas_call x1, Pallas kernels, body(): call(near_second_kernel, 'near_second', [anywhere] + [vmem] * 6, [term, t...  4.4 us
    pallas_call x1, Pallas kernels, body(): call(near_first_kernel, 'near_first', [smem] + [anywhere] + [vmem] * 2 +...  4.16 us
    pallas_call x1, Pallas kernels, body(): call(far_second_kernel, 'far_second', [anywhere] + [vmem] * 8, [share_row...  4.06 us
  transfers between devices with their start and end apart: 13, of which 5 were waited for; matrix products, arithmetic and copies ran while one was open for 0% of the time, Pallas kernels for 42%

profile of v2, /device:TPU:0, one launch (start us, length us, event | category | flops | bytes accessed | tf_op | source)
XLA Modules:
  0.0 62.0 jit_solution(3909892229841840847)
XLA Ops:
  0.6 1.6 %pack.1 = (bf16[80,768]{1,0:T(8,128)(2,1)S(1)}, bf16[80,768]{1,0:T(8,128)(2,1)S(1)}, bf16[80,768]{1,0:T(8,128)(2,1)S(1)}, bf16[80,768]{1,0:T(8,128)(2,1)S(1)}, b...) custom-call(s32[1]{0:T(128)} %bitcast.me_ref, bf16[256,768]{1,0:T(8,128)(2,1)} %refs_0_.1, ...), custom_call_target="tpu_custom_call" | custom-call | tf_op jit(solution)/shard_map/pack/pallas_call | solution.py:399
  2.3 3.0 %collective-permute-start = (bf16[160,768]{1,0:T(8,128)(2,1)S(1)}, bf16[160,768]{1,0:T(8,128)(2,1)S(1)}, u32[]{:S(2)}, u32[]{:S(2)}) collective-permute-start(bf16[160,768]{1,0:T(8,128)(2,1)S(1)} %get-tuple-element.33), channel_id=1, source_target_pairs={{0,1},{1,0},{2,3},{3,2},{4,5},{5,4},{6,7},{7,6},{8,9},{9,8},{10,11... | collective-permute-start | bytes 737288 | tf_op jit(solution)/shard_map/ppermute | solution.py:391
  5.3 1.6 %collective-permute-start.1 = (bf16[80,768]{1,0:T(8,128)(2,1)S(1)}, bf16[80,768]{1,0:T(8,128)(2,1)S(1)}, u32[]{:S(2)}, u32[]{:S(2)}) collective-permute-start(bf16[80,768]{1,0:T(8,128)(2,1)S(1)} %get-tuple-element.36), channel_id=1, source_target_pairs={{0,2},{1,3},{2,0},{3,1},{4,6},{5,7},{6,4},{7,5},{8,10},{9,11},{10,... | collective-permute-start | bytes 368648 | tf_op jit(solution)/shard_map/ppermute | solution.py:391
  6.9 2.6 %collective-permute-start.2 = (bf16[80,768]{1,0:T(8,128)(2,1)S(1)}, bf16[80,768]{1,0:T(8,128)(2,1)S(1)}, u32[]{:S(2)}, u32[]{:S(2)}) collective-permute-start(bf16[80,768]{1,0:T(8,128)(2,1)S(1)} %get-tuple-element.37), channel_id=1, source_target_pairs={{0,4},{1,5},{2,6},{3,7},{4,0},{5,1},{6,2},{7,3},{8,12},{9,13},{10,... | collective-permute-start | bytes 368648 | tf_op jit(solution)/shard_map/ppermute | solution.py:391
  9.5 0.2 collective-permute-start.3
  9.7 1.6 %collective-permute-done.near_ref = bf16[160,768]{1,0:T(8,128)(2,1)S(1)} collective-permute-done((bf16[160,768]{1,0:T(8,128)(2,1)S(1)}, bf16[160,768]{1,0:T(8,128)(2,1)S(1)}, u32[]{:S(2)}, u32[]{:S(2)}) %collective-permute-start) | collective-permute-done | bytes 245792 | tf_op jit(solution)/shard_map/ppermute | solution.py:391
  11.3 0.2 collective-permute-done.1.refs_1_
  11.5 7.4 %collective-permute-done.2.refs_2_ = bf16[80,768]{1,0:T(8,128)(2,1)S(1)} collective-permute-done((bf16[80,768]{1,0:T(8,128)(2,1)S(1)}, bf16[80,768]{1,0:T(8,128)(2,1)S(1)}, u32[]{:S(2)}, u32[]{:S(2)}) %collective-permute-start.2) | collective-permute-done | bytes 122912 | tf_op jit(solution)/shard_map/ppermute | solution.py:391
  18.9 0.0 collective-permute-done.3.refs_3_
  19.0 0.6 collective-permute-start.4
  19.5 1.9 %collective-permute-start.5 = (bf16[80,768]{1,0:T(8,128)(2,1)S(1)}, bf16[80,768]{1,0:T(8,128)(2,1)S(1)}, u32[]{:S(2)}, u32[]{:S(2)}) collective-permute-start(bf16[80,768]{1,0:T(8,128)(2,1)S(1)} %get-tuple-element.42), channel_id=1, source_target_pairs={{0,2},{1,3},{2,0},{3,1},{4,6},{5,7},{6,4},{7,5},{8,10},{9,11},{10,... | collective-permute-start | bytes 368648 | tf_op jit(solution)/shard_map/ppermute | solution.py:391
  21.4 1.2 %collective-permute-start.6 = (bf16[80,768]{1,0:T(8,128)(2,1)S(1)}, bf16[80,768]{1,0:T(8,128)(2,1)S(1)}, u32[]{:S(2)}, u32[]{:S(2)}) collective-permute-start(bf16[80,768]{1,0:T(8,128)(2,1)S(1)} %get-tuple-element.43), channel_id=1, source_target_pairs={{0,4},{1,5},{2,6},{3,7},{4,0},{5,1},{6,2},{7,3},{8,12},{9,13},{10,... | collective-permute-start | bytes 368648 | tf_op jit(solution)/shard_map/ppermute | solution.py:391
  22.6 1.4 %collective-permute-start.7 = (bf16[80,768]{1,0:T(8,128)(2,1)S(1)}, bf16[80,768]{1,0:T(8,128)(2,1)S(1)}, u32[]{:S(2)}, u32[]{:S(2)}) collective-permute-start(bf16[80,768]{1,0:T(8,128)(2,1)S(1)} %get-tuple-element.44), channel_id=1, source_target_pairs={{0,6},{1,7},{2,4},{3,5},{4,2},{5,3},{6,0},{7,1},{8,14},{9,15},{10,... | collective-permute-start | bytes 368648 | tf_op jit(solution)/shard_map/ppermute | solution.py:391
  23.9 1.3 %collective-permute-done.4 = bf16[160,768]{1,0:T(8,128)(2,1)S(1)} collective-permute-done((bf16[160,768]{1,0:T(8,128)(2,1)S(1)}, bf16[160,768]{1,0:T(8,128)(2,1)S(1)}, u32[]{:S(2)}, u32[]{:S(2)}) %collective-permute-start.4) | collective-permute-done | bytes 245792 | tf_op jit(solution)/shard_map/ppermute | solution.py:391
  25.2 0.0 slice-start
  25.2 1.6 %collective-permute-start.9 = (bf16[320,768]{1,0:T(8,128)(2,1)S(1)}, bf16[320,768]{1,0:T(8,128)(2,1)S(1)}, u32[]{:S(2)}, u32[]{:S(2)}) collective-permute-start(bf16[320,768]{1,0:T(8,128)(2,1)S(1)} %constant_dynamic-update-slice_fusion.rows_ref.x_ref), channel_id=1, source_target_pairs={{0,16},{8,24},{16,0},{24,8},{1,17},{9,25},{17,1},{25,9},{2,18},{10... | collective-permute-start | bytes 1474568 | tf_op jit(solution)/shard_map/ppermute | solution.py:394
  26.8 0.0 slice-start.1
  26.8 4.6 %own_first.1 = (bf16[4,320,768]{2,1,0:T(8,128)(2,1)S(1)}, bf16[4,320,768]{2,1,0:T(8,128)(2,1)S(1)}) custom-call(bf16[320,768]{1,0:T(8,128)(2,1)S(1)} %constant_dynamic-update-slice_fusion.rows_ref.x_ref, bf16[3072,768]{1,0:T(8,128)(2,1)} %bitcast.20), custom_call_target="tpu_custom_call" | custom-call | flops 1509949440 | bytes 2949120 | tf_op jit(solution)/shard_map/own_first/pallas_call | solution.py:437
  31.4 0.0 collective-permute-done.5.refs_1_
  31.4 0.6 %collective-permute-done.6.refs_2_ = bf16[80,768]{1,0:T(8,128)(2,1)S(1)} collective-permute-done((bf16[80,768]{1,0:T(8,128)(2,1)S(1)}, bf16[80,768]{1,0:T(8,128)(2,1)S(1)}, u32[]{:S(2)}, u32[]{:S(2)}) %collective-permute-start.6) | collective-permute-done | bytes 122912 | tf_op jit(solution)/shard_map/ppermute | solution.py:391
  32.0 0.0 collective-permute-done.7.refs_3_
  32.0 0.1 join.1.own_ref.a_ref
  32.1 0.1 collective-permute-start.8
  32.2 1.5 %collective-permute-start.10 = (bf16[320,768]{1,0:T(8,128)(2,1)S(1)}, bf16[320,768]{1,0:T(8,128)(2,1)S(1)}, u32[]{:S(2)}, u32[]{:S(2)}) collective-permute-start(bf16[320,768]{1,0:T(8,128)(2,1)S(1)} %slice.4), channel_id=1, source_target_pairs={{0,16},{8,24},{16,0},{24,8},{1,17},{9,25},{17,1},{25,9},{2,18},{10... | collective-permute-start | bytes 1474568 | tf_op jit(solution)/shard_map/ppermute | solution.py:394
  33.7 0.0 slice-done
  33.8 0.0 slice-done.1
  33.8 7.2 %own_second.1.after_ref = bf16[8,248,128]{2,1,0:T(8,128)(2,1)} custom-call(s32[1]{0:T(128)} %bitcast.me_ref, bf16[640,768]{1,0:T(8,128)(2,1)S(1)} %join.1.own_ref.a_ref, bf16[4,320,768]{2,1,0:T(8,128)(2,1)S(1)} %get-tuple-element.41.after_ref.hidden_ref, bf16[4,320,768]{2,1,0:T(8,128)(2,1)S(1)} %get-tuple-element.45.slope_ref, ...), custom_call_target="tpu_custom_call" | custom-call | flops 30198988800 | bytes 58982400 | tf_op jit(solution)/shard_map/own_second/pallas_call | solution.py:456
  40.9 5.2 %all-to-all-start = ((bf16[8,248,128]{2,1,0:T(8,128)(2,1)}), bf16[8,248,128]{2,1,0:T(8,128)(2,1)S(1)}, u32[]{:S(2)}, u32[]{:S(2)}) async-start(bf16[8,248,128]{2,1,0:T(8,128)(2,1)} %own_second.1.after_ref), calls=%async_computation | async-start | bytes 1015808 | tf_op jit(solution)/shard_map/all_to_all | solution.py:473
  46.1 0.0 collective-permute-done.8.b_ref
  46.1 4.2 %near_first.1 = (bf16[768,640]{1,0:T(8,128)(2,1)S(1)}, bf16[768,640]{1,0:T(8,128)(2,1)S(1)}, bf16[640,768]{1,0:T(8,128)(2,1)S(1)}, bf16[768,768]{1,0:T(8,128)(2,1)S(1)}, bf16[768,768]{1,0:T(8,128)(2,1)S(1)}) custom-call(s32[1]{0:T(128)} %bitcast.6.which_ref, bf16[8,248,128]{2,1,0:T(8,128)(2,1)} %own_second.1.after_ref, ...), custom_call_target="tpu_custom_call" | custom-call | flops 754974720 | bytes 1474560 | tf_op jit(solution)/shard_map/near_first/pallas_call | solution.py:478
  50.3 0.0 collective-permute-done.9.x_ref.x_over
  50.3 0.0 collective-permute-done.10.d_ref.d_over
  50.3 0.1 forward.1
  50.4 0.1 collective-permute-start.11
  50.5 4.4 %near_second.1 = (f32[768,768]{1,0:T(8,128)S(1)}, f32[768,768]{1,0:T(8,128)S(1)}) custom-call(bf16[8,248,128]{2,1,0:T(8,128)(2,1)} %own_second.1.after_ref, bf16[640,768]{1,0:T(8,128)(2,1)S(1)} %join.1.own_ref.a_ref, bf16[640,768]{1,0:T(8,128)(2,1)} %collective-permute-done.8.b_ref, bf16[640,768]{1,0:T(8,128)(2,1)S(1)} %get-tuple-element.46.x_ref, ...), custom_call_target="tpu_custom_call" | custom-call | flops 22649241600 | bytes 44236800 | tf_op jit(solution)/shard_map/near_second/pallas_call | solution.py:486
  54.9 0.0 collective-permute-done.11.diagonal_ref
  54.9 1.7 %far_first.1 = (bf16[768,640]{1,0:T(8,128)(2,1)S(1)}, bf16[768,640]{1,0:T(8,128)(2,1)S(1)}, bf16[640,768]{1,0:T(8,128)(2,1)S(1)}) custom-call(f32[768,768]{1,0:T(8,128)S(1)} %get-tuple-element.50.after_ref.gin_near, bf16[320,768]{1,0:T(8,128)(2,1)S(1)} %collective-permute-done.9.x_ref.x_over, bf16[640,768]{1,0:T(8,128)(2,1)S(1)} %collective-permute-done.11.diagonal_ref, ...), custom_call_target="tpu_custom_call" | custom-call | tf_op jit(solution)/shard_map/far_first/pallas_call | solution.py:501
  56.6 0.0 copy-start
  56.6 0.0 copy-start.1
  56.6 0.0 copy-start.2
  56.6 4.1 %far_second.1 = (bf16[768,768]{1,0:T(8,128)(2,1)}, bf16[768,768]{1,0:T(8,128)(2,1)}) custom-call(bf16[768,640]{1,0:T(8,128)(2,1)S(1)} %get-tuple-element.52.after_ref.hidden_ref, bf16[320,768]{1,0:T(8,128)(2,1)S(1)} %collective-permute-done.10.d_ref.d_over, bf16[640,768]{1,0:T(8,128)(2,1)S(1)} %collective-permute-done.11.diagonal_ref, ...), custom_call_target="tpu_custom_call" | custom-call | tf_op jit(solution)/shard_map/far_second/pallas_call | solution.py:508
  60.7 0.0 all-to-all-done.back_ref
  60.7 0.0 copy-done
  60.7 0.0 copy-done.1
  60.7 0.0 copy-done.2
  60.8 1.2 %unpack.1 = (bf16[256,768]{1,0:T(8,128)(2,1)}, f32[1,256]{1,0:T(1,128)}) custom-call(bf16[768,768]{1,0:T(8,128)(2,1)} %get-tuple-element.56.after_ref, bf16[8,248,128]{2,1,0:T(8,128)(2,1)S(1)} %all-to-all-done.back_ref, f32[1,256]{1,0:T(1,128)S(1)} %bitcast.15, s32[1,256]{1,0:T(1,128)S(1)} %bitcast.17, s32[1,256]{1,0:T(1,128)S(1)} %bitcast.19), custom_call_target="tpu_custom_call" | custom-call | tf_op jit(solution)/shard_map/unpack/pallas_call | solution.py:518
  (6 shorter events, 0.1 us)
Async XLA Ops:
  2.3 9.0 %collective-permute-start = (bf16[160,768]{1,0:T(8,128)(2,1)S(1)}, bf16[160,768]{1,0:T(8,128)(2,1)S(1)}, u32[]{:S(2)}, u32[]{:S(2)}) collective-permute-start(bf16[160,768]{1,0:T(8,128)(2,1)S(1)} %get-tuple-element.33), channel_id=1, source_target_pairs={{0,1},{1,0},{2,3},{3,2},{4,5},{5,4},{6,7},{7,6},{8,9},{9,8},{10,11... | collective-permute-start | bytes 737288 | tf_op jit(solution)/shard_map/ppermute | solution.py:391
  5.3 6.2 %collective-permute-start.1 = (bf16[80,768]{1,0:T(8,128)(2,1)S(1)}, bf16[80,768]{1,0:T(8,128)(2,1)S(1)}, u32[]{:S(2)}, u32[]{:S(2)}) collective-permute-start(bf16[80,768]{1,0:T(8,128)(2,1)S(1)} %get-tuple-element.36), channel_id=1, source_target_pairs={{0,2},{1,3},{2,0},{3,1},{4,6},{5,7},{6,4},{7,5},{8,10},{9,11},{10,... | collective-permute-start | bytes 368648 | tf_op jit(solution)/shard_map/ppermute | solution.py:391
  6.9 12.0 %collective-permute-start.2 = (bf16[80,768]{1,0:T(8,128)(2,1)S(1)}, bf16[80,768]{1,0:T(8,128)(2,1)S(1)}, u32[]{:S(2)}, u32[]{:S(2)}) collective-permute-start(bf16[80,768]{1,0:T(8,128)(2,1)S(1)} %get-tuple-element.37), channel_id=1, source_target_pairs={{0,4},{1,5},{2,6},{3,7},{4,0},{5,1},{6,2},{7,3},{8,12},{9,13},{10,... | collective-permute-start | bytes 368648 | tf_op jit(solution)/shard_map/ppermute | solution.py:391
  9.5 9.4 %collective-permute-start.3 = (bf16[80,768]{1,0:T(8,128)(2,1)S(1)}, bf16[80,768]{1,0:T(8,128)(2,1)S(1)}, u32[]{:S(2)}, u32[]{:S(2)}) collective-permute-start(bf16[80,768]{1,0:T(8,128)(2,1)S(1)} %get-tuple-element.38), channel_id=1, source_target_pairs={{0,6},{1,7},{2,4},{3,5},{4,2},{5,3},{6,0},{7,1},{8,14},{9,15},{10,... | collective-permute-start | bytes 368648 | tf_op jit(solution)/shard_map/ppermute | solution.py:391
  19.0 6.3 %collective-permute-start.4 = (bf16[160,768]{1,0:T(8,128)(2,1)S(1)}, bf16[160,768]{1,0:T(8,128)(2,1)S(1)}, u32[]{:S(2)}, u32[]{:S(2)}) collective-permute-start(bf16[160,768]{1,0:T(8,128)(2,1)S(1)} %get-tuple-element.40), channel_id=1, source_target_pairs={{0,1},{1,0},{2,3},{3,2},{4,5},{5,4},{6,7},{7,6},{8,9},{9,8},{10,11... | collective-permute-start | bytes 737288 | tf_op jit(solution)/shard_map/ppermute | solution.py:391
  19.5 11.8 %collective-permute-start.5 = (bf16[80,768]{1,0:T(8,128)(2,1)S(1)}, bf16[80,768]{1,0:T(8,128)(2,1)S(1)}, u32[]{:S(2)}, u32[]{:S(2)}) collective-permute-start(bf16[80,768]{1,0:T(8,128)(2,1)S(1)} %get-tuple-element.42), channel_id=1, source_target_pairs={{0,2},{1,3},{2,0},{3,1},{4,6},{5,7},{6,4},{7,5},{8,10},{9,11},{10,... | collective-permute-start | bytes 368648 | tf_op jit(solution)/shard_map/ppermute | solution.py:391
  21.4 10.6 %collective-permute-start.6 = (bf16[80,768]{1,0:T(8,128)(2,1)S(1)}, bf16[80,768]{1,0:T(8,128)(2,1)S(1)}, u32[]{:S(2)}, u32[]{:S(2)}) collective-permute-start(bf16[80,768]{1,0:T(8,128)(2,1)S(1)} %get-tuple-element.43), channel_id=1, source_target_pairs={{0,4},{1,5},{2,6},{3,7},{4,0},{5,1},{6,2},{7,3},{8,12},{9,13},{10,... | collective-permute-start | bytes 368648 | tf_op jit(solution)/shard_map/ppermute | solution.py:391
  22.6 9.4 %collective-permute-start.7 = (bf16[80,768]{1,0:T(8,128)(2,1)S(1)}, bf16[80,768]{1,0:T(8,128)(2,1)S(1)}, u32[]{:S(2)}, u32[]{:S(2)}) collective-permute-start(bf16[80,768]{1,0:T(8,128)(2,1)S(1)} %get-tuple-element.44), channel_id=1, source_target_pairs={{0,6},{1,7},{2,4},{3,5},{4,2},{5,3},{6,0},{7,1},{8,14},{9,15},{10,... | collective-permute-start | bytes 368648 | tf_op jit(solution)/shard_map/ppermute | solution.py:391
  25.2 8.5 %slice-start = ((s8[4718592]{0:T(1024)(128)(4,1)}), s8[4194304]{0:T(1024)(128)(4,1)S(1)}, s32[]{:S(2)}) async-start(s8[4718592]{0:T(1024)(128)(4,1)} %bitcast.11), calls=%async_computation.1 | async-start | bytes 8388608
  25.2 25.0 %collective-permute-start.9 = (bf16[320,768]{1,0:T(8,128)(2,1)S(1)}, bf16[320,768]{1,0:T(8,128)(2,1)S(1)}, u32[]{:S(2)}, u32[]{:S(2)}) collective-permute-start(bf16[320,768]{1,0:T(8,128)(2,1)S(1)} %constant_dynamic-update-slice_fusion.rows_ref.x_ref), channel_id=1, source_target_pairs={{0,16},{8,24},{16,0},{24,8},{1,17},{9,25},{17,1},{25,9},{2,18},{10... | collective-permute-start | bytes 1474568 | tf_op jit(solution)/shard_map/ppermute | solution.py:394
  26.8 7.0 %slice-start.1 = ((s8[4718592]{0:T(1024)(128)(4,1)}), s8[524288]{0:T(1024)(128)(4,1)S(1)}, s32[]{:S(2)}) async-start(s8[4718592]{0:T(1024)(128)(4,1)} %bitcast.11), calls=%async_computation.2 | async-start | bytes 1048576
  32.1 14.0 %collective-permute-start.8 = (bf16[640,768]{1,0:T(8,128)(2,1)S(1)}, bf16[640,768]{1,0:T(8,128)(2,1)}, u32[]{:S(2)}, u32[]{:S(2)}) collective-permute-start(bf16[640,768]{1,0:T(8,128)(2,1)S(1)} %join.1.own_ref.a_ref), channel_id=1, source_target_pairs={{0,8},{8,0},{16,24},{24,16},{1,9},{9,1},{17,25},{25,17},{2,10},{10... | collective-permute-start | bytes 2949128 | tf_op jit(solution)/shard_map/ppermute | solution.py:394
  32.2 18.1 %collective-permute-start.10 = (bf16[320,768]{1,0:T(8,128)(2,1)S(1)}, bf16[320,768]{1,0:T(8,128)(2,1)S(1)}, u32[]{:S(2)}, u32[]{:S(2)}) collective-permute-start(bf16[320,768]{1,0:T(8,128)(2,1)S(1)} %slice.4), channel_id=1, source_target_pairs={{0,16},{8,24},{16,0},{24,8},{1,17},{9,25},{17,1},{25,9},{2,18},{10... | collective-permute-start | bytes 1474568 | tf_op jit(solution)/shard_map/ppermute | solution.py:394
  40.9 19.8 %all-to-all-start = ((bf16[8,248,128]{2,1,0:T(8,128)(2,1)}), bf16[8,248,128]{2,1,0:T(8,128)(2,1)S(1)}, u32[]{:S(2)}, u32[]{:S(2)}) async-start(bf16[8,248,128]{2,1,0:T(8,128)(2,1)} %own_second.1.after_ref), calls=%async_computation | async-start | bytes 1015808 | tf_op jit(solution)/shard_map/all_to_all | solution.py:473
  50.4 4.5 %collective-permute-start.11 = (bf16[640,768]{1,0:T(8,128)(2,1)S(1)}, bf16[640,768]{1,0:T(8,128)(2,1)S(1)}, u32[]{:S(2)}, u32[]{:S(2)}) collective-permute-start(bf16[640,768]{1,0:T(8,128)(2,1)S(1)} %forward.1), channel_id=1, source_target_pairs={{0,8},{8,0},{16,24},{24,16},{1,9},{9,1},{17,25},{25,17},{2,10},{10... | collective-permute-start | bytes 2949128 | tf_op jit(solution)/shard_map/ppermute | solution.py:394
  56.6 4.1 %copy-start = (f32[256]{0:T(256)S(1)}, f32[256]{0:T(256)}, u32[]{:S(2)}) copy-start(f32[256]{0:T(256)} %param.10) | copy-start | bytes 3076
  56.6 4.1 %copy-start.1 = (s32[256]{0:T(256)S(1)}, s32[256]{0:T(256)}, u32[]{:S(2)}) copy-start(s32[256]{0:T(256)} %param.11) | copy-start | bytes 3076
  56.6 4.1 %copy-start.2 = (s32[256]{0:T(256)S(1)}, s32[256]{0:T(256)}, u32[]{:S(2)}) copy-start(s32[256]{0:T(256)} %param.12) | copy-start | bytes 3076

commit v3 on v2

--- a/solution.py
+++ b/solution.py
@@ -246,39 +246,45 @@
 def near_first_kernel(
     which_ref,
     after_ref,
-    a_ref,
-    b_ref,
+    own,
+    core,
     first_src,
     second_src,
     hidden_ref,
     slope_ref,
-    all_ref,
+    x_ref,
+    d_ref,
     first_ref,
     second_ref,
     sems,
 ):
-    first_copy = copy_share(which_ref, first_src, first_ref, sems.at[0])
-    second_copy = copy_share(which_ref, second_src, second_ref, sems.at[1])
-    first_copy.start()
-    second_copy.start()
-    rows = a_ref.shape[0] // 2
-    gather_rows((a_ref.at[:rows], b_ref.at[:rows]), all_ref)
-    first_copy.wait()
-    gelu_rows(first_ref, all_ref, hidden_ref, slope_ref)
-    second_copy.wait()
-
-
-def near_second_kernel(
-    after_ref, a_ref, b_ref, x_ref, hidden_ref, slope_ref, second_ref, gin_ref, gout_ref, all_ref
-):
-    rows = a_ref.shape[0] // 2
-    gather_rows((a_ref.at[rows:], b_ref.at[rows:]), all_ref)
-
+    rows = x_ref.shape[0] // 2
+    upper, lower = pl.ds(0, rows), pl.ds(rows, rows)
+    now = [
+        copy_share(which_ref, first_src, first_ref, sems.at[0]),
+        pltpu.make_async_copy(own.at[upper, :], x_ref.at[upper, :], sems.at[1]),
+        pltpu.make_async_copy(core.at[upper, :], x_ref.at[lower, :], sems.at[2]),
+    ]
+    later = [
+        copy_share(which_ref, second_src, second_ref, sems.at[3]),
+        pltpu.make_async_copy(own.at[lower, :], d_ref.at[upper, :], sems.at[4]),
+        pltpu.make_async_copy(core.at[lower, :], d_ref.at[lower, :], sems.at[5]),
+    ]
+    for copy in now + later:
+        copy.start()
+    for copy in now:
+        copy.wait()
+    gelu_rows(first_ref, x_ref, hidden_ref, slope_ref)
+    for copy in later:
+        copy.wait()
+
+
+def near_second_kernel(after_ref, x_ref, d_ref, hidden_ref, slope_ref, second_ref, gin_ref, gout_ref):
     def finish(i, here, gin, gout):
         gin_ref[here, :] = gin
         gout_ref[here, :] = gout
 
-    weight_terms(second_ref, x_ref, all_ref, hidden_ref, slope_ref, finish)
+    weight_terms(second_ref, x_ref, d_ref, hidden_ref, slope_ref, finish)
 
 
 def far_first_kernel(after_ref, x_over, diagonal_ref, first_ref, hidden_ref, slope_ref, x_ref):
@@ -475,22 +481,21 @@
     wide = ((share, 2 * slots), bf16)
     share_rows = ((share, width), bf16)
     term = ((share, width), jnp.float32)
-    hidden_t, slope_t, x_near, first_share, second_share = call(
+    hidden_t, slope_t, x_near, d_near, first_share, second_share = call(
         near_first_kernel,
         "near_first",
-        [smem] + [anywhere] + [vmem] * 2 + [anywhere] * 2,
-        [wide, wide, pair_rows, share_rows, share_rows],
-        [pltpu.SemaphoreType.DMA((2,))],
+        [smem] + [anywhere] * 5,
+        [wide, wide, pair_rows, pair_rows, share_rows, share_rows],
+        [pltpu.SemaphoreType.DMA((6,))],
         work=0.5,
     )(which, back, own, core, *in_hbm(weight_in[0], weight_out[0]))
     gin_near, gout_near = call(
         near_second_kernel,
         "near_second",
-        [anywhere] + [vmem] * 6,
+        [anywhere] + [vmem] * 5,
         [term, term],
-        [pltpu.VMEM(*pair_rows)],
         work=15,
-    )(back, own, core, x_near, hidden_t, slope_t, second_share)
+    )(back, x_near, d_near, hidden_t, slope_t, second_share)
     (moved,) = call(
         forward_kernel,
         "forward",

time: 62.3 us -> 62.1 us (level)
  Pallas kernels: 29.1 us -> 26.9 us
  waiting for transfers between devices: 11.1 us -> 13.2 us
    pallas_call x2, Pallas kernels: 8.56 us -> 6.37 us  [the longest x1 3.2 us: body(): call(near_first_kernel, 'near_first', [smem] + [anywhere] * 5, [wide, wid...]
    all_to_all x1, waiting for transfers between devices: 0.01 us -> 2.07 us  [body(): lax.all_to_all(back, 'expert', split_axis=0, concat_axis=0, tiled=True)]
  transfers between devices with their start and end apart: 13 -> 13, of which waited for: 5 -> 6; matrix products, arithmetic and copies ran while one was open for 0% -> 0% of each run, Pallas kernels for 42% -> 39%
where the time goes in v3:
time: 62.1 us; the launch traced here: 61.8 us
  Pallas kernels  26.9 us (43%)
  starting transfers between devices  20.8 us (33%)
  waiting for transfers between devices  13.2 us (21%)
  between operations  0.82 us (1%)
    ppermute x8, starting transfers between devices, across(): lax.ppermute(chunk, 'expert', [(i, i ^ mask) for i in range(experts)])  12.4 us
    ppermute x8, waiting for transfers between devices, across(): lax.ppermute(chunk, 'expert', [(i, i ^ mask) for i in range(experts)])  11.1 us
    pallas_call x1, Pallas kernels, body(): call(partial(own_second_kernel, cap_rows), 'own_second', [smem] + [vmem]...  7.16 us
    all_to_all x1, starting transfers between devices, body(): lax.all_to_all(back, 'expert', split_axis=0, concat_axis=0, tiled=True)  5.19 us
    pallas_call x1, Pallas kernels, body(): call(own_first_kernel, 'own_first', [vmem, anywhere], [wide] * 2, [weight...  4.56 us
    pallas_call x1, Pallas kernels, body(): call(far_second_kernel, 'far_second', [anywhere] + [vmem] * 8, [share_row...  4.06 us
    ppermute x4, starting transfers between devices, over(): return lax.ppermute(chunk, 'dp', [(i, i ^ mask) for i in range(groups)])  3.25 us
    pallas_call x1, Pallas kernels, body(): call(near_first_kernel, 'near_first', [smem] + [anywhere] * 5, [wide, wid...  3.2 us
  transfers between devices with their start and end apart: 13, of which 6 were waited for; matrix products, arithmetic and copies ran while one was open for 0% of the time, Pallas kernels for 39%

profile of v3, /device:TPU:0, one launch (start us, length us, event | category | flops | bytes accessed | tf_op | source)
XLA Modules:
  0.0 61.8 jit_solution(16498378417867087079)
XLA Ops:
  0.6 1.6 %pack.1 = (bf16[80,768]{1,0:T(8,128)(2,1)S(1)}, bf16[80,768]{1,0:T(8,128)(2,1)S(1)}, bf16[80,768]{1,0:T(8,128)(2,1)S(1)}, bf16[80,768]{1,0:T(8,128)(2,1)S(1)}, b...) custom-call(s32[1]{0:T(128)} %bitcast.me_ref, bf16[256,768]{1,0:T(8,128)(2,1)} %refs_0_.1, ...), custom_call_target="tpu_custom_call" | custom-call | tf_op jit(solution)/shard_map/pack/pallas_call | solution.py:405
  2.3 3.0 %collective-permute-start = (bf16[160,768]{1,0:T(8,128)(2,1)S(1)}, bf16[160,768]{1,0:T(8,128)(2,1)S(1)}, u32[]{:S(2)}, u32[]{:S(2)}) collective-permute-start(bf16[160,768]{1,0:T(8,128)(2,1)S(1)} %get-tuple-element.34), channel_id=1, source_target_pairs={{0,1},{1,0},{2,3},{3,2},{4,5},{5,4},{6,7},{7,6},{8,9},{9,8},{10,11... | collective-permute-start | bytes 737288 | tf_op jit(solution)/shard_map/ppermute | solution.py:397
  5.3 1.6 %collective-permute-start.1 = (bf16[80,768]{1,0:T(8,128)(2,1)S(1)}, bf16[80,768]{1,0:T(8,128)(2,1)S(1)}, u32[]{:S(2)}, u32[]{:S(2)}) collective-permute-start(bf16[80,768]{1,0:T(8,128)(2,1)S(1)} %get-tuple-element.37), channel_id=1, source_target_pairs={{0,2},{1,3},{2,0},{3,1},{4,6},{5,7},{6,4},{7,5},{8,10},{9,11},{10,... | collective-permute-start | bytes 368648 | tf_op jit(solution)/shard_map/ppermute | solution.py:397
  6.9 2.6 %collective-permute-start.2 = (bf16[80,768]{1,0:T(8,128)(2,1)S(1)}, bf16[80,768]{1,0:T(8,128)(2,1)S(1)}, u32[]{:S(2)}, u32[]{:S(2)}) collective-permute-start(bf16[80,768]{1,0:T(8,128)(2,1)S(1)} %get-tuple-element.38), channel_id=1, source_target_pairs={{0,4},{1,5},{2,6},{3,7},{4,0},{5,1},{6,2},{7,3},{8,12},{9,13},{10,... | collective-permute-start | bytes 368648 | tf_op jit(solution)/shard_map/ppermute | solution.py:397
  9.5 0.2 collective-permute-start.3
  9.7 1.6 %collective-permute-done.near_ref = bf16[160,768]{1,0:T(8,128)(2,1)S(1)} collective-permute-done((bf16[160,768]{1,0:T(8,128)(2,1)S(1)}, bf16[160,768]{1,0:T(8,128)(2,1)S(1)}, u32[]{:S(2)}, u32[]{:S(2)}) %collective-permute-start) | collective-permute-done | bytes 245792 | tf_op jit(solution)/shard_map/ppermute | solution.py:397
  11.3 0.2 collective-permute-done.1.refs_1_
  11.5 7.4 %collective-permute-done.2.refs_2_ = bf16[80,768]{1,0:T(8,128)(2,1)S(1)} collective-permute-done((bf16[80,768]{1,0:T(8,128)(2,1)S(1)}, bf16[80,768]{1,0:T(8,128)(2,1)S(1)}, u32[]{:S(2)}, u32[]{:S(2)}) %collective-permute-start.2) | collective-permute-done | bytes 122912 | tf_op jit(solution)/shard_map/ppermute | solution.py:397
  18.9 0.0 collective-permute-done.3.refs_3_
  19.0 0.6 collective-permute-start.4
  19.5 1.9 %collective-permute-start.5 = (bf16[80,768]{1,0:T(8,128)(2,1)S(1)}, bf16[80,768]{1,0:T(8,128)(2,1)S(1)}, u32[]{:S(2)}, u32[]{:S(2)}) collective-permute-start(bf16[80,768]{1,0:T(8,128)(2,1)S(1)} %get-tuple-element.43), channel_id=1, source_target_pairs={{0,2},{1,3},{2,0},{3,1},{4,6},{5,7},{6,4},{7,5},{8,10},{9,11},{10,... | collective-permute-start | bytes 368648 | tf_op jit(solution)/shard_map/ppermute | solution.py:397
  21.4 1.2 %collective-permute-start.6 = (bf16[80,768]{1,0:T(8,128)(2,1)S(1)}, bf16[80,768]{1,0:T(8,128)(2,1)S(1)}, u32[]{:S(2)}, u32[]{:S(2)}) collective-permute-start(bf16[80,768]{1,0:T(8,128)(2,1)S(1)} %get-tuple-element.44), channel_id=1, source_target_pairs={{0,4},{1,5},{2,6},{3,7},{4,0},{5,1},{6,2},{7,3},{8,12},{9,13},{10,... | collective-permute-start | bytes 368648 | tf_op jit(solution)/shard_map/ppermute | solution.py:397
  22.6 1.4 %collective-permute-start.7 = (bf16[80,768]{1,0:T(8,128)(2,1)S(1)}, bf16[80,768]{1,0:T(8,128)(2,1)S(1)}, u32[]{:S(2)}, u32[]{:S(2)}) collective-permute-start(bf16[80,768]{1,0:T(8,128)(2,1)S(1)} %get-tuple-element.45), channel_id=1, source_target_pairs={{0,6},{1,7},{2,4},{3,5},{4,2},{5,3},{6,0},{7,1},{8,14},{9,15},{10,... | collective-permute-start | bytes 368648 | tf_op jit(solution)/shard_map/ppermute | solution.py:397
  23.9 1.3 %collective-permute-done.4 = bf16[160,768]{1,0:T(8,128)(2,1)S(1)} collective-permute-done((bf16[160,768]{1,0:T(8,128)(2,1)S(1)}, bf16[160,768]{1,0:T(8,128)(2,1)S(1)}, u32[]{:S(2)}, u32[]{:S(2)}) %collective-permute-start.4) | collective-permute-done | bytes 245792 | tf_op jit(solution)/shard_map/ppermute | solution.py:397
  25.2 0.0 slice-start
  25.2 1.6 %collective-permute-start.9 = (bf16[320,768]{1,0:T(8,128)(2,1)S(1)}, bf16[320,768]{1,0:T(8,128)(2,1)S(1)}, u32[]{:S(2)}, u32[]{:S(2)}) collective-permute-start(bf16[320,768]{1,0:T(8,128)(2,1)S(1)} %constant_dynamic-update-slice_fusion.rows_ref.x_ref), channel_id=1, source_target_pairs={{0,16},{8,24},{16,0},{24,8},{1,17},{9,25},{17,1},{25,9},{2,18},{10... | collective-permute-start | bytes 1474568 | tf_op jit(solution)/shard_map/ppermute | solution.py:400
  26.8 0.0 slice-start.1
  26.8 4.6 %own_first.1 = (bf16[4,320,768]{2,1,0:T(8,128)(2,1)S(1)}, bf16[4,320,768]{2,1,0:T(8,128)(2,1)S(1)}) custom-call(bf16[320,768]{1,0:T(8,128)(2,1)S(1)} %constant_dynamic-update-slice_fusion.rows_ref.x_ref, bf16[3072,768]{1,0:T(8,128)(2,1)} %bitcast.20), custom_call_target="tpu_custom_call" | custom-call | flops 1509949440 | bytes 2949120 | tf_op jit(solution)/shard_map/own_first/pallas_call | solution.py:443
  31.4 0.0 collective-permute-done.5.refs_1_
  31.4 0.6 %collective-permute-done.6.refs_2_ = bf16[80,768]{1,0:T(8,128)(2,1)S(1)} collective-permute-done((bf16[80,768]{1,0:T(8,128)(2,1)S(1)}, bf16[80,768]{1,0:T(8,128)(2,1)S(1)}, u32[]{:S(2)}, u32[]{:S(2)}) %collective-permute-start.6) | collective-permute-done | bytes 122912 | tf_op jit(solution)/shard_map/ppermute | solution.py:397
  32.0 0.0 collective-permute-done.7.refs_3_
  32.0 0.1 join.1.own_ref.own
  32.1 0.1 collective-permute-start.8
  32.2 1.5 %collective-permute-start.10 = (bf16[320,768]{1,0:T(8,128)(2,1)S(1)}, bf16[320,768]{1,0:T(8,128)(2,1)S(1)}, u32[]{:S(2)}, u32[]{:S(2)}) collective-permute-start(bf16[320,768]{1,0:T(8,128)(2,1)S(1)} %slice.4), channel_id=1, source_target_pairs={{0,16},{8,24},{16,0},{24,8},{1,17},{9,25},{17,1},{25,9},{2,18},{10... | collective-permute-start | bytes 1474568 | tf_op jit(solution)/shard_map/ppermute | solution.py:400
  33.7 0.0 slice-done
  33.8 0.0 slice-done.1
  33.8 7.2 %own_second.1.after_ref = bf16[8,248,128]{2,1,0:T(8,128)(2,1)} custom-call(s32[1]{0:T(128)} %bitcast.me_ref, bf16[640,768]{1,0:T(8,128)(2,1)S(1)} %join.1.own_ref.own, bf16[4,320,768]{2,1,0:T(8,128)(2,1)S(1)} %get-tuple-element.42.after_ref.hidden_ref, bf16[4,320,768]{2,1,0:T(8,128)(2,1)S(1)} %get-tuple-element.46.slope_ref, bf16[3072,768]{1,0:T(8,128)(2,1)S(1)} %bitcast.13, ...), custom_call_target="tpu_custom_call" | custom-call | flops 30198988800 | bytes 58982400 | tf_op jit(solution)/shard_map/own_second/pallas_call | solution.py:462
  40.9 5.2 %all-to-all-start = ((bf16[8,248,128]{2,1,0:T(8,128)(2,1)}), bf16[8,248,128]{2,1,0:T(8,128)(2,1)S(1)}, u32[]{:S(2)}, u32[]{:S(2)}) async-start(bf16[8,248,128]{2,1,0:T(8,128)(2,1)} %own_second.1.after_ref), calls=%async_computation | async-start | bytes 1015808 | tf_op jit(solution)/shard_map/all_to_all | solution.py:479
  46.1 0.0 collective-permute-done.8.core
  46.1 3.2 %near_first.1 = (bf16[768,640]{1,0:T(8,128)(2,1)S(1)}, bf16[768,640]{1,0:T(8,128)(2,1)S(1)}, bf16[640,768]{1,0:T(8,128)(2,1)S(1)}, bf16[640,768]{1,0:T(8,128)(2,...) custom-call(s32[1]{0:T(128)} %bitcast.6.which_ref, bf16[8,248,128]{2,1,0:T(8,128)(2,1)} %own_second.1.after_ref, ...), custom_call_target="tpu_custom_call" | custom-call | flops 754974720 | bytes 1474560 | tf_op jit(solution)/shard_map/near_first/pallas_call | solution.py:484
  49.3 0.0 collective-permute-done.9.x_ref.x_over
  49.3 0.0 collective-permute-done.10.d_ref.d_over
  49.3 0.1 forward.1
  49.4 0.1 collective-permute-start.11
  49.5 3.2 %near_second.1 = (f32[768,768]{1,0:T(8,128)S(1)}, f32[768,768]{1,0:T(8,128)S(1)}) custom-call(bf16[8,248,128]{2,1,0:T(8,128)(2,1)} %own_second.1.after_ref, bf16[640,768]{1,0:T(8,128)(2,1)S(1)} %get-tuple-element.47.x_ref, bf16[640,768]{1,0:T(8,128)(2,1)S(1)} %get-tuple-element.48.d_ref, bf16[768,640]{1,0:T(8,128)(2,1)S(1)} %get-tuple-element.49.hidden_ref.after_ref, ...), custom_call_target="tpu_custom_call" | custom-call | flops 22649241600 | bytes 44236800 | tf_op jit(solution)/shard_map/near_second/pallas_call | solution.py:492
  52.7 0.0 collective-permute-done.11.diagonal_ref
  52.7 1.7 %far_first.1 = (bf16[768,640]{1,0:T(8,128)(2,1)S(1)}, bf16[768,640]{1,0:T(8,128)(2,1)S(1)}, bf16[640,768]{1,0:T(8,128)(2,1)S(1)}) custom-call(f32[768,768]{1,0:T(8,128)S(1)} %get-tuple-element.52.after_ref.gin_near, bf16[320,768]{1,0:T(8,128)(2,1)S(1)} %collective-permute-done.9.x_ref.x_over, bf16[640,768]{1,0:T(8,128)(2,1)S(1)} %collective-permute-done.11.diagonal_ref, ...), custom_call_target="tpu_custom_call" | custom-call | tf_op jit(solution)/shard_map/far_first/pallas_call | solution.py:506
  54.4 0.0 copy-start
  54.5 0.0 copy-start.1
  54.5 0.0 copy-start.2
  54.5 4.1 %far_second.1 = (bf16[768,768]{1,0:T(8,128)(2,1)}, bf16[768,768]{1,0:T(8,128)(2,1)}) custom-call(bf16[768,640]{1,0:T(8,128)(2,1)S(1)} %get-tuple-element.54.after_ref.hidden_ref, bf16[320,768]{1,0:T(8,128)(2,1)S(1)} %collective-permute-done.10.d_ref.d_over, bf16[640,768]{1,0:T(8,128)(2,1)S(1)} %collective-permute-done.11.diagonal_ref, ...), custom_call_target="tpu_custom_call" | custom-call | tf_op jit(solution)/shard_map/far_second/pallas_call | solution.py:513
  58.5 2.1 %all-to-all-done.back_ref = bf16[8,248,128]{2,1,0:T(8,128)(2,1)S(1)} async-done(((bf16[8,248,128]{2,1,0:T(8,128)(2,1)}), bf16[8,248,128]{2,1,0:T(8,128)(2,1)S(1)}, u32[]{:S(2)}, u32[]{:S(2)}) %all-to-all-start) | async-done | bytes 507936 | tf_op jit(solution)/shard_map/all_to_all | solution.py:479
  60.6 0.0 copy-done
  60.6 0.0 copy-done.1
  60.6 0.0 copy-done.2
  60.6 1.2 %unpack.1 = (bf16[256,768]{1,0:T(8,128)(2,1)}, f32[1,256]{1,0:T(1,128)}) custom-call(bf16[768,768]{1,0:T(8,128)(2,1)} %get-tuple-element.58.after_ref, bf16[8,248,128]{2,1,0:T(8,128)(2,1)S(1)} %all-to-all-done.back_ref, f32[1,256]{1,0:T(1,128)S(1)} %bitcast.15, s32[1,256]{1,0:T(1,128)S(1)} %bitcast.17, s32[1,256]{1,0:T(1,128)S(1)} %bitcast.19), custom_call_target="tpu_custom_call" | custom-call | tf_op jit(solution)/shard_map/unpack/pallas_call | solution.py:523
  (6 shorter events, 0.1 us)
Async XLA Ops:
  2.3 9.0 %collective-permute-start = (bf16[160,768]{1,0:T(8,128)(2,1)S(1)}, bf16[160,768]{1,0:T(8,128)(2,1)S(1)}, u32[]{:S(2)}, u32[]{:S(2)}) collective-permute-start(bf16[160,768]{1,0:T(8,128)(2,1)S(1)} %get-tuple-element.34), channel_id=1, source_target_pairs={{0,1},{1,0},{2,3},{3,2},{4,5},{5,4},{6,7},{7,6},{8,9},{9,8},{10,11... | collective-permute-start | bytes 737288 | tf_op jit(solution)/shard_map/ppermute | solution.py:397
  5.3 6.2 %collective-permute-start.1 = (bf16[80,768]{1,0:T(8,128)(2,1)S(1)}, bf16[80,768]{1,0:T(8,128)(2,1)S(1)}, u32[]{:S(2)}, u32[]{:S(2)}) collective-permute-start(bf16[80,768]{1,0:T(8,128)(2,1)S(1)} %get-tuple-element.37), channel_id=1, source_target_pairs={{0,2},{1,3},{2,0},{3,1},{4,6},{5,7},{6,4},{7,5},{8,10},{9,11},{10,... | collective-permute-start | bytes 368648 | tf_op jit(solution)/shard_map/ppermute | solution.py:397
  6.9 12.0 %collective-permute-start.2 = (bf16[80,768]{1,0:T(8,128)(2,1)S(1)}, bf16[80,768]{1,0:T(8,128)(2,1)S(1)}, u32[]{:S(2)}, u32[]{:S(2)}) collective-permute-start(bf16[80,768]{1,0:T(8,128)(2,1)S(1)} %get-tuple-element.38), channel_id=1, source_target_pairs={{0,4},{1,5},{2,6},{3,7},{4,0},{5,1},{6,2},{7,3},{8,12},{9,13},{10,... | collective-permute-start | bytes 368648 | tf_op jit(solution)/shard_map/ppermute | solution.py:397
  9.5 9.4 %collective-permute-start.3 = (bf16[80,768]{1,0:T(8,128)(2,1)S(1)}, bf16[80,768]{1,0:T(8,128)(2,1)S(1)}, u32[]{:S(2)}, u32[]{:S(2)}) collective-permute-start(bf16[80,768]{1,0:T(8,128)(2,1)S(1)} %get-tuple-element.39), channel_id=1, source_target_pairs={{0,6},{1,7},{2,4},{3,5},{4,2},{5,3},{6,0},{7,1},{8,14},{9,15},{10,... | collective-permute-start | bytes 368648 | tf_op jit(solution)/shard_map/ppermute | solution.py:397
  19.0 6.3 %collective-permute-start.4 = (bf16[160,768]{1,0:T(8,128)(2,1)S(1)}, bf16[160,768]{1,0:T(8,128)(2,1)S(1)}, u32[]{:S(2)}, u32[]{:S(2)}) collective-permute-start(bf16[160,768]{1,0:T(8,128)(2,1)S(1)} %get-tuple-element.41), channel_id=1, source_target_pairs={{0,1},{1,0},{2,3},{3,2},{4,5},{5,4},{6,7},{7,6},{8,9},{9,8},{10,11... | collective-permute-start | bytes 737288 | tf_op jit(solution)/shard_map/ppermute | solution.py:397
  19.5 11.8 %collective-permute-start.5 = (bf16[80,768]{1,0:T(8,128)(2,1)S(1)}, bf16[80,768]{1,0:T(8,128)(2,1)S(1)}, u32[]{:S(2)}, u32[]{:S(2)}) collective-permute-start(bf16[80,768]{1,0:T(8,128)(2,1)S(1)} %get-tuple-element.43), channel_id=1, source_target_pairs={{0,2},{1,3},{2,0},{3,1},{4,6},{5,7},{6,4},{7,5},{8,10},{9,11},{10,... | collective-permute-start | bytes 368648 | tf_op jit(solution)/shard_map/ppermute | solution.py:397
  21.4 10.6 %collective-permute-start.6 = (bf16[80,768]{1,0:T(8,128)(2,1)S(1)}, bf16[80,768]{1,0:T(8,128)(2,1)S(1)}, u32[]{:S(2)}, u32[]{:S(2)}) collective-permute-start(bf16[80,768]{1,0:T(8,128)(2,1)S(1)} %get-tuple-element.44), channel_id=1, source_target_pairs={{0,4},{1,5},{2,6},{3,7},{4,0},{5,1},{6,2},{7,3},{8,12},{9,13},{10,... | collective-permute-start | bytes 368648 | tf_op jit(solution)/shard_map/ppermute | solution.py:397
  22.6 9.4 %collective-permute-start.7 = (bf16[80,768]{1,0:T(8,128)(2,1)S(1)}, bf16[80,768]{1,0:T(8,128)(2,1)S(1)}, u32[]{:S(2)}, u32[]{:S(2)}) collective-permute-start(bf16[80,768]{1,0:T(8,128)(2,1)S(1)} %get-tuple-element.45), channel_id=1, source_target_pairs={{0,6},{1,7},{2,4},{3,5},{4,2},{5,3},{6,0},{7,1},{8,14},{9,15},{10,... | collective-permute-start | bytes 368648 | tf_op jit(solution)/shard_map/ppermute | solution.py:397
  25.2 8.5 %slice-start = ((s8[4718592]{0:T(1024)(128)(4,1)}), s8[4194304]{0:T(1024)(128)(4,1)S(1)}, s32[]{:S(2)}) async-start(s8[4718592]{0:T(1024)(128)(4,1)} %bitcast.11), calls=%async_computation.1 | async-start | bytes 8388608
  25.2 24.1 %collective-permute-start.9 = (bf16[320,768]{1,0:T(8,128)(2,1)S(1)}, bf16[320,768]{1,0:T(8,128)(2,1)S(1)}, u32[]{:S(2)}, u32[]{:S(2)}) collective-permute-start(bf16[320,768]{1,0:T(8,128)(2,1)S(1)} %constant_dynamic-update-slice_fusion.rows_ref.x_ref), channel_id=1, source_target_pairs={{0,16},{8,24},{16,0},{24,8},{1,17},{9,25},{17,1},{25,9},{2,18},{10... | collective-permute-start | bytes 1474568 | tf_op jit(solution)/shard_map/ppermute | solution.py:400
  26.8 7.0 %slice-start.1 = ((s8[4718592]{0:T(1024)(128)(4,1)}), s8[524288]{0:T(1024)(128)(4,1)S(1)}, s32[]{:S(2)}) async-start(s8[4718592]{0:T(1024)(128)(4,1)} %bitcast.11), calls=%async_computation.2 | async-start | bytes 1048576
  32.1 14.0 %collective-permute-start.8 = (bf16[640,768]{1,0:T(8,128)(2,1)S(1)}, bf16[640,768]{1,0:T(8,128)(2,1)}, u32[]{:S(2)}, u32[]{:S(2)}) collective-permute-start(bf16[640,768]{1,0:T(8,128)(2,1)S(1)} %join.1.own_ref.own), channel_id=1, source_target_pairs={{0,8},{8,0},{16,24},{24,16},{1,9},{9,1},{17,25},{25,17},{2,10},{10... | collective-permute-start | bytes 2949128 | tf_op jit(solution)/shard_map/ppermute | solution.py:400
  32.2 17.1 %collective-permute-start.10 = (bf16[320,768]{1,0:T(8,128)(2,1)S(1)}, bf16[320,768]{1,0:T(8,128)(2,1)S(1)}, u32[]{:S(2)}, u32[]{:S(2)}) collective-permute-start(bf16[320,768]{1,0:T(8,128)(2,1)S(1)} %slice.4), channel_id=1, source_target_pairs={{0,16},{8,24},{16,0},{24,8},{1,17},{9,25},{17,1},{25,9},{2,18},{10... | collective-permute-start | bytes 1474568 | tf_op jit(solution)/shard_map/ppermute | solution.py:400
  40.9 19.7 %all-to-all-start = ((bf16[8,248,128]{2,1,0:T(8,128)(2,1)}), bf16[8,248,128]{2,1,0:T(8,128)(2,1)S(1)}, u32[]{:S(2)}, u32[]{:S(2)}) async-start(bf16[8,248,128]{2,1,0:T(8,128)(2,1)} %own_second.1.after_ref), calls=%async_computation | async-start | bytes 1015808 | tf_op jit(solution)/shard_map/all_to_all | solution.py:479
  49.4 3.3 %collective-permute-start.11 = (bf16[640,768]{1,0:T(8,128)(2,1)S(1)}, bf16[640,768]{1,0:T(8,128)(2,1)S(1)}, u32[]{:S(2)}, u32[]{:S(2)}) collective-permute-start(bf16[640,768]{1,0:T(8,128)(2,1)S(1)} %forward.1), channel_id=1, source_target_pairs={{0,8},{8,0},{16,24},{24,16},{1,9},{9,1},{17,25},{25,17},{2,10},{10... | collective-permute-start | bytes 2949128 | tf_op jit(solution)/shard_map/ppermute | solution.py:400
  54.4 6.2 %copy-start = (f32[256]{0:T(256)S(1)}, f32[256]{0:T(256)}, u32[]{:S(2)}) copy-start(f32[256]{0:T(256)} %param.10) | copy-start | bytes 3076
  54.5 6.2 %copy-start.1 = (s32[256]{0:T(256)S(1)}, s32[256]{0:T(256)}, u32[]{:S(2)}) copy-start(s32[256]{0:T(256)} %param.11) | copy-start | bytes 3076
  54.5 6.2 %copy-start.2 = (s32[256]{0:T(256)S(1)}, s32[256]{0:T(256)}, u32[]{:S(2)}) copy-start(s32[256]{0:T(256)} %param.12) | copy-start | bytes 3076

commit v4 on v3

--- a/solution.py
+++ b/solution.py
@@ -115,40 +115,16 @@
     gather_rows((x_ref, d_ref), out_ref)
 
 
-def tile_copies(pairs, sems, i, tile):
-    here = block(i, tile)
-    return [
-        pltpu.make_async_copy(source.at[here, :], target.at[here, :], sems.at[i, k])
-        for k, (source, target) in enumerate(pairs)
-    ]
-
-
-def over_tiles(pairs, sems, steps, tile, work):
-    for i in range(steps):
-        for copy in tile_copies(pairs, sems, i, tile):
-            copy.start()
+def own_first_kernel(rows_ref, first_ref, hidden_ref, slope_ref):
+    steps, tile = hidden_ref.shape[0], hidden_ref.shape[2]
 
     def step(i, carry):
-        def arrived():
-            for copy in tile_copies(pairs, sems, i, tile):
-                copy.wait()
-
-        work(i, arrived)
-        return carry
-
-    lax.fori_loop(0, steps, step, 0)
-
-
-def own_first_kernel(rows_ref, first_src, hidden_ref, slope_ref, first_ref, sems):
-    steps, tile = hidden_ref.shape[0], hidden_ref.shape[2]
-
-    def work(i, arrived):
-        arrived()
         hidden, slope = gelu_and_slope(dot_nt(rows_ref[...], first_ref[block(i, tile), :]))
         hidden_ref[i] = hidden
         slope_ref[i] = slope.astype(slope_ref.dtype)
-
-    over_tiles([(first_src, first_ref)], sems, steps, tile, work)
+        return carry
+
+    lax.fori_loop(0, steps, step, 0)
 
 
 def own_second_kernel(
@@ -158,19 +134,17 @@
     hidden_ref,
     slope_ref,
     second_ref,
-    first_src,
+    first_ref,
     out_ref,
     total_ref,
     gate_ref,
     held_ref,
-    first_ref,
-    sems,
     out_sems,
 ):
     steps, tile = hidden_ref.shape[0], hidden_ref.shape[2]
     rows = total_ref.shape[0]
 
-    def work(j, arrived):
+    def step(j, carry):
         here = block(j, tile)
         back = dot_nt(own_ref[rows:, :], second_ref[here, :])
         terms = hidden_ref[j].astype(jnp.float32) * back
@@ -179,12 +153,12 @@
             gate = gate + terms[:, i * LANES : (i + 1) * LANES]
         gate_ref[...] = gate
         d_pre = (back * slope_ref[j].astype(jnp.float32)).astype(jnp.bfloat16)
-        arrived()
         total_ref[...] += dot_nn(d_pre, first_ref[here, :])
+        return carry
 
     total_ref[...] = jnp.zeros_like(total_ref)
     gate_ref[...] = jnp.zeros_like(gate_ref)
-    over_tiles([(first_src, first_ref)], sems, steps, tile, work)
+    lax.fori_loop(0, steps, step, 0)
 
     experts, copies = out_ref.shape[0], []
     gates = jnp.sum(gate_ref[...], axis=1, keepdims=True)
@@ -437,18 +411,16 @@
     d_far = [d_parts[0]] + [d_far[s] for s in range(1, pairs)]
     x_own = jnp.concatenate([x_keep, across(x_cross, 1)], axis=0)
 
-    steps = groups
-    wide = ((steps, slots, share), bf16)
-    weights = pltpu.VMEM((hidden_units, width), bf16)
+    steps = hidden_units // 1024
+    wide = ((steps, slots, 1024), bf16)
     hidden, slope = call(
         own_first_kernel,
         "own_first",
-        [vmem, anywhere],
+        [vmem] * 2,
         [wide] * 2,
-        [weights, pltpu.SemaphoreType.DMA((steps, 1))],
-        limit=14,
+        limit=12,
         work=1,
-    )(x_own, *in_hbm(weight_in[0]))
+    )(x_own, weight_in[0])
     pair_rows = ((2 * slots, width), bf16)
     (own,) = call(
         join_kernel,
@@ -462,20 +434,18 @@
     (back,) = call(
         partial(own_second_kernel, cap_rows),
         "own_second",
-        [smem] + [vmem] * 4 + [anywhere],
+        [smem] + [vmem] * 5,
         [((experts, stride, LANES), bf16)],
         [
             pltpu.VMEM((slots, width), jnp.float32),
             pltpu.VMEM((slots, LANES), jnp.float32),
             pltpu.VMEM((experts, stride, LANES), bf16),
-            weights,
-            pltpu.SemaphoreType.DMA((steps, 1)),
             pltpu.SemaphoreType.DMA((experts,)),
         ],
         out_spec=anywhere,
-        limit=14,
+        limit=16,
         work=20,
-    )(me, own, hidden, slope, weight_out[0], *in_hbm(weight_in[0]))
+    )(me, own, hidden, slope, weight_out[0], weight_in[0])
     returned = lax.all_to_all(back, "expert", split_axis=0, concat_axis=0, tiled=True)
 
     wide = ((share, 2 * slots), bf16)

time: 62.1 us -> 64.9 us (1.045)
  local copies, waits for them, and re-layouts: 0.09 us -> 7.1 us
  Pallas kernels: 26.9 us -> 23.9 us
    unnamed x11 -> x13, local copies, waits for them, and re-layouts: 0.04 us -> 7.04 us
    pallas_call x1, Pallas kernels: 7.16 us -> 5.24 us  [body(): call(partial(own_second_kernel, cap_rows), 'own_second', [smem] + [vmem]...]
    pallas_call x1, Pallas kernels: 4.56 us -> 3.44 us  [body(): call(own_first_kernel, 'own_first', [vmem] * 2, [wide] * 2, limit=12, wor...]
  transfers between devices with their start and end apart: 13 -> 13, of which waited for: 6 -> 5; matrix products, arithmetic and copies ran while one was open for 0% -> 0% of each run, Pallas kernels for 39% -> 33%
where the time goes in v4:
time: 64.9 us; the launch traced here: 64.6 us
  Pallas kernels  23.9 us (37%)
  starting transfers between devices  20.2 us (31%)
  waiting for transfers between devices  12.6 us (19%)
  local copies, waits for them, and re-layouts  7.1 us (11%)
  between operations  0.83 us (1%)
    ppermute x8, starting transfers between devices, across(): lax.ppermute(chunk, 'expert', [(i, i ^ mask) for i in range(experts)])  12.4 us
    ppermute x8, waiting for transfers between devices, across(): lax.ppermute(chunk, 'expert', [(i, i ^ mask) for i in range(experts)])  10.5 us
    unnamed x13, local copies, waits for them, and re-layouts  7.04 us
    pallas_call x1, Pallas kernels, body(): call(partial(own_second_kernel, cap_rows), 'own_second', [smem] + [vmem]...  5.24 us
    all_to_all x1, starting transfers between devices, body(): lax.all_to_all(back, 'expert', split_axis=0, concat_axis=0, tiled=True)  5.17 us
    pallas_call x1, Pallas kernels, body(): call(far_second_kernel, 'far_second', [anywhere] + [vmem] * 8, [share_row...  4.06 us
    pallas_call x1, Pallas kernels, body(): call(own_first_kernel, 'own_first', [vmem] * 2, [wide] * 2, limit=12, wor...  3.44 us
    pallas_call x1, Pallas kernels, body(): call(near_first_kernel, 'near_first', [smem] + [anywhere] * 5, [wide, wid...  3.2 us
  transfers between devices with their start and end apart: 13, of which 5 were waited for; matrix products, arithmetic and copies ran while one was open for 0% of the time, Pallas kernels for 33%

profile of v4, /device:TPU:0, one launch (start us, length us, event | category | flops | bytes accessed | tf_op | source)
XLA Modules:
  0.0 64.6 jit_solution(14385341709654213439)
XLA Ops:
  0.6 1.6 %pack.1 = (bf16[80,768]{1,0:T(8,128)(2,1)S(1)}, bf16[80,768]{1,0:T(8,128)(2,1)S(1)}, bf16[80,768]{1,0:T(8,128)(2,1)S(1)}, bf16[80,768]{1,0:T(8,128)(2,1)S(1)}, b...) custom-call(s32[1]{0:T(128)} %bitcast.me_ref, bf16[256,768]{1,0:T(8,128)(2,1)} %refs_0_.1, ...), custom_call_target="tpu_custom_call" | custom-call | tf_op jit(solution)/shard_map/pack/pallas_call | solution.py:379
  2.3 3.0 %collective-permute-start = (bf16[160,768]{1,0:T(8,128)(2,1)S(1)}, bf16[160,768]{1,0:T(8,128)(2,1)S(1)}, u32[]{:S(2)}, u32[]{:S(2)}) collective-permute-start(bf16[160,768]{1,0:T(8,128)(2,1)S(1)} %get-tuple-element.34), channel_id=1, source_target_pairs={{0,1},{1,0},{2,3},{3,2},{4,5},{5,4},{6,7},{7,6},{8,9},{9,8},{10,11... | collective-permute-start | bytes 737288 | tf_op jit(solution)/shard_map/ppermute | solution.py:371
  5.3 1.6 %collective-permute-start.1 = (bf16[80,768]{1,0:T(8,128)(2,1)S(1)}, bf16[80,768]{1,0:T(8,128)(2,1)S(1)}, u32[]{:S(2)}, u32[]{:S(2)}) collective-permute-start(bf16[80,768]{1,0:T(8,128)(2,1)S(1)} %get-tuple-element.37), channel_id=1, source_target_pairs={{0,2},{1,3},{2,0},{3,1},{4,6},{5,7},{6,4},{7,5},{8,10},{9,11},{10,... | collective-permute-start | bytes 368648 | tf_op jit(solution)/shard_map/ppermute | solution.py:371
  6.9 2.6 %collective-permute-start.2 = (bf16[80,768]{1,0:T(8,128)(2,1)S(1)}, bf16[80,768]{1,0:T(8,128)(2,1)S(1)}, u32[]{:S(2)}, u32[]{:S(2)}) collective-permute-start(bf16[80,768]{1,0:T(8,128)(2,1)S(1)} %get-tuple-element.38), channel_id=1, source_target_pairs={{0,4},{1,5},{2,6},{3,7},{4,0},{5,1},{6,2},{7,3},{8,12},{9,13},{10,... | collective-permute-start | bytes 368648 | tf_op jit(solution)/shard_map/ppermute | solution.py:371
  9.5 0.2 collective-permute-start.3
  9.7 1.6 %collective-permute-done.near_ref = bf16[160,768]{1,0:T(8,128)(2,1)S(1)} collective-permute-done((bf16[160,768]{1,0:T(8,128)(2,1)S(1)}, bf16[160,768]{1,0:T(8,128)(2,1)S(1)}, u32[]{:S(2)}, u32[]{:S(2)}) %collective-permute-start) | collective-permute-done | bytes 245792 | tf_op jit(solution)/shard_map/ppermute | solution.py:371
  11.3 0.2 collective-permute-done.1.refs_1_
  11.5 7.4 %collective-permute-done.2.refs_2_ = bf16[80,768]{1,0:T(8,128)(2,1)S(1)} collective-permute-done((bf16[80,768]{1,0:T(8,128)(2,1)S(1)}, bf16[80,768]{1,0:T(8,128)(2,1)S(1)}, u32[]{:S(2)}, u32[]{:S(2)}) %collective-permute-start.2) | collective-permute-done | bytes 122912 | tf_op jit(solution)/shard_map/ppermute | solution.py:371
  18.9 0.0 collective-permute-done.3.refs_3_
  19.0 0.6 collective-permute-start.4
  19.5 1.9 %collective-permute-start.5 = (bf16[80,768]{1,0:T(8,128)(2,1)S(1)}, bf16[80,768]{1,0:T(8,128)(2,1)S(1)}, u32[]{:S(2)}, u32[]{:S(2)}) collective-permute-start(bf16[80,768]{1,0:T(8,128)(2,1)S(1)} %get-tuple-element.43), channel_id=1, source_target_pairs={{0,2},{1,3},{2,0},{3,1},{4,6},{5,7},{6,4},{7,5},{8,10},{9,11},{10,... | collective-permute-start | bytes 368648 | tf_op jit(solution)/shard_map/ppermute | solution.py:371
  21.4 1.2 %collective-permute-start.6 = (bf16[80,768]{1,0:T(8,128)(2,1)S(1)}, bf16[80,768]{1,0:T(8,128)(2,1)S(1)}, u32[]{:S(2)}, u32[]{:S(2)}) collective-permute-start(bf16[80,768]{1,0:T(8,128)(2,1)S(1)} %get-tuple-element.44), channel_id=1, source_target_pairs={{0,4},{1,5},{2,6},{3,7},{4,0},{5,1},{6,2},{7,3},{8,12},{9,13},{10,... | collective-permute-start | bytes 368648 | tf_op jit(solution)/shard_map/ppermute | solution.py:371
  22.6 1.4 %collective-permute-start.7 = (bf16[80,768]{1,0:T(8,128)(2,1)S(1)}, bf16[80,768]{1,0:T(8,128)(2,1)S(1)}, u32[]{:S(2)}, u32[]{:S(2)}) collective-permute-start(bf16[80,768]{1,0:T(8,128)(2,1)S(1)} %get-tuple-element.45), channel_id=1, source_target_pairs={{0,6},{1,7},{2,4},{3,5},{4,2},{5,3},{6,0},{7,1},{8,14},{9,15},{10,... | collective-permute-start | bytes 368648 | tf_op jit(solution)/shard_map/ppermute | solution.py:371
  23.9 1.3 %collective-permute-done.4 = bf16[160,768]{1,0:T(8,128)(2,1)S(1)} collective-permute-done((bf16[160,768]{1,0:T(8,128)(2,1)S(1)}, bf16[160,768]{1,0:T(8,128)(2,1)S(1)}, u32[]{:S(2)}, u32[]{:S(2)}) %collective-permute-start.4) | collective-permute-done | bytes 245792 | tf_op jit(solution)/shard_map/ppermute | solution.py:371
  25.2 1.6 %collective-permute-start.9 = (bf16[320,768]{1,0:T(8,128)(2,1)S(1)}, bf16[320,768]{1,0:T(8,128)(2,1)S(1)}, u32[]{:S(2)}, u32[]{:S(2)}) collective-permute-start(bf16[320,768]{1,0:T(8,128)(2,1)S(1)} %constant_dynamic-update-slice_fusion.rows_ref.x_ref), channel_id=1, source_target_pairs={{0,16},{8,24},{16,0},{24,8},{1,17},{9,25},{17,1},{25,9},{2,18},{10... | collective-permute-start | bytes 1474568 | tf_op jit(solution)/shard_map/ppermute | solution.py:374
  26.8 0.0 copy-start
  26.8 2.3 %copy-done = bf16[1,3072,768]{2,1,0:T(8,128)(2,1)S(1)} copy-done((bf16[1,3072,768]{2,1,0:T(8,128)(2,1)S(1)}, bf16[1,3072,768]{2,1,0:T(8,128)(2,1)}, u32[]{:S(2)}) %copy-start) | copy-done | bytes 4718616
  29.1 3.4 %own_first.1 = (bf16[3,320,1024]{2,1,0:T(8,128)(2,1)S(1)}, bf16[3,320,1024]{2,1,0:T(8,128)(2,1)S(1)}) custom-call(bf16[320,768]{1,0:T(8,128)(2,1)S(1)} %constant_dynamic-update-slice_fusion.rows_ref.x_ref, bf16[3072,768]{1,0:T(8,128)(2,1)S(1)} %bitcast.11), custom_call_target="tpu_custom_call" | custom-call | flops 1509949440 | bytes 2949120 | tf_op jit(solution)/shard_map/own_first/pallas_call | solution.py:416
  32.6 0.0 collective-permute-done.5.refs_1_
  32.6 0.0 collective-permute-done.6.refs_2_
  32.6 0.0 collective-permute-done.7.refs_3_
  32.6 0.1 join.1.own_ref.own
  32.7 0.1 collective-permute-start.8
  32.8 0.9 %collective-permute-start.10 = (bf16[320,768]{1,0:T(8,128)(2,1)S(1)}, bf16[320,768]{1,0:T(8,128)(2,1)S(1)}, u32[]{:S(2)}, u32[]{:S(2)}) collective-permute-start(bf16[320,768]{1,0:T(8,128)(2,1)S(1)} %slice.4), channel_id=1, source_target_pairs={{0,16},{8,24},{16,0},{24,8},{1,17},{9,25},{17,1},{25,9},{2,18},{10... | collective-permute-start | bytes 1474568 | tf_op jit(solution)/shard_map/ppermute | solution.py:374
  33.7 0.0 copy-start.1
  33.8 2.3 %copy-done.1 = bf16[1,3072,768]{2,1,0:T(8,128)(2,1)S(1)} copy-done((bf16[1,3072,768]{2,1,0:T(8,128)(2,1)S(1)}, bf16[1,3072,768]{2,1,0:T(8,128)(2,1)}, u32[]{:S(2)}) %copy-start.1) | copy-done | bytes 4718616
  36.1 0.0 copy-start.2
  36.1 2.3 %copy-done.2 = bf16[1,3072,768]{2,1,0:T(8,128)(2,1)S(1)} copy-done((bf16[1,3072,768]{2,1,0:T(8,128)(2,1)S(1)}, bf16[1,3072,768]{2,1,0:T(8,128)(2,1)}, u32[]{:S(2)}) %copy-start.2) | copy-done | bytes 4718616
  38.4 5.2 %own_second.1.after_ref = bf16[8,248,128]{2,1,0:T(8,128)(2,1)} custom-call(s32[1]{0:T(128)} %bitcast.me_ref, bf16[640,768]{1,0:T(8,128)(2,1)S(1)} %join.1.own_ref.own, bf16[3,320,1024]{2,1,0:T(8,128)(2,1)S(1)} %get-tuple-element.42.after_ref.hidden_ref, bf16[3,320,1024]{2,1,0:T(8,128)(2,1)S(1)} %get-tuple-element.46.slope_ref, ...), custom_call_target="tpu_custom_call" | custom-call | flops 30198988800 | bytes 58982400 | tf_op jit(solution)/shard_map/own_second/pallas_call | solution.py:434
  43.7 5.2 %all-to-all-start = ((bf16[8,248,128]{2,1,0:T(8,128)(2,1)}), bf16[8,248,128]{2,1,0:T(8,128)(2,1)S(1)}, u32[]{:S(2)}, u32[]{:S(2)}) async-start(bf16[8,248,128]{2,1,0:T(8,128)(2,1)} %own_second.1.after_ref), calls=%async_computation | async-start | bytes 1015808 | tf_op jit(solution)/shard_map/all_to_all | solution.py:449
  48.8 0.0 collective-permute-done.8.core
  48.9 3.2 %near_first.1 = (bf16[768,640]{1,0:T(8,128)(2,1)S(1)}, bf16[768,640]{1,0:T(8,128)(2,1)S(1)}, bf16[640,768]{1,0:T(8,128)(2,1)S(1)}, bf16[640,768]{1,0:T(8,128)(2,...) custom-call(s32[1]{0:T(128)} %bitcast.6.which_ref, bf16[8,248,128]{2,1,0:T(8,128)(2,1)} %own_second.1.after_ref, ...), custom_call_target="tpu_custom_call" | custom-call | flops 754974720 | bytes 1474560 | tf_op jit(solution)/shard_map/near_first/pallas_call | solution.py:454
  52.1 0.0 collective-permute-done.9.x_ref.x_over
  52.1 0.0 collective-permute-done.10.d_ref.d_over
  52.1 0.1 forward.1
  52.2 0.1 collective-permute-start.11
  52.2 3.2 %near_second.1 = (f32[768,768]{1,0:T(8,128)S(1)}, f32[768,768]{1,0:T(8,128)S(1)}) custom-call(bf16[8,248,128]{2,1,0:T(8,128)(2,1)} %own_second.1.after_ref, bf16[640,768]{1,0:T(8,128)(2,1)S(1)} %get-tuple-element.47.x_ref, bf16[640,768]{1,0:T(8,128)(2,1)S(1)} %get-tuple-element.48.d_ref, bf16[768,640]{1,0:T(8,128)(2,1)S(1)} %get-tuple-element.49.hidden_ref.after_ref, ...), custom_call_target="tpu_custom_call" | custom-call | flops 22649241600 | bytes 44236800 | tf_op jit(solution)/shard_map/near_second/pallas_call | solution.py:462
  55.4 0.0 collective-permute-done.11.diagonal_ref
  55.4 1.7 %far_first.1 = (bf16[768,640]{1,0:T(8,128)(2,1)S(1)}, bf16[768,640]{1,0:T(8,128)(2,1)S(1)}, bf16[640,768]{1,0:T(8,128)(2,1)S(1)}) custom-call(f32[768,768]{1,0:T(8,128)S(1)} %get-tuple-element.52.after_ref.gin_near, bf16[320,768]{1,0:T(8,128)(2,1)S(1)} %collective-permute-done.9.x_ref.x_over, bf16[640,768]{1,0:T(8,128)(2,1)S(1)} %collective-permute-done.11.diagonal_ref, ...), custom_call_target="tpu_custom_call" | custom-call | tf_op jit(solution)/shard_map/far_first/pallas_call | solution.py:476
  57.2 0.0 copy-start.3
  57.2 0.0 copy-start.4
  57.2 0.0 copy-start.5
  57.2 4.1 %far_second.1 = (bf16[768,768]{1,0:T(8,128)(2,1)}, bf16[768,768]{1,0:T(8,128)(2,1)}) custom-call(bf16[768,640]{1,0:T(8,128)(2,1)S(1)} %get-tuple-element.54.after_ref.hidden_ref, bf16[320,768]{1,0:T(8,128)(2,1)S(1)} %collective-permute-done.10.d_ref.d_over, bf16[640,768]{1,0:T(8,128)(2,1)S(1)} %collective-permute-done.11.diagonal_ref, ...), custom_call_target="tpu_custom_call" | custom-call | tf_op jit(solution)/shard_map/far_second/pallas_call | solution.py:483
  61.3 2.1 %all-to-all-done.back_ref = bf16[8,248,128]{2,1,0:T(8,128)(2,1)S(1)} async-done(((bf16[8,248,128]{2,1,0:T(8,128)(2,1)}), bf16[8,248,128]{2,1,0:T(8,128)(2,1)S(1)}, u32[]{:S(2)}, u32[]{:S(2)}) %all-to-all-start) | async-done | bytes 507936 | tf_op jit(solution)/shard_map/all_to_all | solution.py:449
  63.4 0.0 copy-done.3
  63.4 0.0 copy-done.4
  63.4 0.0 copy-done.5
  63.4 1.2 %unpack.1 = (bf16[256,768]{1,0:T(8,128)(2,1)}, f32[1,256]{1,0:T(1,128)}) custom-call(bf16[768,768]{1,0:T(8,128)(2,1)} %get-tuple-element.58.after_ref, bf16[8,248,128]{2,1,0:T(8,128)(2,1)S(1)} %all-to-all-done.back_ref, f32[1,256]{1,0:T(1,128)S(1)} %bitcast.16, s32[1,256]{1,0:T(1,128)S(1)} %bitcast.18, s32[1,256]{1,0:T(1,128)S(1)} %bitcast.20), custom_call_target="tpu_custom_call" | custom-call | tf_op jit(solution)/shard_map/unpack/pallas_call | solution.py:493
  (5 shorter events, 0.1 us)
Async XLA Ops:
  2.3 9.0 %collective-permute-start = (bf16[160,768]{1,0:T(8,128)(2,1)S(1)}, bf16[160,768]{1,0:T(8,128)(2,1)S(1)}, u32[]{:S(2)}, u32[]{:S(2)}) collective-permute-start(bf16[160,768]{1,0:T(8,128)(2,1)S(1)} %get-tuple-element.34), channel_id=1, source_target_pairs={{0,1},{1,0},{2,3},{3,2},{4,5},{5,4},{6,7},{7,6},{8,9},{9,8},{10,11... | collective-permute-start | bytes 737288 | tf_op jit(solution)/shard_map/ppermute | solution.py:371
  5.3 6.2 %collective-permute-start.1 = (bf16[80,768]{1,0:T(8,128)(2,1)S(1)}, bf16[80,768]{1,0:T(8,128)(2,1)S(1)}, u32[]{:S(2)}, u32[]{:S(2)}) collective-permute-start(bf16[80,768]{1,0:T(8,128)(2,1)S(1)} %get-tuple-element.37), channel_id=1, source_target_pairs={{0,2},{1,3},{2,0},{3,1},{4,6},{5,7},{6,4},{7,5},{8,10},{9,11},{10,... | collective-permute-start | bytes 368648 | tf_op jit(solution)/shard_map/ppermute | solution.py:371
  6.9 12.0 %collective-permute-start.2 = (bf16[80,768]{1,0:T(8,128)(2,1)S(1)}, bf16[80,768]{1,0:T(8,128)(2,1)S(1)}, u32[]{:S(2)}, u32[]{:S(2)}) collective-permute-start(bf16[80,768]{1,0:T(8,128)(2,1)S(1)} %get-tuple-element.38), channel_id=1, source_target_pairs={{0,4},{1,5},{2,6},{3,7},{4,0},{5,1},{6,2},{7,3},{8,12},{9,13},{10,... | collective-permute-start | bytes 368648 | tf_op jit(solution)/shard_map/ppermute | solution.py:371
  9.5 9.4 %collective-permute-start.3 = (bf16[80,768]{1,0:T(8,128)(2,1)S(1)}, bf16[80,768]{1,0:T(8,128)(2,1)S(1)}, u32[]{:S(2)}, u32[]{:S(2)}) collective-permute-start(bf16[80,768]{1,0:T(8,128)(2,1)S(1)} %get-tuple-element.39), channel_id=1, source_target_pairs={{0,6},{1,7},{2,4},{3,5},{4,2},{5,3},{6,0},{7,1},{8,14},{9,15},{10,... | collective-permute-start | bytes 368648 | tf_op jit(solution)/shard_map/ppermute | solution.py:371
  19.0 6.3 %collective-permute-start.4 = (bf16[160,768]{1,0:T(8,128)(2,1)S(1)}, bf16[160,768]{1,0:T(8,128)(2,1)S(1)}, u32[]{:S(2)}, u32[]{:S(2)}) collective-permute-start(bf16[160,768]{1,0:T(8,128)(2,1)S(1)} %get-tuple-element.41), channel_id=1, source_target_pairs={{0,1},{1,0},{2,3},{3,2},{4,5},{5,4},{6,7},{7,6},{8,9},{9,8},{10,11... | collective-permute-start | bytes 737288 | tf_op jit(solution)/shard_map/ppermute | solution.py:371
  19.5 13.1 %collective-permute-start.5 = (bf16[80,768]{1,0:T(8,128)(2,1)S(1)}, bf16[80,768]{1,0:T(8,128)(2,1)S(1)}, u32[]{:S(2)}, u32[]{:S(2)}) collective-permute-start(bf16[80,768]{1,0:T(8,128)(2,1)S(1)} %get-tuple-element.43), channel_id=1, source_target_pairs={{0,2},{1,3},{2,0},{3,1},{4,6},{5,7},{6,4},{7,5},{8,10},{9,11},{10,... | collective-permute-start | bytes 368648 | tf_op jit(solution)/shard_map/ppermute | solution.py:371
  21.4 11.2 %collective-permute-start.6 = (bf16[80,768]{1,0:T(8,128)(2,1)S(1)}, bf16[80,768]{1,0:T(8,128)(2,1)S(1)}, u32[]{:S(2)}, u32[]{:S(2)}) collective-permute-start(bf16[80,768]{1,0:T(8,128)(2,1)S(1)} %get-tuple-element.44), channel_id=1, source_target_pairs={{0,4},{1,5},{2,6},{3,7},{4,0},{5,1},{6,2},{7,3},{8,12},{9,13},{10,... | collective-permute-start | bytes 368648 | tf_op jit(solution)/shard_map/ppermute | solution.py:371
  22.6 10.0 %collective-permute-start.7 = (bf16[80,768]{1,0:T(8,128)(2,1)S(1)}, bf16[80,768]{1,0:T(8,128)(2,1)S(1)}, u32[]{:S(2)}, u32[]{:S(2)}) collective-permute-start(bf16[80,768]{1,0:T(8,128)(2,1)S(1)} %get-tuple-element.45), channel_id=1, source_target_pairs={{0,6},{1,7},{2,4},{3,5},{4,2},{5,3},{6,0},{7,1},{8,14},{9,15},{10,... | collective-permute-start | bytes 368648 | tf_op jit(solution)/shard_map/ppermute | solution.py:371
  25.2 26.8 %collective-permute-start.9 = (bf16[320,768]{1,0:T(8,128)(2,1)S(1)}, bf16[320,768]{1,0:T(8,128)(2,1)S(1)}, u32[]{:S(2)}, u32[]{:S(2)}) collective-permute-start(bf16[320,768]{1,0:T(8,128)(2,1)S(1)} %constant_dynamic-update-slice_fusion.rows_ref.x_ref), channel_id=1, source_target_pairs={{0,16},{8,24},{16,0},{24,8},{1,17},{9,25},{17,1},{25,9},{2,18},{10... | collective-permute-start | bytes 1474568 | tf_op jit(solution)/shard_map/ppermute | solution.py:374
  26.8 2.3 %copy-start = (bf16[1,3072,768]{2,1,0:T(8,128)(2,1)S(1)}, bf16[1,3072,768]{2,1,0:T(8,128)(2,1)}, u32[]{:S(2)}) copy-start(bf16[1,3072,768]{2,1,0:T(8,128)(2,1)} %param.14) | copy-start | bytes 14155780
  32.7 16.2 %collective-permute-start.8 = (bf16[640,768]{1,0:T(8,128)(2,1)S(1)}, bf16[640,768]{1,0:T(8,128)(2,1)}, u32[]{:S(2)}, u32[]{:S(2)}) collective-permute-start(bf16[640,768]{1,0:T(8,128)(2,1)S(1)} %join.1.own_ref.own), channel_id=1, source_target_pairs={{0,8},{8,0},{16,24},{24,16},{1,9},{9,1},{17,25},{25,17},{2,10},{10... | collective-permute-start | bytes 2949128 | tf_op jit(solution)/shard_map/ppermute | solution.py:374
  32.8 19.3 %collective-permute-start.10 = (bf16[320,768]{1,0:T(8,128)(2,1)S(1)}, bf16[320,768]{1,0:T(8,128)(2,1)S(1)}, u32[]{:S(2)}, u32[]{:S(2)}) collective-permute-start(bf16[320,768]{1,0:T(8,128)(2,1)S(1)} %slice.4), channel_id=1, source_target_pairs={{0,16},{8,24},{16,0},{24,8},{1,17},{9,25},{17,1},{25,9},{2,18},{10... | collective-permute-start | bytes 1474568 | tf_op jit(solution)/shard_map/ppermute | solution.py:374
  33.7 2.3 %copy-start.1 = (bf16[1,3072,768]{2,1,0:T(8,128)(2,1)S(1)}, bf16[1,3072,768]{2,1,0:T(8,128)(2,1)}, u32[]{:S(2)}) copy-start(bf16[1,3072,768]{2,1,0:T(8,128)(2,1)} %param.14) | copy-start | bytes 14155780
  36.1 2.3 %copy-start.2 = (bf16[1,3072,768]{2,1,0:T(8,128)(2,1)S(1)}, bf16[1,3072,768]{2,1,0:T(8,128)(2,1)}, u32[]{:S(2)}) copy-start(bf16[1,3072,768]{2,1,0:T(8,128)(2,1)} %param.15) | copy-start | bytes 14155780
  43.7 19.7 %all-to-all-start = ((bf16[8,248,128]{2,1,0:T(8,128)(2,1)}), bf16[8,248,128]{2,1,0:T(8,128)(2,1)S(1)}, u32[]{:S(2)}, u32[]{:S(2)}) async-start(bf16[8,248,128]{2,1,0:T(8,128)(2,1)} %own_second.1.after_ref), calls=%async_computation | async-start | bytes 1015808 | tf_op jit(solution)/shard_map/all_to_all | solution.py:449
  52.2 3.3 %collective-permute-start.11 = (bf16[640,768]{1,0:T(8,128)(2,1)S(1)}, bf16[640,768]{1,0:T(8,128)(2,1)S(1)}, u32[]{:S(2)}, u32[]{:S(2)}) collective-permute-start(bf16[640,768]{1,0:T(8,128)(2,1)S(1)} %forward.1), channel_id=1, source_target_pairs={{0,8},{8,0},{16,24},{24,16},{1,9},{9,1},{17,25},{25,17},{2,10},{10... | collective-permute-start | bytes 2949128 | tf_op jit(solution)/shard_map/ppermute | solution.py:374
  57.2 6.2 %copy-start.3 = (f32[256]{0:T(256)S(1)}, f32[256]{0:T(256)}, u32[]{:S(2)}) copy-start(f32[256]{0:T(256)} %param.10) | copy-start | bytes 3076
  57.2 6.2 %copy-start.4 = (s32[256]{0:T(256)S(1)}, s32[256]{0:T(256)}, u32[]{:S(2)}) copy-start(s32[256]{0:T(256)} %param.11) | copy-start | bytes 3076
  57.2 6.2 %copy-start.5 = (s32[256]{0:T(256)S(1)}, s32[256]{0:T(256)}, u32[]{:S(2)}) copy-start(s32[256]{0:T(256)} %param.12) | copy-start | bytes 3076

commit v5 on v3

--- a/solution.py
+++ b/solution.py
@@ -158,19 +158,17 @@
     hidden_ref,
     slope_ref,
     second_ref,
-    first_src,
+    first_ref,
     out_ref,
     total_ref,
     gate_ref,
     held_ref,
-    first_ref,
-    sems,
     out_sems,
 ):
     steps, tile = hidden_ref.shape[0], hidden_ref.shape[2]
     rows = total_ref.shape[0]
 
-    def work(j, arrived):
+    def step(j, carry):
         here = block(j, tile)
         back = dot_nt(own_ref[rows:, :], second_ref[here, :])
         terms = hidden_ref[j].astype(jnp.float32) * back
@@ -179,12 +177,12 @@
             gate = gate + terms[:, i * LANES : (i + 1) * LANES]
         gate_ref[...] = gate
         d_pre = (back * slope_ref[j].astype(jnp.float32)).astype(jnp.bfloat16)
-        arrived()
         total_ref[...] += dot_nn(d_pre, first_ref[here, :])
+        return carry
 
     total_ref[...] = jnp.zeros_like(total_ref)
     gate_ref[...] = jnp.zeros_like(gate_ref)
-    over_tiles([(first_src, first_ref)], sems, steps, tile, work)
+    lax.fori_loop(0, steps, step, 0)
 
     experts, copies = out_ref.shape[0], []
     gates = jnp.sum(gate_ref[...], axis=1, keepdims=True)
@@ -437,8 +435,8 @@
     d_far = [d_parts[0]] + [d_far[s] for s in range(1, pairs)]
     x_own = jnp.concatenate([x_keep, across(x_cross, 1)], axis=0)
 
-    steps = groups
-    wide = ((steps, slots, share), bf16)
+    steps = hidden_units // 1024
+    wide = ((steps, slots, 1024), bf16)
     weights = pltpu.VMEM((hidden_units, width), bf16)
     hidden, slope = call(
         own_first_kernel,
@@ -446,7 +444,7 @@
         [vmem, anywhere],
         [wide] * 2,
         [weights, pltpu.SemaphoreType.DMA((steps, 1))],
-        limit=14,
+        limit=11,
         work=1,
     )(x_own, *in_hbm(weight_in[0]))
     pair_rows = ((2 * slots, width), bf16)
@@ -462,20 +460,18 @@
     (back,) = call(
         partial(own_second_kernel, cap_rows),
         "own_second",
-        [smem] + [vmem] * 4 + [anywhere],
+        [smem] + [vmem] * 5,
         [((experts, stride, LANES), bf16)],
         [
             pltpu.VMEM((slots, width), jnp.float32),
             pltpu.VMEM((slots, LANES), jnp.float32),
             pltpu.VMEM((experts, stride, LANES), bf16),
-            weights,
-            pltpu.SemaphoreType.DMA((steps, 1)),
             pltpu.SemaphoreType.DMA((experts,)),
         ],
         out_spec=anywhere,
-        limit=14,
+        limit=10,
         work=20,
-    )(me, own, hidden, slope, weight_out[0], *in_hbm(weight_in[0]))
+    )(me, own, hidden, slope, weight_out[0], weight_in[0])
     returned = lax.all_to_all(back, "expert", split_axis=0, concat_axis=0, tiled=True)
 
     wide = ((share, 2 * slots), bf16)

time: 62.1 us -> 60.2 us (0.969)
  Pallas kernels: 26.9 us -> 25.4 us
  waiting for transfers between devices: 13.2 us -> 12.3 us
    pallas_call x1, Pallas kernels: 7.16 us -> 5.24 us  [body(): call(partial(own_second_kernel, cap_rows), 'own_second', [smem] + [vmem]...]
  transfers between devices with their start and end apart: 13 -> 13, of which waited for: 6 -> 6; matrix products, arithmetic and copies ran while one was open for 0% -> 0% of each run, Pallas kernels for 39% -> 38%
where the time goes in v5:
time: 60.2 us; the launch traced here: 60 us
  Pallas kernels  25.4 us (42%)
  starting transfers between devices  20.8 us (35%)
  waiting for transfers between devices  12.3 us (20%)
  between operations  0.82 us (1%)
  local copies, waits for them, and re-layouts  0.69 us (1%)
    ppermute x8, starting transfers between devices, across(): lax.ppermute(chunk, 'expert', [(i, i ^ mask) for i in range(experts)])  12.4 us
    ppermute x8, waiting for transfers between devices, across(): lax.ppermute(chunk, 'expert', [(i, i ^ mask) for i in range(experts)])  10.7 us
    pallas_call x1, Pallas kernels, body(): call(partial(own_second_kernel, cap_rows), 'own_second', [smem] + [vmem]...  5.24 us
    all_to_all x1, starting transfers between devices, body(): lax.all_to_all(back, 'expert', split_axis=0, concat_axis=0, tiled=True)  5.19 us
    pallas_call x1, Pallas kernels, body(): call(own_first_kernel, 'own_first', [vmem, anywhere], [wide] * 2, [weight...  4.94 us
    pallas_call x1, Pallas kernels, body(): call(far_second_kernel, 'far_second', [anywhere] + [vmem] * 8, [share_row...  4.06 us
    ppermute x4, starting transfers between devices, over(): return lax.ppermute(chunk, 'dp', [(i, i ^ mask) for i in range(groups)])  3.25 us
    pallas_call x1, Pallas kernels, body(): call(near_first_kernel, 'near_first', [smem] + [anywhere] * 5, [wide, wid...  3.21 us
  transfers between devices with their start and end apart: 13, of which 6 were waited for; matrix products, arithmetic and copies ran while one was open for 0% of the time, Pallas kernels for 38%

profile of v5, /device:TPU:0, one launch (start us, length us, event | category | flops | bytes accessed | tf_op | source)
XLA Modules:
  0.0 60.0 jit_solution(2531609534615841383)
XLA Ops:
  0.6 1.6 %pack.1 = (bf16[80,768]{1,0:T(8,128)(2,1)S(1)}, bf16[80,768]{1,0:T(8,128)(2,1)S(1)}, bf16[80,768]{1,0:T(8,128)(2,1)S(1)}, bf16[80,768]{1,0:T(8,128)(2,1)S(1)}, b...) custom-call(s32[1]{0:T(128)} %bitcast.me_ref, bf16[256,768]{1,0:T(8,128)(2,1)} %refs_0_.1, ...), custom_call_target="tpu_custom_call" | custom-call | tf_op jit(solution)/shard_map/pack/pallas_call | solution.py:403
  2.3 3.0 %collective-permute-start = (bf16[160,768]{1,0:T(8,128)(2,1)S(1)}, bf16[160,768]{1,0:T(8,128)(2,1)S(1)}, u32[]{:S(2)}, u32[]{:S(2)}) collective-permute-start(bf16[160,768]{1,0:T(8,128)(2,1)S(1)} %get-tuple-element.34), channel_id=1, source_target_pairs={{0,1},{1,0},{2,3},{3,2},{4,5},{5,4},{6,7},{7,6},{8,9},{9,8},{10,11... | collective-permute-start | bytes 737288 | tf_op jit(solution)/shard_map/ppermute | solution.py:395
  5.3 1.6 %collective-permute-start.1 = (bf16[80,768]{1,0:T(8,128)(2,1)S(1)}, bf16[80,768]{1,0:T(8,128)(2,1)S(1)}, u32[]{:S(2)}, u32[]{:S(2)}) collective-permute-start(bf16[80,768]{1,0:T(8,128)(2,1)S(1)} %get-tuple-element.37), channel_id=1, source_target_pairs={{0,2},{1,3},{2,0},{3,1},{4,6},{5,7},{6,4},{7,5},{8,10},{9,11},{10,... | collective-permute-start | bytes 368648 | tf_op jit(solution)/shard_map/ppermute | solution.py:395
  6.9 2.6 %collective-permute-start.2 = (bf16[80,768]{1,0:T(8,128)(2,1)S(1)}, bf16[80,768]{1,0:T(8,128)(2,1)S(1)}, u32[]{:S(2)}, u32[]{:S(2)}) collective-permute-start(bf16[80,768]{1,0:T(8,128)(2,1)S(1)} %get-tuple-element.38), channel_id=1, source_target_pairs={{0,4},{1,5},{2,6},{3,7},{4,0},{5,1},{6,2},{7,3},{8,12},{9,13},{10,... | collective-permute-start | bytes 368648 | tf_op jit(solution)/shard_map/ppermute | solution.py:395
  9.5 0.2 collective-permute-start.3
  9.7 1.6 %collective-permute-done.near_ref = bf16[160,768]{1,0:T(8,128)(2,1)S(1)} collective-permute-done((bf16[160,768]{1,0:T(8,128)(2,1)S(1)}, bf16[160,768]{1,0:T(8,128)(2,1)S(1)}, u32[]{:S(2)}, u32[]{:S(2)}) %collective-permute-start) | collective-permute-done | bytes 245792 | tf_op jit(solution)/shard_map/ppermute | solution.py:395
  11.3 0.2 collective-permute-done.1.refs_1_
  11.5 7.4 %collective-permute-done.2.refs_2_ = bf16[80,768]{1,0:T(8,128)(2,1)S(1)} collective-permute-done((bf16[80,768]{1,0:T(8,128)(2,1)S(1)}, bf16[80,768]{1,0:T(8,128)(2,1)S(1)}, u32[]{:S(2)}, u32[]{:S(2)}) %collective-permute-start.2) | collective-permute-done | bytes 122912 | tf_op jit(solution)/shard_map/ppermute | solution.py:395
  18.9 0.0 collective-permute-done.3.refs_3_
  19.0 0.6 collective-permute-start.4
  19.5 1.9 %collective-permute-start.5 = (bf16[80,768]{1,0:T(8,128)(2,1)S(1)}, bf16[80,768]{1,0:T(8,128)(2,1)S(1)}, u32[]{:S(2)}, u32[]{:S(2)}) collective-permute-start(bf16[80,768]{1,0:T(8,128)(2,1)S(1)} %get-tuple-element.43), channel_id=1, source_target_pairs={{0,2},{1,3},{2,0},{3,1},{4,6},{5,7},{6,4},{7,5},{8,10},{9,11},{10,... | collective-permute-start | bytes 368648 | tf_op jit(solution)/shard_map/ppermute | solution.py:395
  21.4 1.2 %collective-permute-start.6 = (bf16[80,768]{1,0:T(8,128)(2,1)S(1)}, bf16[80,768]{1,0:T(8,128)(2,1)S(1)}, u32[]{:S(2)}, u32[]{:S(2)}) collective-permute-start(bf16[80,768]{1,0:T(8,128)(2,1)S(1)} %get-tuple-element.44), channel_id=1, source_target_pairs={{0,4},{1,5},{2,6},{3,7},{4,0},{5,1},{6,2},{7,3},{8,12},{9,13},{10,... | collective-permute-start | bytes 368648 | tf_op jit(solution)/shard_map/ppermute | solution.py:395
  22.6 1.4 %collective-permute-start.7 = (bf16[80,768]{1,0:T(8,128)(2,1)S(1)}, bf16[80,768]{1,0:T(8,128)(2,1)S(1)}, u32[]{:S(2)}, u32[]{:S(2)}) collective-permute-start(bf16[80,768]{1,0:T(8,128)(2,1)S(1)} %get-tuple-element.45), channel_id=1, source_target_pairs={{0,6},{1,7},{2,4},{3,5},{4,2},{5,3},{6,0},{7,1},{8,14},{9,15},{10,... | collective-permute-start | bytes 368648 | tf_op jit(solution)/shard_map/ppermute | solution.py:395
  23.9 1.3 %collective-permute-done.4 = bf16[160,768]{1,0:T(8,128)(2,1)S(1)} collective-permute-done((bf16[160,768]{1,0:T(8,128)(2,1)S(1)}, bf16[160,768]{1,0:T(8,128)(2,1)S(1)}, u32[]{:S(2)}, u32[]{:S(2)}) %collective-permute-start.4) | collective-permute-done | bytes 245792 | tf_op jit(solution)/shard_map/ppermute | solution.py:395
  25.2 0.0 slice-start
  25.2 1.6 %collective-permute-start.9 = (bf16[320,768]{1,0:T(8,128)(2,1)S(1)}, bf16[320,768]{1,0:T(8,128)(2,1)S(1)}, u32[]{:S(2)}, u32[]{:S(2)}) collective-permute-start(bf16[320,768]{1,0:T(8,128)(2,1)S(1)} %constant_dynamic-update-slice_fusion.rows_ref.x_ref), channel_id=1, source_target_pairs={{0,16},{8,24},{16,0},{24,8},{1,17},{9,25},{17,1},{25,9},{2,18},{10... | collective-permute-start | bytes 1474568 | tf_op jit(solution)/shard_map/ppermute | solution.py:398
  26.8 0.0 slice-start.1
  26.8 4.9 %own_first.1 = (bf16[3,320,1024]{2,1,0:T(8,128)(2,1)S(1)}, bf16[3,320,1024]{2,1,0:T(8,128)(2,1)S(1)}) custom-call(bf16[320,768]{1,0:T(8,128)(2,1)S(1)} %constant_dynamic-update-slice_fusion.rows_ref.x_ref, bf16[3072,768]{1,0:T(8,128)(2,1)} %bitcast.10), custom_call_target="tpu_custom_call" | custom-call | flops 1509949440 | bytes 2949120 | tf_op jit(solution)/shard_map/own_first/pallas_call | solution.py:441
  31.8 0.0 collective-permute-done.5.refs_1_
  31.8 0.2 collective-permute-done.6.refs_2_
  32.0 0.0 collective-permute-done.7.refs_3_
  32.0 0.0 copy-start
  32.0 0.1 join.1.own_ref.own
  32.1 0.1 collective-permute-start.8
  32.2 1.5 %collective-permute-start.10 = (bf16[320,768]{1,0:T(8,128)(2,1)S(1)}, bf16[320,768]{1,0:T(8,128)(2,1)S(1)}, u32[]{:S(2)}, u32[]{:S(2)}) collective-permute-start(bf16[320,768]{1,0:T(8,128)(2,1)S(1)} %slice.4), channel_id=1, source_target_pairs={{0,16},{8,24},{16,0},{24,8},{1,17},{9,25},{17,1},{25,9},{2,18},{10... | collective-permute-start | bytes 1474568 | tf_op jit(solution)/shard_map/ppermute | solution.py:398
  33.8 0.0 slice-done
  33.8 0.0 slice-done.1
  33.8 0.6 copy-done
  34.4 5.2 %own_second.1.after_ref = bf16[8,248,128]{2,1,0:T(8,128)(2,1)} custom-call(s32[1]{0:T(128)} %bitcast.me_ref, bf16[640,768]{1,0:T(8,128)(2,1)S(1)} %join.1.own_ref.own, bf16[3,320,1024]{2,1,0:T(8,128)(2,1)S(1)} %get-tuple-element.42.after_ref.hidden_ref, bf16[3,320,1024]{2,1,0:T(8,128)(2,1)S(1)} %get-tuple-element.46.slope_ref, ...), custom_call_target="tpu_custom_call" | custom-call | flops 30198988800 | bytes 58982400 | tf_op jit(solution)/shard_map/own_second/pallas_call | solution.py:460
  39.6 5.2 %all-to-all-start = ((bf16[8,248,128]{2,1,0:T(8,128)(2,1)}), bf16[8,248,128]{2,1,0:T(8,128)(2,1)S(1)}, u32[]{:S(2)}, u32[]{:S(2)}) async-start(bf16[8,248,128]{2,1,0:T(8,128)(2,1)} %own_second.1.after_ref), calls=%async_computation | async-start | bytes 1015808 | tf_op jit(solution)/shard_map/all_to_all | solution.py:475
  44.8 0.0 collective-permute-done.8.core
  44.8 3.2 %near_first.1 = (bf16[768,640]{1,0:T(8,128)(2,1)S(1)}, bf16[768,640]{1,0:T(8,128)(2,1)S(1)}, bf16[640,768]{1,0:T(8,128)(2,1)S(1)}, bf16[640,768]{1,0:T(8,128)(2,...) custom-call(s32[1]{0:T(128)} %bitcast.6.which_ref, bf16[8,248,128]{2,1,0:T(8,128)(2,1)} %own_second.1.after_ref, ...), custom_call_target="tpu_custom_call" | custom-call | flops 754974720 | bytes 1474560 | tf_op jit(solution)/shard_map/near_first/pallas_call | solution.py:480
  48.0 0.0 collective-permute-done.9.x_ref.x_over
  48.0 0.0 collective-permute-done.10.d_ref.d_over
  48.0 0.1 forward.1
  48.1 0.1 collective-permute-start.11
  48.2 3.2 %near_second.1 = (f32[768,768]{1,0:T(8,128)S(1)}, f32[768,768]{1,0:T(8,128)S(1)}) custom-call(bf16[8,248,128]{2,1,0:T(8,128)(2,1)} %own_second.1.after_ref, bf16[640,768]{1,0:T(8,128)(2,1)S(1)} %get-tuple-element.47.x_ref, bf16[640,768]{1,0:T(8,128)(2,1)S(1)} %get-tuple-element.48.d_ref, bf16[768,640]{1,0:T(8,128)(2,1)S(1)} %get-tuple-element.49.hidden_ref.after_ref, ...), custom_call_target="tpu_custom_call" | custom-call | flops 22649241600 | bytes 44236800 | tf_op jit(solution)/shard_map/near_second/pallas_call | solution.py:488
  51.4 0.0 collective-permute-done.11.diagonal_ref
  51.4 1.7 %far_first.1 = (bf16[768,640]{1,0:T(8,128)(2,1)S(1)}, bf16[768,640]{1,0:T(8,128)(2,1)S(1)}, bf16[640,768]{1,0:T(8,128)(2,1)S(1)}) custom-call(f32[768,768]{1,0:T(8,128)S(1)} %get-tuple-element.52.after_ref.gin_near, bf16[320,768]{1,0:T(8,128)(2,1)S(1)} %collective-permute-done.9.x_ref.x_over, bf16[640,768]{1,0:T(8,128)(2,1)S(1)} %collective-permute-done.11.diagonal_ref, ...), custom_call_target="tpu_custom_call" | custom-call | tf_op jit(solution)/shard_map/far_first/pallas_call | solution.py:502
  53.1 0.0 copy-start.1
  53.1 0.0 copy-start.2
  53.1 0.0 copy-start.3
  53.2 4.1 %far_second.1 = (bf16[768,768]{1,0:T(8,128)(2,1)}, bf16[768,768]{1,0:T(8,128)(2,1)}) custom-call(bf16[768,640]{1,0:T(8,128)(2,1)S(1)} %get-tuple-element.54.after_ref.hidden_ref, bf16[320,768]{1,0:T(8,128)(2,1)S(1)} %collective-permute-done.10.d_ref.d_over, bf16[640,768]{1,0:T(8,128)(2,1)S(1)} %collective-permute-done.11.diagonal_ref, ...), custom_call_target="tpu_custom_call" | custom-call | tf_op jit(solution)/shard_map/far_second/pallas_call | solution.py:509
  57.2 1.5 %all-to-all-done.back_ref = bf16[8,248,128]{2,1,0:T(8,128)(2,1)S(1)} async-done(((bf16[8,248,128]{2,1,0:T(8,128)(2,1)}), bf16[8,248,128]{2,1,0:T(8,128)(2,1)S(1)}, u32[]{:S(2)}, u32[]{:S(2)}) %all-to-all-start) | async-done | bytes 507936 | tf_op jit(solution)/shard_map/all_to_all | solution.py:475
  58.8 0.0 copy-done.1
  58.8 0.0 copy-done.2
  58.8 0.0 copy-done.3
  58.8 1.2 %unpack.1 = (bf16[256,768]{1,0:T(8,128)(2,1)}, f32[1,256]{1,0:T(1,128)}) custom-call(bf16[768,768]{1,0:T(8,128)(2,1)} %get-tuple-element.58.after_ref, bf16[8,248,128]{2,1,0:T(8,128)(2,1)S(1)} %all-to-all-done.back_ref, f32[1,256]{1,0:T(1,128)S(1)} %bitcast.18, s32[1,256]{1,0:T(1,128)S(1)} %bitcast.20, s32[1,256]{1,0:T(1,128)S(1)} %bitcast.22), custom_call_target="tpu_custom_call" | custom-call | tf_op jit(solution)/shard_map/unpack/pallas_call | solution.py:519
  (6 shorter events, 0.1 us)
Async XLA Ops:
  2.3 9.0 %collective-permute-start = (bf16[160,768]{1,0:T(8,128)(2,1)S(1)}, bf16[160,768]{1,0:T(8,128)(2,1)S(1)}, u32[]{:S(2)}, u32[]{:S(2)}) collective-permute-start(bf16[160,768]{1,0:T(8,128)(2,1)S(1)} %get-tuple-element.34), channel_id=1, source_target_pairs={{0,1},{1,0},{2,3},{3,2},{4,5},{5,4},{6,7},{7,6},{8,9},{9,8},{10,11... | collective-permute-start | bytes 737288 | tf_op jit(solution)/shard_map/ppermute | solution.py:395
  5.3 6.2 %collective-permute-start.1 = (bf16[80,768]{1,0:T(8,128)(2,1)S(1)}, bf16[80,768]{1,0:T(8,128)(2,1)S(1)}, u32[]{:S(2)}, u32[]{:S(2)}) collective-permute-start(bf16[80,768]{1,0:T(8,128)(2,1)S(1)} %get-tuple-element.37), channel_id=1, source_target_pairs={{0,2},{1,3},{2,0},{3,1},{4,6},{5,7},{6,4},{7,5},{8,10},{9,11},{10,... | collective-permute-start | bytes 368648 | tf_op jit(solution)/shard_map/ppermute | solution.py:395
  6.9 12.0 %collective-permute-start.2 = (bf16[80,768]{1,0:T(8,128)(2,1)S(1)}, bf16[80,768]{1,0:T(8,128)(2,1)S(1)}, u32[]{:S(2)}, u32[]{:S(2)}) collective-permute-start(bf16[80,768]{1,0:T(8,128)(2,1)S(1)} %get-tuple-element.38), channel_id=1, source_target_pairs={{0,4},{1,5},{2,6},{3,7},{4,0},{5,1},{6,2},{7,3},{8,12},{9,13},{10,... | collective-permute-start | bytes 368648 | tf_op jit(solution)/shard_map/ppermute | solution.py:395
  9.5 9.4 %collective-permute-start.3 = (bf16[80,768]{1,0:T(8,128)(2,1)S(1)}, bf16[80,768]{1,0:T(8,128)(2,1)S(1)}, u32[]{:S(2)}, u32[]{:S(2)}) collective-permute-start(bf16[80,768]{1,0:T(8,128)(2,1)S(1)} %get-tuple-element.39), channel_id=1, source_target_pairs={{0,6},{1,7},{2,4},{3,5},{4,2},{5,3},{6,0},{7,1},{8,14},{9,15},{10,... | collective-permute-start | bytes 368648 | tf_op jit(solution)/shard_map/ppermute | solution.py:395
  19.0 6.3 %collective-permute-start.4 = (bf16[160,768]{1,0:T(8,128)(2,1)S(1)}, bf16[160,768]{1,0:T(8,128)(2,1)S(1)}, u32[]{:S(2)}, u32[]{:S(2)}) collective-permute-start(bf16[160,768]{1,0:T(8,128)(2,1)S(1)} %get-tuple-element.41), channel_id=1, source_target_pairs={{0,1},{1,0},{2,3},{3,2},{4,5},{5,4},{6,7},{7,6},{8,9},{9,8},{10,11... | collective-permute-start | bytes 737288 | tf_op jit(solution)/shard_map/ppermute | solution.py:395
  19.5 12.2 %collective-permute-start.5 = (bf16[80,768]{1,0:T(8,128)(2,1)S(1)}, bf16[80,768]{1,0:T(8,128)(2,1)S(1)}, u32[]{:S(2)}, u32[]{:S(2)}) collective-permute-start(bf16[80,768]{1,0:T(8,128)(2,1)S(1)} %get-tuple-element.43), channel_id=1, source_target_pairs={{0,2},{1,3},{2,0},{3,1},{4,6},{5,7},{6,4},{7,5},{8,10},{9,11},{10,... | collective-permute-start | bytes 368648 | tf_op jit(solution)/shard_map/ppermute | solution.py:395
  21.4 10.6 %collective-permute-start.6 = (bf16[80,768]{1,0:T(8,128)(2,1)S(1)}, bf16[80,768]{1,0:T(8,128)(2,1)S(1)}, u32[]{:S(2)}, u32[]{:S(2)}) collective-permute-start(bf16[80,768]{1,0:T(8,128)(2,1)S(1)} %get-tuple-element.44), channel_id=1, source_target_pairs={{0,4},{1,5},{2,6},{3,7},{4,0},{5,1},{6,2},{7,3},{8,12},{9,13},{10,... | collective-permute-start | bytes 368648 | tf_op jit(solution)/shard_map/ppermute | solution.py:395
  22.6 9.4 %collective-permute-start.7 = (bf16[80,768]{1,0:T(8,128)(2,1)S(1)}, bf16[80,768]{1,0:T(8,128)(2,1)S(1)}, u32[]{:S(2)}, u32[]{:S(2)}) collective-permute-start(bf16[80,768]{1,0:T(8,128)(2,1)S(1)} %get-tuple-element.45), channel_id=1, source_target_pairs={{0,6},{1,7},{2,4},{3,5},{4,2},{5,3},{6,0},{7,1},{8,14},{9,15},{10,... | collective-permute-start | bytes 368648 | tf_op jit(solution)/shard_map/ppermute | solution.py:395
  25.2 8.5 %slice-start = ((s8[4718592]{0:T(1024)(128)(4,1)}), s8[4194304]{0:T(1024)(128)(4,1)S(1)}, s32[]{:S(2)}) async-start(s8[4718592]{0:T(1024)(128)(4,1)} %bitcast.12), calls=%async_computation.1 | async-start | bytes 8388608
  25.2 22.8 %collective-permute-start.9 = (bf16[320,768]{1,0:T(8,128)(2,1)S(1)}, bf16[320,768]{1,0:T(8,128)(2,1)S(1)}, u32[]{:S(2)}, u32[]{:S(2)}) collective-permute-start(bf16[320,768]{1,0:T(8,128)(2,1)S(1)} %constant_dynamic-update-slice_fusion.rows_ref.x_ref), channel_id=1, source_target_pairs={{0,16},{8,24},{16,0},{24,8},{1,17},{9,25},{17,1},{25,9},{2,18},{10... | collective-permute-start | bytes 1474568 | tf_op jit(solution)/shard_map/ppermute | solution.py:398
  26.8 7.0 %slice-start.1 = ((s8[4718592]{0:T(1024)(128)(4,1)}), s8[524288]{0:T(1024)(128)(4,1)S(1)}, s32[]{:S(2)}) async-start(s8[4718592]{0:T(1024)(128)(4,1)} %bitcast.12), calls=%async_computation.2 | async-start | bytes 1048576
  32.0 2.3 %copy-start = (bf16[1,3072,768]{2,1,0:T(8,128)(2,1)S(1)}, bf16[1,3072,768]{2,1,0:T(8,128)(2,1)}, u32[]{:S(2)}) copy-start(bf16[1,3072,768]{2,1,0:T(8,128)(2,1)} %param.15) | copy-start | bytes 14155780
  32.1 12.7 %collective-permute-start.8 = (bf16[640,768]{1,0:T(8,128)(2,1)S(1)}, bf16[640,768]{1,0:T(8,128)(2,1)}, u32[]{:S(2)}, u32[]{:S(2)}) collective-permute-start(bf16[640,768]{1,0:T(8,128)(2,1)S(1)} %join.1.own_ref.own), channel_id=1, source_target_pairs={{0,8},{8,0},{16,24},{24,16},{1,9},{9,1},{17,25},{25,17},{2,10},{10... | collective-permute-start | bytes 2949128 | tf_op jit(solution)/shard_map/ppermute | solution.py:398
  32.2 15.8 %collective-permute-start.10 = (bf16[320,768]{1,0:T(8,128)(2,1)S(1)}, bf16[320,768]{1,0:T(8,128)(2,1)S(1)}, u32[]{:S(2)}, u32[]{:S(2)}) collective-permute-start(bf16[320,768]{1,0:T(8,128)(2,1)S(1)} %slice.4), channel_id=1, source_target_pairs={{0,16},{8,24},{16,0},{24,8},{1,17},{9,25},{17,1},{25,9},{2,18},{10... | collective-permute-start | bytes 1474568 | tf_op jit(solution)/shard_map/ppermute | solution.py:398
  39.6 19.2 %all-to-all-start = ((bf16[8,248,128]{2,1,0:T(8,128)(2,1)}), bf16[8,248,128]{2,1,0:T(8,128)(2,1)S(1)}, u32[]{:S(2)}, u32[]{:S(2)}) async-start(bf16[8,248,128]{2,1,0:T(8,128)(2,1)} %own_second.1.after_ref), calls=%async_computation | async-start | bytes 1015808 | tf_op jit(solution)/shard_map/all_to_all | solution.py:475
  48.1 3.3 %collective-permute-start.11 = (bf16[640,768]{1,0:T(8,128)(2,1)S(1)}, bf16[640,768]{1,0:T(8,128)(2,1)S(1)}, u32[]{:S(2)}, u32[]{:S(2)}) collective-permute-start(bf16[640,768]{1,0:T(8,128)(2,1)S(1)} %forward.1), channel_id=1, source_target_pairs={{0,8},{8,0},{16,24},{24,16},{1,9},{9,1},{17,25},{25,17},{2,10},{10... | collective-permute-start | bytes 2949128 | tf_op jit(solution)/shard_map/ppermute | solution.py:398
  53.1 5.6 %copy-start.1 = (f32[256]{0:T(256)S(1)}, f32[256]{0:T(256)}, u32[]{:S(2)}) copy-start(f32[256]{0:T(256)} %param.10) | copy-start | bytes 3076
  53.1 5.6 %copy-start.2 = (s32[256]{0:T(256)S(1)}, s32[256]{0:T(256)}, u32[]{:S(2)}) copy-start(s32[256]{0:T(256)} %param.11) | copy-start | bytes 3076
  53.1 5.6 %copy-start.3 = (s32[256]{0:T(256)S(1)}, s32[256]{0:T(256)}, u32[]{:S(2)}) copy-start(s32[256]{0:T(256)} %param.12) | copy-start | bytes 3076

commit v6 on v5

--- a/solution.py
+++ b/solution.py
@@ -435,8 +435,8 @@
     d_far = [d_parts[0]] + [d_far[s] for s in range(1, pairs)]
     x_own = jnp.concatenate([x_keep, across(x_cross, 1)], axis=0)
 
-    steps = hidden_units // 1024
-    wide = ((steps, slots, 1024), bf16)
+    steps = hidden_units // 1536
+    wide = ((steps, slots, 1536), bf16)
     weights = pltpu.VMEM((hidden_units, width), bf16)
     hidden, slope = call(
         own_first_kernel,
@@ -444,7 +444,7 @@
         [vmem, anywhere],
         [wide] * 2,
         [weights, pltpu.SemaphoreType.DMA((steps, 1))],
-        limit=11,
+        limit=16,
         work=1,
     )(x_own, *in_hbm(weight_in[0]))
     pair_rows = ((2 * slots, width), bf16)
@@ -469,7 +469,7 @@
             pltpu.SemaphoreType.DMA((experts,)),
         ],
         out_spec=anywhere,
-        limit=10,
+        limit=16,
         work=20,
     )(me, own, hidden, slope, weight_out[0], weight_in[0])
     returned = lax.all_to_all(back, "expert", split_axis=0, concat_axis=0, tiled=True)

time: 60.2 us -> 60 us (level)
  transfers between devices with their start and end apart: 13 -> 13, of which waited for: 6 -> 5; matrix products, arithmetic and copies ran while one was open for 0% -> 0% of each run, Pallas kernels for 38% -> 38%
where the time goes in v6:
time: 60 us; the launch traced here: 59.7 us
  Pallas kernels  25.4 us (42%)
  starting transfers between devices  20.7 us (34%)
  waiting for transfers between devices  12 us (20%)
  between operations  0.84 us (1%)
  local copies, waits for them, and re-layouts  0.72 us (1%)
    ppermute x8, starting transfers between devices, across(): lax.ppermute(chunk, 'expert', [(i, i ^ mask) for i in range(experts)])  12.4 us
    ppermute x8, waiting for transfers between devices, across(): lax.ppermute(chunk, 'expert', [(i, i ^ mask) for i in range(experts)])  10.5 us
    pallas_call x1, Pallas kernels, body(): call(own_first_kernel, 'own_first', [vmem, anywhere], [wide] * 2, [weight...  5.2 us
    all_to_all x1, starting transfers between devices, body(): lax.all_to_all(back, 'expert', split_axis=0, concat_axis=0, tiled=True)  5.16 us
    pallas_call x1, Pallas kernels, body(): call(partial(own_second_kernel, cap_rows), 'own_second', [smem] + [vmem]...  4.95 us
    pallas_call x1, Pallas kernels, body(): call(far_second_kernel, 'far_second', [anywhere] + [vmem] * 8, [share_row...  4.06 us
    pallas_call x1, Pallas kernels, body(): call(near_first_kernel, 'near_first', [smem] + [anywhere] * 5, [wide, wid...  3.2 us
    ppermute x4, starting transfers between devices, over(): return lax.ppermute(chunk, 'dp', [(i, i ^ mask) for i in range(groups)])  3.2 us
  transfers between devices with their start and end apart: 13, of which 5 were waited for; matrix products, arithmetic and copies ran while one was open for 0% of the time, Pallas kernels for 38%

profile of v6, /device:TPU:0, one launch (start us, length us, event | category | flops | bytes accessed | tf_op | source)
XLA Modules:
  0.0 59.7 jit_solution(11958628759260101828)
XLA Ops:
  0.6 1.6 %pack.1 = (bf16[80,768]{1,0:T(8,128)(2,1)S(1)}, bf16[80,768]{1,0:T(8,128)(2,1)S(1)}, bf16[80,768]{1,0:T(8,128)(2,1)S(1)}, bf16[80,768]{1,0:T(8,128)(2,1)S(1)}, b...) custom-call(s32[1]{0:T(128)} %bitcast.me_ref, bf16[256,768]{1,0:T(8,128)(2,1)} %refs_0_.1, ...), custom_call_target="tpu_custom_call" | custom-call | tf_op jit(solution)/shard_map/pack/pallas_call | solution.py:403
  2.3 3.0 %collective-permute-start = (bf16[160,768]{1,0:T(8,128)(2,1)S(1)}, bf16[160,768]{1,0:T(8,128)(2,1)S(1)}, u32[]{:S(2)}, u32[]{:S(2)}) collective-permute-start(bf16[160,768]{1,0:T(8,128)(2,1)S(1)} %get-tuple-element.34), channel_id=1, source_target_pairs={{0,1},{1,0},{2,3},{3,2},{4,5},{5,4},{6,7},{7,6},{8,9},{9,8},{10,11... | collective-permute-start | bytes 737288 | tf_op jit(solution)/shard_map/ppermute | solution.py:395
  5.3 1.6 %collective-permute-start.1 = (bf16[80,768]{1,0:T(8,128)(2,1)S(1)}, bf16[80,768]{1,0:T(8,128)(2,1)S(1)}, u32[]{:S(2)}, u32[]{:S(2)}) collective-permute-start(bf16[80,768]{1,0:T(8,128)(2,1)S(1)} %get-tuple-element.37), channel_id=1, source_target_pairs={{0,2},{1,3},{2,0},{3,1},{4,6},{5,7},{6,4},{7,5},{8,10},{9,11},{10,... | collective-permute-start | bytes 368648 | tf_op jit(solution)/shard_map/ppermute | solution.py:395
  6.9 2.6 %collective-permute-start.2 = (bf16[80,768]{1,0:T(8,128)(2,1)S(1)}, bf16[80,768]{1,0:T(8,128)(2,1)S(1)}, u32[]{:S(2)}, u32[]{:S(2)}) collective-permute-start(bf16[80,768]{1,0:T(8,128)(2,1)S(1)} %get-tuple-element.38), channel_id=1, source_target_pairs={{0,4},{1,5},{2,6},{3,7},{4,0},{5,1},{6,2},{7,3},{8,12},{9,13},{10,... | collective-permute-start | bytes 368648 | tf_op jit(solution)/shard_map/ppermute | solution.py:395
  9.5 0.2 collective-permute-start.3
  9.7 1.6 %collective-permute-done.near_ref = bf16[160,768]{1,0:T(8,128)(2,1)S(1)} collective-permute-done((bf16[160,768]{1,0:T(8,128)(2,1)S(1)}, bf16[160,768]{1,0:T(8,128)(2,1)S(1)}, u32[]{:S(2)}, u32[]{:S(2)}) %collective-permute-start) | collective-permute-done | bytes 245792 | tf_op jit(solution)/shard_map/ppermute | solution.py:395
  11.3 0.2 collective-permute-done.1.refs_1_
  11.5 7.4 %collective-permute-done.2.refs_2_ = bf16[80,768]{1,0:T(8,128)(2,1)S(1)} collective-permute-done((bf16[80,768]{1,0:T(8,128)(2,1)S(1)}, bf16[80,768]{1,0:T(8,128)(2,1)S(1)}, u32[]{:S(2)}, u32[]{:S(2)}) %collective-permute-start.2) | collective-permute-done | bytes 122912 | tf_op jit(solution)/shard_map/ppermute | solution.py:395
  18.9 0.0 collective-permute-done.3.refs_3_
  19.0 0.6 collective-permute-start.4
  19.5 1.9 %collective-permute-start.5 = (bf16[80,768]{1,0:T(8,128)(2,1)S(1)}, bf16[80,768]{1,0:T(8,128)(2,1)S(1)}, u32[]{:S(2)}, u32[]{:S(2)}) collective-permute-start(bf16[80,768]{1,0:T(8,128)(2,1)S(1)} %get-tuple-element.43), channel_id=1, source_target_pairs={{0,2},{1,3},{2,0},{3,1},{4,6},{5,7},{6,4},{7,5},{8,10},{9,11},{10,... | collective-permute-start | bytes 368648 | tf_op jit(solution)/shard_map/ppermute | solution.py:395
  21.4 1.2 %collective-permute-start.6 = (bf16[80,768]{1,0:T(8,128)(2,1)S(1)}, bf16[80,768]{1,0:T(8,128)(2,1)S(1)}, u32[]{:S(2)}, u32[]{:S(2)}) collective-permute-start(bf16[80,768]{1,0:T(8,128)(2,1)S(1)} %get-tuple-element.44), channel_id=1, source_target_pairs={{0,4},{1,5},{2,6},{3,7},{4,0},{5,1},{6,2},{7,3},{8,12},{9,13},{10,... | collective-permute-start | bytes 368648 | tf_op jit(solution)/shard_map/ppermute | solution.py:395
  22.6 1.4 %collective-permute-start.7 = (bf16[80,768]{1,0:T(8,128)(2,1)S(1)}, bf16[80,768]{1,0:T(8,128)(2,1)S(1)}, u32[]{:S(2)}, u32[]{:S(2)}) collective-permute-start(bf16[80,768]{1,0:T(8,128)(2,1)S(1)} %get-tuple-element.45), channel_id=1, source_target_pairs={{0,6},{1,7},{2,4},{3,5},{4,2},{5,3},{6,0},{7,1},{8,14},{9,15},{10,... | collective-permute-start | bytes 368648 | tf_op jit(solution)/shard_map/ppermute | solution.py:395
  23.9 1.3 %collective-permute-done.4 = bf16[160,768]{1,0:T(8,128)(2,1)S(1)} collective-permute-done((bf16[160,768]{1,0:T(8,128)(2,1)S(1)}, bf16[160,768]{1,0:T(8,128)(2,1)S(1)}, u32[]{:S(2)}, u32[]{:S(2)}) %collective-permute-start.4) | collective-permute-done | bytes 245792 | tf_op jit(solution)/shard_map/ppermute | solution.py:395
  25.2 0.0 slice-start
  25.2 1.6 %collective-permute-start.9 = (bf16[320,768]{1,0:T(8,128)(2,1)S(1)}, bf16[320,768]{1,0:T(8,128)(2,1)S(1)}, u32[]{:S(2)}, u32[]{:S(2)}) collective-permute-start(bf16[320,768]{1,0:T(8,128)(2,1)S(1)} %constant_dynamic-update-slice_fusion.rows_ref.x_ref), channel_id=1, source_target_pairs={{0,16},{8,24},{16,0},{24,8},{1,17},{9,25},{17,1},{25,9},{2,18},{10... | collective-permute-start | bytes 1474568 | tf_op jit(solution)/shard_map/ppermute | solution.py:398
  26.8 0.0 slice-start.1
  26.8 5.2 %own_first.1 = (bf16[2,320,1536]{2,1,0:T(8,128)(2,1)S(1)}, bf16[2,320,1536]{2,1,0:T(8,128)(2,1)S(1)}) custom-call(bf16[320,768]{1,0:T(8,128)(2,1)S(1)} %constant_dynamic-update-slice_fusion.rows_ref.x_ref, bf16[3072,768]{1,0:T(8,128)(2,1)} %bitcast.10), custom_call_target="tpu_custom_call" | custom-call | flops 1509949440 | bytes 2949120 | tf_op jit(solution)/shard_map/own_first/pallas_call | solution.py:441
  32.0 0.0 collective-permute-done.5.refs_1_
  32.0 0.0 collective-permute-done.6.refs_2_
  32.0 0.0 collective-permute-done.7.refs_3_
  32.0 0.0 copy-start
  32.1 0.1 join.1.own_ref.own
  32.1 0.1 collective-permute-start.8
  32.2 1.5 %collective-permute-start.10 = (bf16[320,768]{1,0:T(8,128)(2,1)S(1)}, bf16[320,768]{1,0:T(8,128)(2,1)S(1)}, u32[]{:S(2)}, u32[]{:S(2)}) collective-permute-start(bf16[320,768]{1,0:T(8,128)(2,1)S(1)} %slice.4), channel_id=1, source_target_pairs={{0,16},{8,24},{16,0},{24,8},{1,17},{9,25},{17,1},{25,9},{2,18},{10... | collective-permute-start | bytes 1474568 | tf_op jit(solution)/shard_map/ppermute | solution.py:398
  33.8 0.0 slice-done
  33.8 0.0 slice-done.1
  33.8 0.6 %copy-done = bf16[1,3072,768]{2,1,0:T(8,128)(2,1)S(1)} copy-done((bf16[1,3072,768]{2,1,0:T(8,128)(2,1)S(1)}, bf16[1,3072,768]{2,1,0:T(8,128)(2,1)}, u32[]{:S(2)}) %copy-start) | copy-done | bytes 4718616
  34.4 5.0 %own_second.1.after_ref = bf16[8,248,128]{2,1,0:T(8,128)(2,1)} custom-call(s32[1]{0:T(128)} %bitcast.me_ref, bf16[640,768]{1,0:T(8,128)(2,1)S(1)} %join.1.own_ref.own, bf16[2,320,1536]{2,1,0:T(8,128)(2,1)S(1)} %get-tuple-element.42.after_ref.hidden_ref, bf16[2,320,1536]{2,1,0:T(8,128)(2,1)S(1)} %get-tuple-element.46.slope_ref, ...), custom_call_target="tpu_custom_call" | custom-call | flops 30198988800 | bytes 58982400 | tf_op jit(solution)/shard_map/own_second/pallas_call | solution.py:460
  39.3 5.2 %all-to-all-start = ((bf16[8,248,128]{2,1,0:T(8,128)(2,1)}), bf16[8,248,128]{2,1,0:T(8,128)(2,1)S(1)}, u32[]{:S(2)}, u32[]{:S(2)}) async-start(bf16[8,248,128]{2,1,0:T(8,128)(2,1)} %own_second.1.after_ref), calls=%async_computation | async-start | bytes 1015808 | tf_op jit(solution)/shard_map/all_to_all | solution.py:475
  44.5 0.0 collective-permute-done.8.core
  44.5 3.2 %near_first.1 = (bf16[768,640]{1,0:T(8,128)(2,1)S(1)}, bf16[768,640]{1,0:T(8,128)(2,1)S(1)}, bf16[640,768]{1,0:T(8,128)(2,1)S(1)}, bf16[640,768]{1,0:T(8,128)(2,...) custom-call(s32[1]{0:T(128)} %bitcast.6.which_ref, bf16[8,248,128]{2,1,0:T(8,128)(2,1)} %own_second.1.after_ref, ...), custom_call_target="tpu_custom_call" | custom-call | flops 754974720 | bytes 1474560 | tf_op jit(solution)/shard_map/near_first/pallas_call | solution.py:480
  47.7 0.0 collective-permute-done.9.x_ref.x_over
  47.7 0.0 collective-permute-done.10.d_ref.d_over
  47.7 0.1 forward.1
  47.8 0.1 collective-permute-start.11
  47.9 3.2 %near_second.1 = (f32[768,768]{1,0:T(8,128)S(1)}, f32[768,768]{1,0:T(8,128)S(1)}) custom-call(bf16[8,248,128]{2,1,0:T(8,128)(2,1)} %own_second.1.after_ref, bf16[640,768]{1,0:T(8,128)(2,1)S(1)} %get-tuple-element.47.x_ref, bf16[640,768]{1,0:T(8,128)(2,1)S(1)} %get-tuple-element.48.d_ref, bf16[768,640]{1,0:T(8,128)(2,1)S(1)} %get-tuple-element.49.hidden_ref.after_ref, ...), custom_call_target="tpu_custom_call" | custom-call | flops 22649241600 | bytes 44236800 | tf_op jit(solution)/shard_map/near_second/pallas_call | solution.py:488
  51.1 0.0 collective-permute-done.11.diagonal_ref
  51.1 1.7 %far_first.1 = (bf16[768,640]{1,0:T(8,128)(2,1)S(1)}, bf16[768,640]{1,0:T(8,128)(2,1)S(1)}, bf16[640,768]{1,0:T(8,128)(2,1)S(1)}) custom-call(f32[768,768]{1,0:T(8,128)S(1)} %get-tuple-element.52.after_ref.gin_near, bf16[320,768]{1,0:T(8,128)(2,1)S(1)} %collective-permute-done.9.x_ref.x_over, bf16[640,768]{1,0:T(8,128)(2,1)S(1)} %collective-permute-done.11.diagonal_ref, ...), custom_call_target="tpu_custom_call" | custom-call | tf_op jit(solution)/shard_map/far_first/pallas_call | solution.py:502
  52.8 0.0 copy-start.1
  52.8 0.0 copy-start.2
  52.9 0.0 copy-start.3
  52.9 4.1 %far_second.1 = (bf16[768,768]{1,0:T(8,128)(2,1)}, bf16[768,768]{1,0:T(8,128)(2,1)}) custom-call(bf16[768,640]{1,0:T(8,128)(2,1)S(1)} %get-tuple-element.54.after_ref.hidden_ref, bf16[320,768]{1,0:T(8,128)(2,1)S(1)} %collective-permute-done.10.d_ref.d_over, bf16[640,768]{1,0:T(8,128)(2,1)S(1)} %collective-permute-done.11.diagonal_ref, ...), custom_call_target="tpu_custom_call" | custom-call | tf_op jit(solution)/shard_map/far_second/pallas_call | solution.py:509
  56.9 1.5 %all-to-all-done.back_ref = bf16[8,248,128]{2,1,0:T(8,128)(2,1)S(1)} async-done(((bf16[8,248,128]{2,1,0:T(8,128)(2,1)}), bf16[8,248,128]{2,1,0:T(8,128)(2,1)S(1)}, u32[]{:S(2)}, u32[]{:S(2)}) %all-to-all-start) | async-done | bytes 507936 | tf_op jit(solution)/shard_map/all_to_all | solution.py:475
  58.5 0.0 copy-done.1
  58.5 0.0 copy-done.2
  58.5 0.0 copy-done.3
  58.5 1.2 %unpack.1 = (bf16[256,768]{1,0:T(8,128)(2,1)}, f32[1,256]{1,0:T(1,128)}) custom-call(bf16[768,768]{1,0:T(8,128)(2,1)} %get-tuple-element.58.after_ref, bf16[8,248,128]{2,1,0:T(8,128)(2,1)S(1)} %all-to-all-done.back_ref, f32[1,256]{1,0:T(1,128)S(1)} %bitcast.18, s32[1,256]{1,0:T(1,128)S(1)} %bitcast.20, s32[1,256]{1,0:T(1,128)S(1)} %bitcast.22), custom_call_target="tpu_custom_call" | custom-call | tf_op jit(solution)/shard_map/unpack/pallas_call | solution.py:519
  (6 shorter events, 0.1 us)
Async XLA Ops:
  2.3 9.0 %collective-permute-start = (bf16[160,768]{1,0:T(8,128)(2,1)S(1)}, bf16[160,768]{1,0:T(8,128)(2,1)S(1)}, u32[]{:S(2)}, u32[]{:S(2)}) collective-permute-start(bf16[160,768]{1,0:T(8,128)(2,1)S(1)} %get-tuple-element.34), channel_id=1, source_target_pairs={{0,1},{1,0},{2,3},{3,2},{4,5},{5,4},{6,7},{7,6},{8,9},{9,8},{10,11... | collective-permute-start | bytes 737288 | tf_op jit(solution)/shard_map/ppermute | solution.py:395
  5.3 6.2 %collective-permute-start.1 = (bf16[80,768]{1,0:T(8,128)(2,1)S(1)}, bf16[80,768]{1,0:T(8,128)(2,1)S(1)}, u32[]{:S(2)}, u32[]{:S(2)}) collective-permute-start(bf16[80,768]{1,0:T(8,128)(2,1)S(1)} %get-tuple-element.37), channel_id=1, source_target_pairs={{0,2},{1,3},{2,0},{3,1},{4,6},{5,7},{6,4},{7,5},{8,10},{9,11},{10,... | collective-permute-start | bytes 368648 | tf_op jit(solution)/shard_map/ppermute | solution.py:395
  6.9 12.0 %collective-permute-start.2 = (bf16[80,768]{1,0:T(8,128)(2,1)S(1)}, bf16[80,768]{1,0:T(8,128)(2,1)S(1)}, u32[]{:S(2)}, u32[]{:S(2)}) collective-permute-start(bf16[80,768]{1,0:T(8,128)(2,1)S(1)} %get-tuple-element.38), channel_id=1, source_target_pairs={{0,4},{1,5},{2,6},{3,7},{4,0},{5,1},{6,2},{7,3},{8,12},{9,13},{10,... | collective-permute-start | bytes 368648 | tf_op jit(solution)/shard_map/ppermute | solution.py:395
  9.5 9.4 %collective-permute-start.3 = (bf16[80,768]{1,0:T(8,128)(2,1)S(1)}, bf16[80,768]{1,0:T(8,128)(2,1)S(1)}, u32[]{:S(2)}, u32[]{:S(2)}) collective-permute-start(bf16[80,768]{1,0:T(8,128)(2,1)S(1)} %get-tuple-element.39), channel_id=1, source_target_pairs={{0,6},{1,7},{2,4},{3,5},{4,2},{5,3},{6,0},{7,1},{8,14},{9,15},{10,... | collective-permute-start | bytes 368648 | tf_op jit(solution)/shard_map/ppermute | solution.py:395
  19.0 6.3 %collective-permute-start.4 = (bf16[160,768]{1,0:T(8,128)(2,1)S(1)}, bf16[160,768]{1,0:T(8,128)(2,1)S(1)}, u32[]{:S(2)}, u32[]{:S(2)}) collective-permute-start(bf16[160,768]{1,0:T(8,128)(2,1)S(1)} %get-tuple-element.41), channel_id=1, source_target_pairs={{0,1},{1,0},{2,3},{3,2},{4,5},{5,4},{6,7},{7,6},{8,9},{9,8},{10,11... | collective-permute-start | bytes 737288 | tf_op jit(solution)/shard_map/ppermute | solution.py:395
  19.5 12.5 %collective-permute-start.5 = (bf16[80,768]{1,0:T(8,128)(2,1)S(1)}, bf16[80,768]{1,0:T(8,128)(2,1)S(1)}, u32[]{:S(2)}, u32[]{:S(2)}) collective-permute-start(bf16[80,768]{1,0:T(8,128)(2,1)S(1)} %get-tuple-element.43), channel_id=1, source_target_pairs={{0,2},{1,3},{2,0},{3,1},{4,6},{5,7},{6,4},{7,5},{8,10},{9,11},{10,... | collective-permute-start | bytes 368648 | tf_op jit(solution)/shard_map/ppermute | solution.py:395
  21.4 10.6 %collective-permute-start.6 = (bf16[80,768]{1,0:T(8,128)(2,1)S(1)}, bf16[80,768]{1,0:T(8,128)(2,1)S(1)}, u32[]{:S(2)}, u32[]{:S(2)}) collective-permute-start(bf16[80,768]{1,0:T(8,128)(2,1)S(1)} %get-tuple-element.44), channel_id=1, source_target_pairs={{0,4},{1,5},{2,6},{3,7},{4,0},{5,1},{6,2},{7,3},{8,12},{9,13},{10,... | collective-permute-start | bytes 368648 | tf_op jit(solution)/shard_map/ppermute | solution.py:395
  22.6 9.5 %collective-permute-start.7 = (bf16[80,768]{1,0:T(8,128)(2,1)S(1)}, bf16[80,768]{1,0:T(8,128)(2,1)S(1)}, u32[]{:S(2)}, u32[]{:S(2)}) collective-permute-start(bf16[80,768]{1,0:T(8,128)(2,1)S(1)} %get-tuple-element.45), channel_id=1, source_target_pairs={{0,6},{1,7},{2,4},{3,5},{4,2},{5,3},{6,0},{7,1},{8,14},{9,15},{10,... | collective-permute-start | bytes 368648 | tf_op jit(solution)/shard_map/ppermute | solution.py:395
  25.2 8.5 %slice-start = ((s8[4718592]{0:T(1024)(128)(4,1)}), s8[4194304]{0:T(1024)(128)(4,1)S(1)}, s32[]{:S(2)}) async-start(s8[4718592]{0:T(1024)(128)(4,1)} %bitcast.12), calls=%async_computation.1 | async-start | bytes 8388608
  25.2 22.5 %collective-permute-start.9 = (bf16[320,768]{1,0:T(8,128)(2,1)S(1)}, bf16[320,768]{1,0:T(8,128)(2,1)S(1)}, u32[]{:S(2)}, u32[]{:S(2)}) collective-permute-start(bf16[320,768]{1,0:T(8,128)(2,1)S(1)} %constant_dynamic-update-slice_fusion.rows_ref.x_ref), channel_id=1, source_target_pairs={{0,16},{8,24},{16,0},{24,8},{1,17},{9,25},{17,1},{25,9},{2,18},{10... | collective-permute-start | bytes 1474568 | tf_op jit(solution)/shard_map/ppermute | solution.py:398
  26.8 7.0 %slice-start.1 = ((s8[4718592]{0:T(1024)(128)(4,1)}), s8[524288]{0:T(1024)(128)(4,1)S(1)}, s32[]{:S(2)}) async-start(s8[4718592]{0:T(1024)(128)(4,1)} %bitcast.12), calls=%async_computation.2 | async-start | bytes 1048576
  32.0 2.3 %copy-start = (bf16[1,3072,768]{2,1,0:T(8,128)(2,1)S(1)}, bf16[1,3072,768]{2,1,0:T(8,128)(2,1)}, u32[]{:S(2)}) copy-start(bf16[1,3072,768]{2,1,0:T(8,128)(2,1)} %param.15) | copy-start | bytes 14155780
  32.1 12.4 %collective-permute-start.8 = (bf16[640,768]{1,0:T(8,128)(2,1)S(1)}, bf16[640,768]{1,0:T(8,128)(2,1)}, u32[]{:S(2)}, u32[]{:S(2)}) collective-permute-start(bf16[640,768]{1,0:T(8,128)(2,1)S(1)} %join.1.own_ref.own), channel_id=1, source_target_pairs={{0,8},{8,0},{16,24},{24,16},{1,9},{9,1},{17,25},{25,17},{2,10},{10... | collective-permute-start | bytes 2949128 | tf_op jit(solution)/shard_map/ppermute | solution.py:398
  32.2 15.5 %collective-permute-start.10 = (bf16[320,768]{1,0:T(8,128)(2,1)S(1)}, bf16[320,768]{1,0:T(8,128)(2,1)S(1)}, u32[]{:S(2)}, u32[]{:S(2)}) collective-permute-start(bf16[320,768]{1,0:T(8,128)(2,1)S(1)} %slice.4), channel_id=1, source_target_pairs={{0,16},{8,24},{16,0},{24,8},{1,17},{9,25},{17,1},{25,9},{2,18},{10... | collective-permute-start | bytes 1474568 | tf_op jit(solution)/shard_map/ppermute | solution.py:398
  39.3 19.1 %all-to-all-start = ((bf16[8,248,128]{2,1,0:T(8,128)(2,1)}), bf16[8,248,128]{2,1,0:T(8,128)(2,1)S(1)}, u32[]{:S(2)}, u32[]{:S(2)}) async-start(bf16[8,248,128]{2,1,0:T(8,128)(2,1)} %own_second.1.after_ref), calls=%async_computation | async-start | bytes 1015808 | tf_op jit(solution)/shard_map/all_to_all | solution.py:475
  47.8 3.3 %collective-permute-start.11 = (bf16[640,768]{1,0:T(8,128)(2,1)S(1)}, bf16[640,768]{1,0:T(8,128)(2,1)S(1)}, u32[]{:S(2)}, u32[]{:S(2)}) collective-permute-start(bf16[640,768]{1,0:T(8,128)(2,1)S(1)} %forward.1), channel_id=1, source_target_pairs={{0,8},{8,0},{16,24},{24,16},{1,9},{9,1},{17,25},{25,17},{2,10},{10... | collective-permute-start | bytes 2949128 | tf_op jit(solution)/shard_map/ppermute | solution.py:398
  52.8 5.6 %copy-start.1 = (f32[256]{0:T(256)S(1)}, f32[256]{0:T(256)}, u32[]{:S(2)}) copy-start(f32[256]{0:T(256)} %param.10) | copy-start | bytes 3076
  52.8 5.6 %copy-start.2 = (s32[256]{0:T(256)S(1)}, s32[256]{0:T(256)}, u32[]{:S(2)}) copy-start(s32[256]{0:T(256)} %param.11) | copy-start | bytes 3076
  52.9 5.6 %copy-start.3 = (s32[256]{0:T(256)S(1)}, s32[256]{0:T(256)}, u32[]{:S(2)}) copy-start(s32[256]{0:T(256)} %param.12) | copy-start | bytes 3076
